TPU v7x, 32 devices: a whole 2x2x4 slice. The times are simulated.
32 devices in a mesh: row: 16 (over z, y, core), col: 2 (over x).
Axes of the slice: x: 2, y: 2, z: 4, core: 2. Of those that a mesh axis runs over, the one named last changes fastest.
Arguments:
- alignment: bfloat16 [64, 768, 256], P('row', 'col'), may hold values from -10 to 10
- alignment_norm_gain: float32 [256], replicated, may hold values from 0.1 to 1.9
- alignment_norm_bias: float32 [256], replicated, may hold values from -1.75 to 1.75
- projection_weight: bfloat16 [256, 64], replicated, may hold values from -0.375 to 0.375
- projection_bias_pair: float32 [64], replicated, may hold values from -3 to 3
- w_out: bfloat16 [1024, 128], replicated, may hold values from -0.1875 to 0.1875
- b_out: float32 [128], replicated, may hold values from -1.75 to 1.75
- pair_gain: float32 [128], replicated, may hold values from 0.1 to 1.9
- pair_bias: float32 [128], replicated, may hold values from -1.75 to 1.75
- w_up: bfloat16 [128, 512], replicated, may hold values from -0.5 to 0.5
- b_up: float32 [512], replicated, may hold values from -1.75 to 1.75
- w_down: bfloat16 [512, 128], replicated, may hold values from -0.25 to 0.25
- b_down: float32 [128], replicated, may hold values from -1.75 to 1.75
Outputs:
- pair_out: bfloat16 [768, 768, 128], P('row', 'col')
All inputs are finite; a program needn't handle non-finite values.
Results may differ from a plain program's by a relative error of at most 0.0052.
Values may be sent and summed in bfloat16 or wider, within the bound.
No kernel may reach another device: no remote copies, remote signals or barrier semaphores. Data moves between devices by JAX's collectives and lax.ppermute only.
A program may use at most 64 MiB of HBM per device.

v0:
```python
import math

import jax
import jax.numpy as jnp
from jax import lax
from jax.sharding import PartitionSpec as P

EPSILON = 1e-05


def layer_norm(values, gain_vec, bias_vec):
    average = jnp.mean(values, axis=-1, keepdims=True)
    centered = values - average
    variance = jnp.mean(centered * centered, axis=-1, keepdims=True)
    return centered * lax.rsqrt(variance + EPSILON) * gain_vec + bias_vec


def channel_norm(values, gain_vec, bias_vec):
    average = jnp.mean(values, axis=0, keepdims=True)
    centered = values - average
    variance = jnp.mean(centered * centered, axis=0, keepdims=True)
    return (
        centered * lax.rsqrt(variance + EPSILON) * gain_vec[:, None, None] + bias_vec[:, None, None]
    )


def project_split(
    rows_in,
    seq_rows,
    residues,
    alignment_norm_gain,
    alignment_norm_bias,
    projection_weight,
    projection_bias_pair,
):
    channel_count = rows_in.shape[-1]
    width = projection_weight.shape[1]
    half_width = width // 2
    normed = layer_norm(
        rows_in.reshape(seq_rows * residues, channel_count).astype(jnp.float32),
        alignment_norm_gain,
        alignment_norm_bias,
    ).astype(jnp.bfloat16)
    result = (
        jnp.dot(normed, projection_weight, preferred_element_type=jnp.float32)
        + projection_bias_pair
    ).astype(jnp.bfloat16)
    return result.reshape(seq_rows, residues, 2, half_width).transpose(0, 2, 3, 1)


def outer_channels(rows_side, cols_side, weight, bias_vec, total):
    seq_rows, block_size, half_width = rows_side.shape
    column_length = cols_side.shape[2]
    flat_cols = cols_side.reshape(seq_rows, half_width * column_length)
    product = (
        lax.dot_general(
            rows_side, flat_cols, (((0,), (0,)), ((), ())), preferred_element_type=jnp.float32
        )
        / total
    )
    product = product.astype(jnp.bfloat16).reshape(
        block_size, half_width * half_width, column_length
    )
    projected_z = lax.dot_general(
        weight, product, (((0,), (1,)), ((), ())), preferred_element_type=jnp.float32
    )
    return jax.nn.relu(projected_z + bias_vec[:, None, None])


def finish(pair, pair_gain, pair_bias, w_up, b_up, w_down, b_down):
    normed = channel_norm(pair, pair_gain, pair_bias).astype(jnp.bfloat16)
    hidden = lax.dot_general(
        w_up, normed, (((0,), (0,)), ((), ())), preferred_element_type=jnp.float32
    )
    hidden = jax.nn.relu(hidden + b_up[:, None, None]).astype(jnp.bfloat16)
    update = lax.dot_general(
        w_down, hidden, (((0,), (0,)), ((), ())), preferred_element_type=jnp.float32
    )
    result = (pair + update + b_down[:, None, None]).astype(jnp.bfloat16)
    return result.transpose(1, 2, 0)


def shards(
    alignment,
    alignment_norm_gain,
    alignment_norm_bias,
    projection_weight,
    projection_bias_pair,
    w_out,
    b_out,
    pair_gain,
    pair_bias,
    w_up,
    b_up,
    w_down,
    b_down,
):
    alignment_local, column_length, channel_count = alignment.shape
    projection_width = projection_weight.shape[1]
    half_width = projection_width // 2
    row_count = lax.axis_size("row")
    col_count = lax.axis_size("col")
    row_length = column_length * col_count // row_count
    local_projected = project_split(
        alignment,
        alignment_local,
        column_length,
        alignment_norm_gain,
        alignment_norm_bias,
        projection_weight,
        projection_bias_pair,
    )
    column_projected = lax.all_gather(local_projected, "row", axis=0, tiled=True)
    alignment_total = column_projected.shape[0]
    col_wide = lax.all_gather(local_projected, "col", axis=3, tiled=True)
    row_projected = lax.all_to_all(col_wide, "row", split_axis=3, concat_axis=0, tiled=True)
    col_left = column_projected[:, 0]
    col_right = column_projected[:, 1]
    row_left = row_projected[:, 0]
    row_right = row_projected[:, 1]
    out_width = w_out.shape[1]
    w_mirror = (
        w_out.reshape(half_width, half_width, out_width)
        .transpose(1, 0, 2)
        .reshape(half_width * half_width, out_width)
    )
    block_size = math.gcd(row_length, 8)

    def pair_block(block_index):
        first_row = block_index * block_size
        left_here = lax.dynamic_slice_in_dim(row_left, first_row, block_size, 2).transpose(0, 2, 1)
        right_here = lax.dynamic_slice_in_dim(row_right, first_row, block_size, 2).transpose(
            0, 2, 1
        )
        pair = outer_channels(left_here, col_right, w_out, b_out, alignment_total)
        pair = pair + outer_channels(right_here, col_left, w_mirror, b_out, alignment_total)
        return finish(pair, pair_gain, pair_bias, w_up, b_up, w_down, b_down)

    blocks_out = lax.map(pair_block, jnp.arange(row_length // block_size, dtype=jnp.int32))
    return blocks_out.reshape(row_length, column_length, out_width)


def solution(mesh):
    return jax.shard_map(
        shards,
        mesh=mesh,
        in_specs=(
            P("row", "col", None),
            P(),
            P(),
            P(),
            P(),
            P(),
            P(),
            P(),
            P(),
            P(),
            P(),
            P(),
            P(),
        ),
        out_specs=P("row", "col", None),
        check_vma=False,
    )
```

profile of v0, /device:TPU:0, one launch (start us, length us, event | category | flops | bytes accessed | tf_op | source)
XLA Modules:
  0.0 348.6 jit_solution(4467526325544950523)
XLA Ops:
  6.6 1.5 convert_reduce_fusion
  8.1 1.6 multiply_reduce_fusion.1
  11.4 8.8 %all_gather.6 = bf16[4,2,32,768]{3,2,1,0:T(8,128)(2,1)S(1)} all-gather(bf16[4,2,32,384]{3,2,1,0:T(8,128)(2,1)} %bitcast.142), channel_id=1, replica_groups=mesh['row'=16,'col'=2] {'col'}, dimensions={3}, use_global_device_ids=true | all-gather | bytes 589824 | tf_op jit(solution)/shard_map/all_gather | solution.py:115
  20.2 1.0 copy.53
  21.3 2.2 reshape.88
  23.5 6.1 %all-to-all-start = ((bf16[16,2,6144]{2,1,0:T(2,128)(2,1)}), bf16[16,2,6144]{2,1,0:T(2,128)(2,1)S(1)}, u32[]{:S(2)}, u32[]{:S(2)}) async-start(bf16[16,2,6144]{2,1,0:T(2,128)(2,1)} %reshape.88), calls=%async_computation | async-start | bytes 786432 | tf_op jit(solution)/shard_map/all_to_all | solution.py:116
  29.9 0.9 copy.61
  30.8 12.1 %all-to-all-done = bf16[16,2,6144]{2,1,0:T(2,128)(2,1)S(1)} async-done(((bf16[16,2,6144]{2,1,0:T(2,128)(2,1)}), bf16[16,2,6144]{2,1,0:T(2,128)(2,1)S(1)}, u32[]{:S(2)}, u32[]{:S(2)}) %all-to-all-start) | async-done | bytes 393248 | tf_op jit(solution)/shard_map/all_to_all | solution.py:116
  43.6 1.9 copy.54
  45.6 1.6 copy.56
  47.2 1.7 copy.59
  48.9 13.3 %all-gather.2.cloned.1.call-done = bf16[64,2,32,384]{3,2,1,0:T(8,128)(2,1)} async-done(((bf16[4,2,32,384]{3,2,1,0:T(8,128)(2,1)}), bf16[64,2,32,384]{3,2,1,0:T(8,128)(2,1)}) %all-gather.2.cloned.1.call-update) | async-done | bytes 3145744 | tf_op jit(solution)/shard_map/all_gather | solution.py:113
  62.2 2.2 slice_bitcast_fusion
  64.5 2.1 reshape.90
  66.6 1.6 reshape.91
  68.2 273.5 %while.11 = (s32[]{:T(128)}, bf16[6,8,384,128]{3,2,1,0:T(8,128)(2,1)}, s32[6]{0:T(128)S(1)}, bf16[64,32,48]{0,1,2:T(8,128)(2,1)}, bf16[64,1,32,384]{3,2,0,1:T(8,...) while((s32[]{:T(128)}, ...), condition=%wide.wide.region_5.6_spmd, body=%wide.wide.region_2.5_spmd.sunk | while | flops 3245214720 | bytes 67355456 | solution.py:139
  69.7 5.9 %fusion.85 = bf16[8,32,12288]{2,1,0:T(8,128)(2,1)} fusion(bf16[64,12288,1]{1,0,2:T(8,128)(2,1)} %get-tuple-element.445, bf16[64,32,48]{0,1,2:T(8,128)(2,1)} %get-tuple-element.431, s32[]{:T(128)S(6)} %select_n.6), kind=kOutput, calls=%fused_computation.2.clone.clone.1 | convolution fusion | flops 408944640 | bytes 7929860 | tf_op jit(solution)/shard_map/while/body/eval_jaxpr/dot_general | solution.py:56
  75.6 10.1 %reshape.99 = bf16[8,1024,384]{2,1,0:T(8,128)(2,1)} reshape(bf16[8,32,12288]{2,1,0:T(8,128)(2,1)} %fusion.85) | data formatting | bytes 12582912 | tf_op jit(solution)/shard_map/while/body/eval_jaxpr/reshape | solution.py:61
  85.7 3.8 %fusion.86 = f32[8,384,128]{1,2,0:T(8,128)S(1)} fusion(bf16[8,1024,384]{2,1,0:T(8,128)(2,1)} %reshape.99, bf16[1024,128]{0,1:T(8,128)(2,1)S(1)} %get-tuple-element.433), kind=kOutput, calls=%fused_computation.22.clone.clone.1 | convolution fusion | flops 805306368 | bytes 8126464 | tf_op jit(solution)/shard_map/while/body/eval_jaxpr/dot_general | solution.py:64
  89.5 5.9 %fusion.84 = bf16[8,32,12288]{2,1,0:T(8,128)(2,1)} fusion(bf16[64,12288,1]{1,0,2:T(8,128)(2,1)} %get-tuple-element.444, bf16[64,32,48]{0,1,2:T(8,128)(2,1)} %get-tuple-element.435, s32[]{:T(128)S(6)} %select_n.6), kind=kOutput, calls=%fused_computation.3.clone.clone.1 | convolution fusion | flops 408944640 | bytes 7929860 | tf_op jit(solution)/shard_map/while/body/eval_jaxpr/dot_general | solution.py:56
  95.4 10.1 %reshape.98 = bf16[8,1024,384]{2,1,0:T(8,128)(2,1)} reshape(bf16[8,32,12288]{2,1,0:T(8,128)(2,1)} %fusion.84) | data formatting | bytes 12582912 | tf_op jit(solution)/shard_map/while/body/eval_jaxpr/reshape | solution.py:61
  105.5 4.0 %bitcast_reduce_fusion.3 = (f32[8,384]{1,0:T(8,128)S(1)}, f32[8,384,128]{1,2,0:T(8,128)S(1)}) fusion(bf16[8,1024,384]{2,1,0:T(8,128)(2,1)} %reshape.98, bf16[1024,128]{0,1:T(8,128)(2,1)} %get-tuple-element.437, f32[8,384,128]{1,2,0:T(8,128)S(1)} %fusion.86, f32[128]{0:T(128)S(1)} %get-tuple-element.434), kind=kOutput, calls=%fused_computation.11.clone.clone.1 | convolution fusion | flops 807662592 | bytes 9712128 | tf_op jit(solution)/shard_map/while/body/eval_jaxpr/dot_general | solution.py:64
  110.5 2.1 fusion.87
  113.0 0.9 constant_dynamic-update-slice_fusion.3
  115.2 5.9 %fusion.85 = bf16[8,32,12288]{2,1,0:T(8,128)(2,1)} fusion(bf16[64,12288,1]{1,0,2:T(8,128)(2,1)} %get-tuple-element.445, bf16[64,32,48]{0,1,2:T(8,128)(2,1)} %get-tuple-element.431, s32[]{:T(128)S(6)} %select_n.6), kind=kOutput, calls=%fused_computation.2.clone.clone.1 | convolution fusion | flops 408944640 | bytes 7929860 | tf_op jit(solution)/shard_map/while/body/eval_jaxpr/dot_general | solution.py:56
  121.1 10.1 %reshape.99 = bf16[8,1024,384]{2,1,0:T(8,128)(2,1)} reshape(bf16[8,32,12288]{2,1,0:T(8,128)(2,1)} %fusion.85) | data formatting | bytes 12582912 | tf_op jit(solution)/shard_map/while/body/eval_jaxpr/reshape | solution.py:61
  131.3 3.8 %fusion.86 = f32[8,384,128]{1,2,0:T(8,128)S(1)} fusion(bf16[8,1024,384]{2,1,0:T(8,128)(2,1)} %reshape.99, bf16[1024,128]{0,1:T(8,128)(2,1)S(1)} %get-tuple-element.433), kind=kOutput, calls=%fused_computation.22.clone.clone.1 | convolution fusion | flops 805306368 | bytes 8126464 | tf_op jit(solution)/shard_map/while/body/eval_jaxpr/dot_general | solution.py:64
  135.0 5.9 %fusion.84 = bf16[8,32,12288]{2,1,0:T(8,128)(2,1)} fusion(bf16[64,12288,1]{1,0,2:T(8,128)(2,1)} %get-tuple-element.444, bf16[64,32,48]{0,1,2:T(8,128)(2,1)} %get-tuple-element.435, s32[]{:T(128)S(6)} %select_n.6), kind=kOutput, calls=%fused_computation.3.clone.clone.1 | convolution fusion | flops 408944640 | bytes 7929860 | tf_op jit(solution)/shard_map/while/body/eval_jaxpr/dot_general | solution.py:56
  140.9 10.1 %reshape.98 = bf16[8,1024,384]{2,1,0:T(8,128)(2,1)} reshape(bf16[8,32,12288]{2,1,0:T(8,128)(2,1)} %fusion.84) | data formatting | bytes 12582912 | tf_op jit(solution)/shard_map/while/body/eval_jaxpr/reshape | solution.py:61
  151.1 4.0 %bitcast_reduce_fusion.3 = (f32[8,384]{1,0:T(8,128)S(1)}, f32[8,384,128]{1,2,0:T(8,128)S(1)}) fusion(bf16[8,1024,384]{2,1,0:T(8,128)(2,1)} %reshape.98, bf16[1024,128]{0,1:T(8,128)(2,1)} %get-tuple-element.437, f32[8,384,128]{1,2,0:T(8,128)S(1)} %fusion.86, f32[128]{0:T(128)S(1)} %get-tuple-element.434), kind=kOutput, calls=%fused_computation.11.clone.clone.1 | convolution fusion | flops 807662592 | bytes 9712128 | tf_op jit(solution)/shard_map/while/body/eval_jaxpr/dot_general | solution.py:64
  156.1 2.1 fusion.87
  158.6 0.9 constant_dynamic-update-slice_fusion.3
  160.8 5.9 %fusion.85 = bf16[8,32,12288]{2,1,0:T(8,128)(2,1)} fusion(bf16[64,12288,1]{1,0,2:T(8,128)(2,1)} %get-tuple-element.445, bf16[64,32,48]{0,1,2:T(8,128)(2,1)} %get-tuple-element.431, s32[]{:T(128)S(6)} %select_n.6), kind=kOutput, calls=%fused_computation.2.clone.clone.1 | convolution fusion | flops 408944640 | bytes 7929860 | tf_op jit(solution)/shard_map/while/body/eval_jaxpr/dot_general | solution.py:56
  166.7 10.1 %reshape.99 = bf16[8,1024,384]{2,1,0:T(8,128)(2,1)} reshape(bf16[8,32,12288]{2,1,0:T(8,128)(2,1)} %fusion.85) | data formatting | bytes 12582912 | tf_op jit(solution)/shard_map/while/body/eval_jaxpr/reshape | solution.py:61
  176.8 3.8 %fusion.86 = f32[8,384,128]{1,2,0:T(8,128)S(1)} fusion(bf16[8,1024,384]{2,1,0:T(8,128)(2,1)} %reshape.99, bf16[1024,128]{0,1:T(8,128)(2,1)S(1)} %get-tuple-element.433), kind=kOutput, calls=%fused_computation.22.clone.clone.1 | convolution fusion | flops 805306368 | bytes 8126464 | tf_op jit(solution)/shard_map/while/body/eval_jaxpr/dot_general | solution.py:64
  180.6 5.9 %fusion.84 = bf16[8,32,12288]{2,1,0:T(8,128)(2,1)} fusion(bf16[64,12288,1]{1,0,2:T(8,128)(2,1)} %get-tuple-element.444, bf16[64,32,48]{0,1,2:T(8,128)(2,1)} %get-tuple-element.435, s32[]{:T(128)S(6)} %select_n.6), kind=kOutput, calls=%fused_computation.3.clone.clone.1 | convolution fusion | flops 408944640 | bytes 7929860 | tf_op jit(solution)/shard_map/while/body/eval_jaxpr/dot_general | solution.py:56
  186.5 10.1 %reshape.98 = bf16[8,1024,384]{2,1,0:T(8,128)(2,1)} reshape(bf16[8,32,12288]{2,1,0:T(8,128)(2,1)} %fusion.84) | data formatting | bytes 12582912 | tf_op jit(solution)/shard_map/while/body/eval_jaxpr/reshape | solution.py:61
  196.6 4.0 %bitcast_reduce_fusion.3 = (f32[8,384]{1,0:T(8,128)S(1)}, f32[8,384,128]{1,2,0:T(8,128)S(1)}) fusion(bf16[8,1024,384]{2,1,0:T(8,128)(2,1)} %reshape.98, bf16[1024,128]{0,1:T(8,128)(2,1)} %get-tuple-element.437, f32[8,384,128]{1,2,0:T(8,128)S(1)} %fusion.86, f32[128]{0:T(128)S(1)} %get-tuple-element.434), kind=kOutput, calls=%fused_computation.11.clone.clone.1 | convolution fusion | flops 807662592 | bytes 9712128 | tf_op jit(solution)/shard_map/while/body/eval_jaxpr/dot_general | solution.py:64
  201.6 2.1 fusion.87
  204.1 0.9 constant_dynamic-update-slice_fusion.3
  206.3 5.9 %fusion.85 = bf16[8,32,12288]{2,1,0:T(8,128)(2,1)} fusion(bf16[64,12288,1]{1,0,2:T(8,128)(2,1)} %get-tuple-element.445, bf16[64,32,48]{0,1,2:T(8,128)(2,1)} %get-tuple-element.431, s32[]{:T(128)S(6)} %select_n.6), kind=kOutput, calls=%fused_computation.2.clone.clone.1 | convolution fusion | flops 408944640 | bytes 7929860 | tf_op jit(solution)/shard_map/while/body/eval_jaxpr/dot_general | solution.py:56
  212.2 10.1 %reshape.99 = bf16[8,1024,384]{2,1,0:T(8,128)(2,1)} reshape(bf16[8,32,12288]{2,1,0:T(8,128)(2,1)} %fusion.85) | data formatting | bytes 12582912 | tf_op jit(solution)/shard_map/while/body/eval_jaxpr/reshape | solution.py:61
  222.4 3.8 %fusion.86 = f32[8,384,128]{1,2,0:T(8,128)S(1)} fusion(bf16[8,1024,384]{2,1,0:T(8,128)(2,1)} %reshape.99, bf16[1024,128]{0,1:T(8,128)(2,1)S(1)} %get-tuple-element.433), kind=kOutput, calls=%fused_computation.22.clone.clone.1 | convolution fusion | flops 805306368 | bytes 8126464 | tf_op jit(solution)/shard_map/while/body/eval_jaxpr/dot_general | solution.py:64
  226.1 5.9 %fusion.84 = bf16[8,32,12288]{2,1,0:T(8,128)(2,1)} fusion(bf16[64,12288,1]{1,0,2:T(8,128)(2,1)} %get-tuple-element.444, bf16[64,32,48]{0,1,2:T(8,128)(2,1)} %get-tuple-element.435, s32[]{:T(128)S(6)} %select_n.6), kind=kOutput, calls=%fused_computation.3.clone.clone.1 | convolution fusion | flops 408944640 | bytes 7929860 | tf_op jit(solution)/shard_map/while/body/eval_jaxpr/dot_general | solution.py:56
  232.0 10.1 %reshape.98 = bf16[8,1024,384]{2,1,0:T(8,128)(2,1)} reshape(bf16[8,32,12288]{2,1,0:T(8,128)(2,1)} %fusion.84) | data formatting | bytes 12582912 | tf_op jit(solution)/shard_map/while/body/eval_jaxpr/reshape | solution.py:61
  242.2 4.0 %bitcast_reduce_fusion.3 = (f32[8,384]{1,0:T(8,128)S(1)}, f32[8,384,128]{1,2,0:T(8,128)S(1)}) fusion(bf16[8,1024,384]{2,1,0:T(8,128)(2,1)} %reshape.98, bf16[1024,128]{0,1:T(8,128)(2,1)} %get-tuple-element.437, f32[8,384,128]{1,2,0:T(8,128)S(1)} %fusion.86, f32[128]{0:T(128)S(1)} %get-tuple-element.434), kind=kOutput, calls=%fused_computation.11.clone.clone.1 | convolution fusion | flops 807662592 | bytes 9712128 | tf_op jit(solution)/shard_map/while/body/eval_jaxpr/dot_general | solution.py:64
  247.2 2.1 fusion.87
  249.7 0.9 constant_dynamic-update-slice_fusion.3
  251.9 5.9 %fusion.85 = bf16[8,32,12288]{2,1,0:T(8,128)(2,1)} fusion(bf16[64,12288,1]{1,0,2:T(8,128)(2,1)} %get-tuple-element.445, bf16[64,32,48]{0,1,2:T(8,128)(2,1)} %get-tuple-element.431, s32[]{:T(128)S(6)} %select_n.6), kind=kOutput, calls=%fused_computation.2.clone.clone.1 | convolution fusion | flops 408944640 | bytes 7929860 | tf_op jit(solution)/shard_map/while/body/eval_jaxpr/dot_general | solution.py:56
  257.8 10.1 %reshape.99 = bf16[8,1024,384]{2,1,0:T(8,128)(2,1)} reshape(bf16[8,32,12288]{2,1,0:T(8,128)(2,1)} %fusion.85) | data formatting | bytes 12582912 | tf_op jit(solution)/shard_map/while/body/eval_jaxpr/reshape | solution.py:61
  267.9 3.8 %fusion.86 = f32[8,384,128]{1,2,0:T(8,128)S(1)} fusion(bf16[8,1024,384]{2,1,0:T(8,128)(2,1)} %reshape.99, bf16[1024,128]{0,1:T(8,128)(2,1)S(1)} %get-tuple-element.433), kind=kOutput, calls=%fused_computation.22.clone.clone.1 | convolution fusion | flops 805306368 | bytes 8126464 | tf_op jit(solution)/shard_map/while/body/eval_jaxpr/dot_general | solution.py:64
  271.7 5.9 %fusion.84 = bf16[8,32,12288]{2,1,0:T(8,128)(2,1)} fusion(bf16[64,12288,1]{1,0,2:T(8,128)(2,1)} %get-tuple-element.444, bf16[64,32,48]{0,1,2:T(8,128)(2,1)} %get-tuple-element.435, s32[]{:T(128)S(6)} %select_n.6), kind=kOutput, calls=%fused_computation.3.clone.clone.1 | convolution fusion | flops 408944640 | bytes 7929860 | tf_op jit(solution)/shard_map/while/body/eval_jaxpr/dot_general | solution.py:56
  277.6 10.1 %reshape.98 = bf16[8,1024,384]{2,1,0:T(8,128)(2,1)} reshape(bf16[8,32,12288]{2,1,0:T(8,128)(2,1)} %fusion.84) | data formatting | bytes 12582912 | tf_op jit(solution)/shard_map/while/body/eval_jaxpr/reshape | solution.py:61
  287.7 4.0 %bitcast_reduce_fusion.3 = (f32[8,384]{1,0:T(8,128)S(1)}, f32[8,384,128]{1,2,0:T(8,128)S(1)}) fusion(bf16[8,1024,384]{2,1,0:T(8,128)(2,1)} %reshape.98, bf16[1024,128]{0,1:T(8,128)(2,1)} %get-tuple-element.437, f32[8,384,128]{1,2,0:T(8,128)S(1)} %fusion.86, f32[128]{0:T(128)S(1)} %get-tuple-element.434), kind=kOutput, calls=%fused_computation.11.clone.clone.1 | convolution fusion | flops 807662592 | bytes 9712128 | tf_op jit(solution)/shard_map/while/body/eval_jaxpr/dot_general | solution.py:64
  292.7 2.1 fusion.87
  295.2 0.9 constant_dynamic-update-slice_fusion.3
  297.4 5.9 %fusion.85 = bf16[8,32,12288]{2,1,0:T(8,128)(2,1)} fusion(bf16[64,12288,1]{1,0,2:T(8,128)(2,1)} %get-tuple-element.445, bf16[64,32,48]{0,1,2:T(8,128)(2,1)} %get-tuple-element.431, s32[]{:T(128)S(6)} %select_n.6), kind=kOutput, calls=%fused_computation.2.clone.clone.1 | convolution fusion | flops 408944640 | bytes 7929860 | tf_op jit(solution)/shard_map/while/body/eval_jaxpr/dot_general | solution.py:56
  303.3 10.1 %reshape.99 = bf16[8,1024,384]{2,1,0:T(8,128)(2,1)} reshape(bf16[8,32,12288]{2,1,0:T(8,128)(2,1)} %fusion.85) | data formatting | bytes 12582912 | tf_op jit(solution)/shard_map/while/body/eval_jaxpr/reshape | solution.py:61
  313.5 3.8 %fusion.86 = f32[8,384,128]{1,2,0:T(8,128)S(1)} fusion(bf16[8,1024,384]{2,1,0:T(8,128)(2,1)} %reshape.99, bf16[1024,128]{0,1:T(8,128)(2,1)S(1)} %get-tuple-element.433), kind=kOutput, calls=%fused_computation.22.clone.clone.1 | convolution fusion | flops 805306368 | bytes 8126464 | tf_op jit(solution)/shard_map/while/body/eval_jaxpr/dot_general | solution.py:64
  317.2 5.9 %fusion.84 = bf16[8,32,12288]{2,1,0:T(8,128)(2,1)} fusion(bf16[64,12288,1]{1,0,2:T(8,128)(2,1)} %get-tuple-element.444, bf16[64,32,48]{0,1,2:T(8,128)(2,1)} %get-tuple-element.435, s32[]{:T(128)S(6)} %select_n.6), kind=kOutput, calls=%fused_computation.3.clone.clone.1 | convolution fusion | flops 408944640 | bytes 7929860 | tf_op jit(solution)/shard_map/while/body/eval_jaxpr/dot_general | solution.py:56
  323.1 10.1 %reshape.98 = bf16[8,1024,384]{2,1,0:T(8,128)(2,1)} reshape(bf16[8,32,12288]{2,1,0:T(8,128)(2,1)} %fusion.84) | data formatting | bytes 12582912 | tf_op jit(solution)/shard_map/while/body/eval_jaxpr/reshape | solution.py:61
  333.3 4.0 %bitcast_reduce_fusion.3 = (f32[8,384]{1,0:T(8,128)S(1)}, f32[8,384,128]{1,2,0:T(8,128)S(1)}) fusion(bf16[8,1024,384]{2,1,0:T(8,128)(2,1)} %reshape.98, bf16[1024,128]{0,1:T(8,128)(2,1)} %get-tuple-element.437, f32[8,384,128]{1,2,0:T(8,128)S(1)} %fusion.86, f32[128]{0:T(128)S(1)} %get-tuple-element.434), kind=kOutput, calls=%fused_computation.11.clone.clone.1 | convolution fusion | flops 807662592 | bytes 9712128 | tf_op jit(solution)/shard_map/while/body/eval_jaxpr/dot_general | solution.py:64
  338.3 2.1 fusion.87
  340.8 0.9 constant_dynamic-update-slice_fusion.3
  (96 shorter events, 14.3 us)
Async XLA Ops:
  6.5 3.7 %copy-start = (bf16[256,64]{0,1:T(8,128)(2,1)S(1)}, bf16[256,64]{0,1:T(8,128)(2,1)}, u32[]{:S(2)}) copy-start(bf16[256,64]{0,1:T(8,128)(2,1)} %param.18) | copy-start | bytes 98308
  6.5 3.2 copy-start.1
  6.5 3.2 copy-start.7
  6.5 3.2 copy-start.6
  6.5 3.7 %copy-start.8 = (f32[64]{0:T(128)S(1)}, f32[64]{0:T(128)}, u32[]{:S(2)}) copy-start(f32[64]{0:T(128)} %param.19) | copy-start | bytes 772
  6.5 55.7 %all-gather.2.cloned.1.call-start = ((), (), s32[]{:S(2)}) async-start(), calls=%async_computation.1 | async-start | bytes 3342336 | tf_op jit(solution)/shard_map/all_gather | solution.py:113
  21.3 8.4 %copy-start.4 = (bf16[1024,128]{1,0:T(8,128)(2,1)S(1)}, bf16[1024,128]{1,0:T(8,128)(2,1)}, u32[]{:S(2)}) copy-start(bf16[1024,128]{1,0:T(8,128)(2,1)} %param.20) | copy-start | bytes 786436
  23.5 19.4 %all-to-all-start = ((bf16[16,2,6144]{2,1,0:T(2,128)(2,1)}), bf16[16,2,6144]{2,1,0:T(2,128)(2,1)S(1)}, u32[]{:S(2)}, u32[]{:S(2)}) async-start(bf16[16,2,6144]{2,1,0:T(2,128)(2,1)} %reshape.88), calls=%async_computation | async-start | bytes 786432 | tf_op jit(solution)/shard_map/all_to_all | solution.py:116
  64.4 2.1 copy-start.2
  64.4 2.1 copy-start.3
  66.5 1.7 copy-start.5
  66.5 1.7 copy-start.11
  66.5 1.7 copy-start.12
  66.5 1.7 copy-start.13
  66.6 1.7 copy-start.14
  109.5 0.9 copy-start.9
  109.6 1.0 copy-start.10
  155.1 0.9 copy-start.9
  155.1 1.0 copy-start.10
  200.6 0.9 copy-start.9
  200.7 1.0 copy-start.10
  246.2 0.9 copy-start.9
  246.2 1.0 copy-start.10
  291.7 0.9 copy-start.9
  291.7 1.0 copy-start.10
  337.3 0.9 copy-start.9
  337.3 1.0 copy-start.10
Sparse Core Ops, SparseCore 0:
  11.6 50.6 all-gather.1
where the time goes:
time: 352 us; the launch traced here: 349 us
  local copies, waits for them, and re-layouts  155 us (44%)
  matrix products  130 us (37%)
  waiting for transfers between devices  25.4 us (7%)
  between operations  13.6 us (4%)
  blocking collectives  8.77 us (2%)
  starting transfers between devices  6.18 us (2%)
  other arithmetic  4.74 us (1%)
  loops' own time  4.5 us (1%)
    reshape x12, local copies, waits for them, and re-layouts, outer_channels(): product.astype(jnp.bfloat16)  122 us
    dot_general x12, matrix products, outer_channels(): lax.dot_general(rows_side, flat_cols, (((0,), (0,)), ((), ())), preferred...  70.6 us
    dot_general x12, matrix products, outer_channels(): lax.dot_general(weight, product, (((0,), (1,)), ((), ())), preferred_elem...  46.7 us
    all_gather x1, waiting for transfers between devices, shards(): lax.all_gather(local_projected, 'row', axis=0, tiled=True)  13.3 us
    dot_general x6, matrix products, finish(): lax.dot_general(w_down, hidden, (((0,), (0,)), ((), ())), preferred_eleme...  12.8 us
    all_to_all x1, waiting for transfers between devices, shards(): lax.all_to_all(col_wide, 'row', split_axis=3, concat_axis=0, tiled=True)  12.1 us
    all_gather x1, blocking collectives, shards(): col_wide = lax.all_gather(local_projected, 'col', axis=3, tiled=True)  8.77 us
    dynamic_update_slice x12, local copies, waits for them, and re-layouts, shards(): lax.map(pair_block, jnp.arange(row_length // block_size, dtype=jnp.int32))  7.93 us
  transfers between devices with their start and end apart: 2, of which 2 were waited for; matrix products, arithmetic and copies ran while one was open for 3% of the time, Pallas kernels for 0%

commit v1 on v0

v1 whole, which is shorter than its diff:
```python
import functools

import jax
import jax.numpy as jnp
from jax import lax
from jax.experimental import pallas as pl
from jax.experimental.pallas import tpu as pltpu
from jax.sharding import PartitionSpec as P

EPSILON = 1e-05
F32 = jnp.float32
BF16 = jnp.bfloat16


def norm_rows(values, gain, bias):
    average = jnp.mean(values, axis=-1, keepdims=True)
    centered = values - average
    variance = jnp.mean(centered * centered, axis=-1, keepdims=True)
    return centered * lax.rsqrt(variance + EPSILON) * gain + bias


def project_body(core_ref, x_ref, gain_ref, bias_ref, weight_ref, pbias_ref, out_ref):
    local, _, _ = x_ref.shape
    width = weight_ref.shape[1]
    group = 2 * local
    lanes = width * group
    first = core_ref[0] * local
    ch = lax.broadcasted_iota(jnp.int32, (width, lanes), 0)
    lane = lax.broadcasted_iota(jnp.int32, (width, lanes), 1)
    total = None
    for s in range(local):
        normed = norm_rows(x_ref[s].astype(F32), gain_ref[...], bias_ref[...]).astype(BF16)
        y = jnp.dot(normed, weight_ref[...], preferred_element_type=F32) + pbias_ref[...]
        spread = (lane == ch * group + (first + s)).astype(F32).astype(BF16)
        part = jnp.dot(y.astype(BF16), spread, preferred_element_type=F32)
        total = part if total is None else total + part
    half = lanes // 2
    out_ref[0] = total[:, :half].astype(BF16)
    out_ref[1] = total[:, half:].astype(BF16)


def project(core, x, gain, bias, weight, pbias):
    local, residues, _ = x.shape
    lanes = weight.shape[1] * local
    vmem = pl.BlockSpec(memory_space=pltpu.VMEM)
    return pl.pallas_call(
        project_body,
        in_specs=[pl.BlockSpec(memory_space=pltpu.SMEM)] + [vmem] * 5,
        out_specs=vmem,
        out_shape=jax.ShapeDtypeStruct((2, residues, lanes), BF16),
        compiler_params=pltpu.CompilerParams(vmem_limit_bytes=32 << 20),
    )(core, x, gain, bias, weight, pbias)


def pair_body(
    chips, rows_here, rows_ref, *refs
):
    cols = refs[:chips]
    (w_ref, b_out_ref, gain_ref, bias_ref, w_up_ref, b_up_ref, w_down_ref, b_down_ref) = refs[
        chips : chips + 8
    ]
    out_ref, col_scr, t_scr, z_scr = refs[chips + 8 :]
    part = cols[0].shape[2]
    depth = chips * part
    zc = out_ref.shape[2]
    group = part // (w_ref.shape[1] // (2 * zc))
    total = chips * group
    half = part // group

    @pl.when(pl.program_id(0) == 0)
    def _():
        for q in range(chips):
            for d in range(2):
                col_scr[d, :, q * part : (q + 1) * part] = cols[q][d]

    lhs = rows_ref[...].reshape(rows_here * total, rows_ref.shape[2])
    for d in range(2):
        for bp in range(half // 2):
            lane = (d * half + 2 * bp) * zc
            t = jnp.dot(lhs, w_ref[:, lane : lane + 2 * zc], preferred_element_type=F32)
            t = t.reshape(rows_here * chips, group, 2 * zc)
            t = jnp.concatenate([t[:, :, :zc], t[:, :, zc:]], axis=1).astype(BF16)
            t = t.reshape(rows_here, chips, 2 * group, zc)
            for g in range(rows_here):
                for q in range(chips):
                    k = q * part + bp * 2 * group
                    t_scr[d, g // 2, k : k + 2 * group, (g % 2) * zc : (g % 2 + 1) * zc] = t[g, q]
    for p in range(rows_here // 2):
        for d in range(2):
            z_scr[d, p] = jnp.dot(col_scr[d], t_scr[d, p], preferred_element_type=F32)
    for g in range(rows_here):
        lanes = slice((g % 2) * zc, (g % 2 + 1) * zc)
        forward = z_scr[0, g // 2, :, lanes] * (1.0 / total) + b_out_ref[...]
        mirror = z_scr[1, g // 2, :, lanes] * (1.0 / total) + b_out_ref[...]
        pair = jnp.maximum(forward, 0.0) + jnp.maximum(mirror, 0.0)
        normed = norm_rows(pair, gain_ref[...], bias_ref[...]).astype(BF16)
        hidden = jnp.dot(normed, w_up_ref[...], preferred_element_type=F32) + b_up_ref[...]
        hidden = jnp.maximum(hidden, 0.0).astype(BF16)
        update = jnp.dot(hidden, w_down_ref[...], preferred_element_type=F32)
        out_ref[g] = (pair + update + b_down_ref[...]).astype(BF16)


def pair_kernel(rows, cols, w, b_out, gain, bias, w_up, b_up, w_down, b_down):
    row_length, total, width = rows.shape
    chips = len(cols)
    _, column_length, part = cols[0].shape
    zc = w_down.shape[1]
    here = 4
    depth = chips * part

    def whole(a):
        return pl.BlockSpec(a.shape, lambda i: (0,) * a.ndim)

    rest = (w, b_out, gain, bias, w_up, b_up, w_down, b_down)
    return pl.pallas_call(
        functools.partial(pair_body, chips, here),
        grid=(row_length // here,),
        in_specs=[pl.BlockSpec((here, total, width), lambda i: (i, 0, 0))]
        + [whole(a) for a in cols]
        + [whole(a) for a in rest],
        out_specs=pl.BlockSpec((here, column_length, zc), lambda i: (i, 0, 0)),
        out_shape=jax.ShapeDtypeStruct((row_length, column_length, zc), BF16),
        scratch_shapes=[
            pltpu.VMEM((2, column_length, depth), BF16),
            pltpu.VMEM((2, here // 2, depth, 2 * zc), BF16),
            pltpu.VMEM((2, here // 2, column_length, 2 * zc), F32),
        ],
        compiler_params=pltpu.CompilerParams(vmem_limit_bytes=56 << 20),
    )(rows, *cols, *rest)


def chip_ring(chips):
    order = list(range(0, chips, 2)) + list(range(chips - 1, 0, -2))
    after = {order[i]: order[(i + 1) % chips] for i in range(chips)}
    before = {v: k for k, v in after.items()}
    return [
        (2 * q + core, 2 * (after if core == 0 else before)[q] + core)
        for q in range(chips)
        for core in range(2)
    ]


def shards(
    alignment,
    alignment_norm_gain,
    alignment_norm_bias,
    projection_weight,
    projection_bias_pair,
    w_out,
    b_out,
    pair_gain,
    pair_bias,
    w_up,
    b_up,
    w_down,
    b_down,
):
    local, column_length, _ = alignment.shape
    width = projection_weight.shape[1]
    half = width // 2
    row_count = lax.axis_size("row")
    col_count = lax.axis_size("col")
    row_length = column_length * col_count // row_count
    chips = row_count // 2
    zc = w_out.shape[1]
    row_index = lax.axis_index("row")
    col_index = lax.axis_index("col")
    core = row_index % 2

    def swap(a):
        return lax.ppermute(a, "row", [(r, r ^ 1) for r in range(row_count)])

    ring = chip_ring(chips)

    weight = jnp.concatenate([projection_weight[:, half:], projection_weight[:, :half]], axis=1)
    pbias = jnp.concatenate([projection_bias_pair[half:], projection_bias_pair[:half]])
    mine = project(
        core.reshape(1),
        alignment,
        alignment_norm_gain[None],
        alignment_norm_bias[None],
        weight,
        pbias[None],
    )
    own = mine + swap(mine)
    right, left = own[0], own[1]
    cols = [own]
    others = []
    for _ in range(chips // 2 - 1):
        right = lax.ppermute(right, "row", ring)
        left = lax.ppermute(left, "row", ring)
        cols.append(jnp.stack([right, left]))
        others.append(jnp.stack([swap(right), swap(left)]))
    far = lax.ppermute(jnp.where(core == 0, right, left), "row", ring)
    far_other = swap(far)
    far = jnp.stack([jnp.where(core == 0, far, far_other), jnp.where(core == 0, far_other, far)])
    cols = cols + others + [far]

    per_col = column_length // row_length
    start = (row_index % per_col) * row_length
    source = row_index // per_col
    block = jnp.stack([lax.dynamic_slice_in_dim(c, start, row_length, 1) for c in cols])
    if col_count == 2:
        there = lax.ppermute(block, "col", [(0, 1), (1, 0)])
        block = jnp.where(source == col_index, block, there)
    else:
        block = lax.dynamic_index_in_dim(lax.all_gather(block, "col"), source, 0, False)
    group = 2 * local
    rows = block.reshape(chips, 2, row_length, half, group).transpose(2, 0, 4, 1, 3)
    rows = rows.reshape(row_length, chips * group, width)

    w3 = w_out.reshape(half, half, zc)
    w_forward = w3.reshape(half, half * zc)
    w_mirror = w3.transpose(1, 0, 2).reshape(half, half * zc)
    zero = jnp.zeros_like(w_forward)
    w = jnp.concatenate(
        [
            jnp.concatenate([zero, w_mirror], axis=1),
            jnp.concatenate([w_forward, zero], axis=1),
        ],
        axis=0,
    )
    return pair_kernel(
        rows,
        cols,
        w,
        b_out[None],
        pair_gain[None],
        pair_bias[None],
        w_up,
        b_up[None],
        w_down,
        b_down[None],
    )


def solution(mesh):
    return jax.shard_map(
        shards,
        mesh=mesh,
        in_specs=(P("row", "col", None),) + (P(),) * 12,
        out_specs=P("row", "col", None),
        check_vma=False,
    )
```

time: 352 us -> 100 us (0.28)
  local copies, waits for them, and re-layouts: 155 us -> 8.32 us
  matrix products: 130 us -> 0 us
  Pallas kernels: 0 us -> 51.6 us
  between operations: 13.6 us -> 0.19 us
  starting transfers between devices: 6.18 us -> 17.7 us
  waiting for transfers between devices: 25.4 us -> 14.8 us
  blocking collectives: 8.77 us -> 0 us
  loops' own time: 4.5 us -> 0 us
    dot_general x31 -> x0, matrix products: 130 us -> none  [the longest x12 70.6 us: outer_channels(): lax.dot_general(rows_side, flat_cols, (((0,), (0,)), ((), ())), preferred...]
    reshape x14 -> x2, local copies, waits for them, and re-layouts: 122 us -> 2.1 us  [the longest x1 2 us: shards(): rows = rows.reshape(row_length, chips * group, width)]
    pallas_call x0 -> x2, Pallas kernels: none -> 51.6 us  [the longest x1 50.4 us: pair_kernel(): pl.pallas_call(functools.partial(pair_body, chips, here), grid=(row_lengt...]
    ppermute x0 -> x16, starting transfers between devices: none -> 17.7 us  [the longest x3 7.13 us: shards(): right = lax.ppermute(right, 'row', ring)]
    ppermute x0 -> x16, waiting for transfers between devices: none -> 14.8 us  [the longest x1 6.28 us: shards(): there = lax.ppermute(block, 'col', [(0, 1), (1, 0)])]
    all_gather x1 -> x0, waiting for transfers between devices: 13.3 us -> none  [shards(): lax.all_gather(local_projected, 'row', axis=0, tiled=True)]
    all_to_all x1 -> x0, waiting for transfers between devices: 12.1 us -> none  [shards(): lax.all_to_all(col_wide, 'row', split_axis=3, concat_axis=0, tiled=True)]
    while x29 -> x0, local copies, waits for them, and re-layouts: 11 us -> none  [the longest x5 6.55 us: shards(): lax.map(pair_block, jnp.arange(row_length // block_size, dtype=jnp.int32))]
  transfers between devices with their start and end apart: 2 -> 16, of which waited for: 2 -> 7; matrix products, arithmetic and copies ran while one was open for 3% -> 8% of each run, Pallas kernels for 0% -> 0%
where the time goes in v1:
time: 100 us; the launch traced here: 99.7 us
  Pallas kernels  51.6 us (52%)
  starting transfers between devices  17.7 us (18%)
  waiting for transfers between devices  14.8 us (15%)
  local copies, waits for them, and re-layouts  8.32 us (8%)
  other arithmetic  7.01 us (7%)
    pallas_call x1, Pallas kernels, pair_kernel(): pl.pallas_call(functools.partial(pair_body, chips, here), grid=(row_lengt...  50.4 us
    ppermute x3, starting transfers between devices, shards(): right = lax.ppermute(right, 'row', ring)  7.13 us
    ppermute x1, waiting for transfers between devices, shards(): there = lax.ppermute(block, 'col', [(0, 1), (1, 0)])  6.28 us
    ppermute x3, starting transfers between devices, shards(): left = lax.ppermute(left, 'row', ring)  5.43 us
    ppermute x1, waiting for transfers between devices, shards(): far = lax.ppermute(jnp.where(core == 0, right, left), 'row', ring)  3.22 us
    unnamed x14, local copies, waits for them, and re-layouts  2.84 us
    another operation x3, other arithmetic, shards(): cols.append(jnp.stack([right, left]))  2.38 us
    another operation x3, other arithmetic, shards(): others.append(jnp.stack([swap(right), swap(left)]))  2.37 us
  transfers between devices with their start and end apart: 16, of which 7 were waited for; matrix products, arithmetic and copies ran while one was open for 8% of the time, Pallas kernels for 0%

profile of v1, /device:TPU:0, one launch (start us, length us, event | category | flops | bytes accessed | tf_op | source)
XLA Modules:
  0.0 99.7 jit_solution(11014000437729789522)
XLA Ops:
  0.0 0.0 copy-start.4
  0.0 0.8 fusion.11
  0.8 0.7 fusion.10
  1.5 0.1 copy.28
  1.7 0.1 copy.29
  1.8 0.1 maximum_bitcast_fusion.pbias_ref
  1.9 0.1 pad_maximum_fusion.7.weight_ref
  2.0 0.0 copy-start
  2.0 1.1 %copy-done = bf16[4,384,256]{2,1,0:T(8,128)(2,1)S(1)} copy-done((bf16[4,384,256]{2,1,0:T(8,128)(2,1)S(1)}, bf16[4,384,256]{2,1,0:T(8,128)(2,1)}, u32[]{:S(2)}) %copy-start) | copy-done | bytes 786456
  3.1 0.0 copy-start.1
  3.1 0.7 copy-done.1
  3.8 0.7 copy-done.2
  4.5 1.2 %shard_map.127 = bf16[2,384,256]{2,1,0:T(8,128)(2,1)S(1)} custom-call(s32[1]{0:T(128)} %bitcast.core_ref, bf16[4,384,256]{2,1,0:T(8,128)(2,1)S(1)} %copy-done, f32[1,256]{1,0:T(1,128)S(1)} %bitcast.56, f32[1,256]{1,0:T(1,128)S(1)} %bitcast.57, bf16[256,64]{1,0:T(8,128)(2,1)S(1)} %pad_maximum_fusion.7.weight_ref, f32[1,64]{1,0:T(1,128)S(1)} %maximum_bitcast_fusion.pbias_ref), custom_call_target="tpu_custom_call" | custom-call | tf_op jit(solution)/shard_map/pallas_call | solution.py:46
  5.6 0.5 collective-permute-start
  6.2 1.1 %reshape_reshape.3 = bf16[32,4096]{1,0:T(8,128)(2,1)S(1)} reshape(bf16[1024,128]{1,0:T(8,128)(2,1)} %param.18) | data formatting | bytes 524288 | tf_op jit(solution)/shard_map/reshape;reshape | solution.py:213
  7.2 0.0 copy-done.4
  7.2 0.1 copy.26
  7.3 0.1 copy.32
  7.5 0.0 collective-permute-done
  7.5 0.1 add.26.refs_0_
  7.6 0.0 copy-start.3
  7.7 3.0 %collective-permute-start.1 = (bf16[384,256]{1,0:T(8,128)(2,1)S(1)}, bf16[384,256]{1,0:T(8,128)(2,1)S(1)}, u32[]{:S(2)}, u32[]{:S(2)}) collective-permute-start(bf16[384,256]{1,0:T(8,128)(2,1)S(1)} %get-tuple-element.7), channel_id=1, source_target_pairs={{0,8},{2,6},{4,0},{6,14},{8,16},{10,2},{12,4},{14,22},{16,24},{18,... | collective-permute-start | bytes 589832 | tf_op jit(solution)/shard_map/ppermute | solution.py:190
  10.6 1.6 %collective-permute-start.2 = (bf16[384,256]{1,0:T(8,128)(2,1)S(1)}, bf16[384,256]{1,0:T(8,128)(2,1)S(1)}, u32[]{:S(2)}, u32[]{:S(2)}) collective-permute-start(bf16[384,256]{1,0:T(8,128)(2,1)S(1)} %get-tuple-element.8), channel_id=1, source_target_pairs={{0,8},{2,6},{4,0},{6,14},{8,16},{10,2},{12,4},{14,22},{16,24},{18,... | collective-permute-start | bytes 589832 | tf_op jit(solution)/shard_map/ppermute | solution.py:191
  12.2 1.1 %fusion.2.refs_8_ = bf16[64,8192]{1,0:T(8,128)(2,1)} fusion(bf16[32,4096]{1,0:T(8,128)(2,1)S(1)} %reshape_reshape.3, bf16[32,4096]{1,0:T(8,128)(2,1)S(1)} %bitcast.66), kind=kLoop, calls=%fused_computation.4 | loop fusion | flops 4194304 | bytes 1572864 | tf_op jit(solution)/shard_map/concatenate | solution.py:216
  13.3 1.0 collective-permute-done.1
  14.2 0.0 collective-permute-start.7
  14.3 2.1 %collective-permute-start.3 = (bf16[384,256]{1,0:T(8,128)(2,1)S(1)}, bf16[384,256]{1,0:T(8,128)(2,1)S(1)}, u32[]{:S(2)}, u32[]{:S(2)}) collective-permute-start(bf16[384,256]{1,0:T(8,128)(2,1)S(1)} %collective-permute-done.1), channel_id=1, source_target_pairs={{0,8},{2,6},{4,0},{6,14},{8,16},{10,2},{12,4},{14,22},{16,24},{18,... | collective-permute-start | bytes 589832 | tf_op jit(solution)/shard_map/ppermute | solution.py:190
  16.3 0.0 collective-permute-done.2
  16.4 0.1 collective-permute-start.8
  16.5 1.9 %collective-permute-start.4 = (bf16[384,256]{1,0:T(8,128)(2,1)S(1)}, bf16[384,256]{1,0:T(8,128)(2,1)S(1)}, u32[]{:S(2)}, u32[]{:S(2)}) collective-permute-start(bf16[384,256]{1,0:T(8,128)(2,1)S(1)} %collective-permute-done.2), channel_id=1, source_target_pairs={{0,8},{2,6},{4,0},{6,14},{8,16},{10,2},{12,4},{14,22},{16,24},{18,... | collective-permute-start | bytes 589832 | tf_op jit(solution)/shard_map/ppermute | solution.py:191
  18.4 0.8 pad_maximum_fusion.refs_1_
  19.2 0.7 collective-permute-done.3
  19.9 0.0 collective-permute-start.9
  19.9 2.1 %collective-permute-start.5 = (bf16[384,256]{1,0:T(8,128)(2,1)S(1)}, bf16[384,256]{1,0:T(8,128)(2,1)S(1)}, u32[]{:S(2)}, u32[]{:S(2)}) collective-permute-start(bf16[384,256]{1,0:T(8,128)(2,1)S(1)} %collective-permute-done.3), channel_id=1, source_target_pairs={{0,8},{2,6},{4,0},{6,14},{8,16},{10,2},{12,4},{14,22},{16,24},{18,... | collective-permute-start | bytes 589832 | tf_op jit(solution)/shard_map/ppermute | solution.py:190
  22.0 0.2 collective-permute-done.4
  22.2 1.9 %collective-permute-start.6 = (bf16[384,256]{1,0:T(8,128)(2,1)S(1)}, bf16[384,256]{1,0:T(8,128)(2,1)S(1)}, u32[]{:S(2)}, u32[]{:S(2)}) collective-permute-start(bf16[384,256]{1,0:T(8,128)(2,1)S(1)} %collective-permute-done.4), channel_id=1, source_target_pairs={{0,8},{2,6},{4,0},{6,14},{8,16},{10,2},{12,4},{14,22},{16,24},{18,... | collective-permute-start | bytes 589832 | tf_op jit(solution)/shard_map/ppermute | solution.py:191
  24.1 0.8 pad_maximum_fusion.1.refs_2_
  24.9 0.0 copy-done.3
  24.9 0.0 collective-permute-done.7
  24.9 0.1 collective-permute-start.10
  25.0 0.0 collective-permute-done.8
  25.0 0.8 pad_maximum_fusion.3.refs_4_
  25.8 0.0 collective-permute-done.5
  25.8 2.0 %collective-permute-done.6 = bf16[384,256]{1,0:T(8,128)(2,1)S(1)} collective-permute-done((bf16[384,256]{1,0:T(8,128)(2,1)S(1)}, bf16[384,256]{1,0:T(8,128)(2,1)S(1)}, u32[]{:S(2)}, u32[]{:S(2)}) %collective-permute-start.6) | collective-permute-done | bytes 196640 | tf_op jit(solution)/shard_map/ppermute | solution.py:191
  27.9 2.0 %collective-permute-start.13 = (bf16[384,256]{1,0:T(8,128)(2,1)S(1)}, bf16[384,256]{1,0:T(8,128)(2,1)S(1)}, u32[]{:S(2)}, u32[]{:S(2)}) collective-permute-start(bf16[384,256]{1,0:T(8,128)(2,1)S(1)} %broadcast_select_fusion.1), channel_id=1, source_target_pairs={{0,8},{2,6},{4,0},{6,14},{8,16},{10,2},{12,4},{14,22},{16,24},{18,... | collective-permute-start | bytes 589832 | tf_op jit(solution)/shard_map/ppermute | solution.py:194
  29.9 0.0 collective-permute-start.11
  29.9 0.5 collective-permute-start.12
  30.4 3.2 %collective-permute-done.13 = bf16[384,256]{1,0:T(8,128)(2,1)S(1)} collective-permute-done((bf16[384,256]{1,0:T(8,128)(2,1)S(1)}, bf16[384,256]{1,0:T(8,128)(2,1)S(1)}, u32[]{:S(2)}, u32[]{:S(2)}) %collective-permute-start.13) | collective-permute-done | bytes 196640 | tf_op jit(solution)/shard_map/ppermute | solution.py:194
  33.6 0.0 collective-permute-start.14
  33.6 0.0 collective-permute-done.9
  33.6 0.0 collective-permute-done.10
  33.6 0.0 collective-permute-done.11
  33.6 0.0 collective-permute-done.12
  33.7 1.4 %collective-permute-done.14 = bf16[384,256]{1,0:T(8,128)(2,1)S(1)} collective-permute-done((bf16[384,256]{1,0:T(8,128)(2,1)S(1)}, bf16[384,256]{1,0:T(8,128)(2,1)S(1)}, u32[]{:S(2)}, u32[]{:S(2)}) %collective-permute-start.14) | collective-permute-done | bytes 196640 | tf_op jit(solution)/shard_map/ppermute | solution.py:171
  35.1 1.9 %collective-permute-start.15 = (bf16[8,2,48,256]{3,2,1,0:T(8,128)(2,1)S(1)}, bf16[8,2,48,256]{3,2,1,0:T(8,128)(2,1)S(1)}, u32[]{:S(2)}, u32[]{:S(2)}) collective-permute-start(bf16[8,2,48,256]{3,2,1,0:T(8,128)(2,1)S(1)} %bitcast_dynamic-update-slice_fusion), channel_id=1, source_target_pairs={{0,1},{1,0},{2,3},{3,2},{4,5},{5,4},{6,7},{7,6},{8,9},{9,8},{10,11... | collective-permute-start | bytes 1179656 | tf_op jit(solution)/shard_map/ppermute | solution.py:204
  37.0 0.8 pad_maximum_fusion.4.refs_5_
  37.8 0.8 pad_maximum_fusion.2.refs_3_
  38.6 0.8 pad_maximum_fusion.5.refs_6_
  39.4 0.8 pad_maximum_fusion.6.refs_7_
  40.1 6.3 %collective-permute-done.15 = bf16[8,2,48,256]{3,2,1,0:T(8,128)(2,1)S(1)} collective-permute-done((bf16[8,2,48,256]{3,2,1,0:T(8,128)(2,1)S(1)}, bf16[8,2,48,256]{3,2,1,0:T(8,128)(2,1)S(1)}, u32[]{:S(2)}, u32[]{:S(2)}) %collective-permute-start.15) | collective-permute-done | bytes 393248 | tf_op jit(solution)/shard_map/ppermute | solution.py:204
  46.5 0.5 copy.24
  47.0 0.3 copy.25
  47.2 2.0 %copy.27.rows_ref = bf16[48,64,64]{2,1,0:T(8,128)(2,1)} copy(bf16[48,64,64]{0,2,1:T(8,128)(2,1)S(1)} %bitcast.58) | data formatting | bytes 786432 | tf_op jit(solution)/shard_map/reshape | solution.py:210
  49.2 50.4 %shard_map.128 = bf16[48,384,128]{2,1,0:T(8,128)(2,1)} custom-call(bf16[48,64,64]{2,1,0:T(8,128)(2,1)} %copy.27.rows_ref, bf16[2,384,256]{2,1,0:T(8,128)(2,1)} %copy-done.3, bf16[2,384,256]{2,1,0:T(8,128)(2,1)} %pad_maximum_fusion.refs_1_, bf16[2,384,256]{2,1,0:T(8,128)(2,1)} %pad_maximum_fusion.1.refs_2_, bf16[2,384,256]{2,1,0:T(8,128)(2,1)} %pad_maximum_fusion.2.refs_3_, ...), custom_call_target="tpu_custom_call" | custom-call | tf_op jit(solution)/shard_map/pallas_call | solution.py:115
  (13 shorter events, 0.2 us)
Async XLA Ops:
  0.0 7.2 %copy-start.4 = (bf16[1024,128]{1,0:T(8,128)(2,1)S(1)}, bf16[1024,128]{1,0:T(8,128)(2,1)}, u32[]{:S(2)}) copy-start(bf16[1024,128]{1,0:T(8,128)(2,1)} %param.18) | copy-start | bytes 786436
  2.0 1.1 %copy-start = (bf16[4,384,256]{2,1,0:T(8,128)(2,1)S(1)}, bf16[4,384,256]{2,1,0:T(8,128)(2,1)}, u32[]{:S(2)}) copy-start(bf16[4,384,256]{2,1,0:T(8,128)(2,1)} %x_ref.1) | copy-start | bytes 2359300
  3.1 0.7 copy-start.1
  3.8 0.7 copy-start.2
  5.6 1.9 %collective-permute-start = (bf16[2,384,256]{2,1,0:T(8,128)(2,1)S(1)}, bf16[2,384,256]{2,1,0:T(8,128)(2,1)S(1)}, u32[]{:S(2)}, u32[]{:S(2)}) collective-permute-start(bf16[2,384,256]{2,1,0:T(8,128)(2,1)S(1)} %shard_map.127), channel_id=1, source_target_pairs={{0,2},{2,0},{4,6},{6,4},{8,10},{10,8},{12,14},{14,12},{16,18},{18,... | collective-permute-start | bytes 1179656 | tf_op jit(solution)/shard_map/ppermute | solution.py:171
  7.6 17.3 %copy-start.3 = (bf16[2,384,256]{2,1,0:T(8,128)(2,1)}, bf16[2,384,256]{2,1,0:T(8,128)(2,1)S(1)}, u32[]{:S(2)}) copy-start(bf16[2,384,256]{2,1,0:T(8,128)(2,1)S(1)} %add.26.refs_0_) | copy-start | bytes 1179652
  7.7 6.6 %collective-permute-start.1 = (bf16[384,256]{1,0:T(8,128)(2,1)S(1)}, bf16[384,256]{1,0:T(8,128)(2,1)S(1)}, u32[]{:S(2)}, u32[]{:S(2)}) collective-permute-start(bf16[384,256]{1,0:T(8,128)(2,1)S(1)} %get-tuple-element.7), channel_id=1, source_target_pairs={{0,8},{2,6},{4,0},{6,14},{8,16},{10,2},{12,4},{14,22},{16,24},{18,... | collective-permute-start | bytes 589832 | tf_op jit(solution)/shard_map/ppermute | solution.py:190
  10.6 5.7 %collective-permute-start.2 = (bf16[384,256]{1,0:T(8,128)(2,1)S(1)}, bf16[384,256]{1,0:T(8,128)(2,1)S(1)}, u32[]{:S(2)}, u32[]{:S(2)}) collective-permute-start(bf16[384,256]{1,0:T(8,128)(2,1)S(1)} %get-tuple-element.8), channel_id=1, source_target_pairs={{0,8},{2,6},{4,0},{6,14},{8,16},{10,2},{12,4},{14,22},{16,24},{18,... | collective-permute-start | bytes 589832 | tf_op jit(solution)/shard_map/ppermute | solution.py:191
  14.2 10.7 %collective-permute-start.7 = (bf16[384,256]{1,0:T(8,128)(2,1)S(1)}, bf16[384,256]{1,0:T(8,128)(2,1)S(1)}, u32[]{:S(2)}, u32[]{:S(2)}) collective-permute-start(bf16[384,256]{1,0:T(8,128)(2,1)S(1)} %collective-permute-done.1), channel_id=1, source_target_pairs={{0,2},{2,0},{4,6},{6,4},{8,10},{10,8},{12,14},{14,12},{16,18},{18,... | collective-permute-start | bytes 589832 | tf_op jit(solution)/shard_map/ppermute | solution.py:171
  14.3 5.7 %collective-permute-start.3 = (bf16[384,256]{1,0:T(8,128)(2,1)S(1)}, bf16[384,256]{1,0:T(8,128)(2,1)S(1)}, u32[]{:S(2)}, u32[]{:S(2)}) collective-permute-start(bf16[384,256]{1,0:T(8,128)(2,1)S(1)} %collective-permute-done.1), channel_id=1, source_target_pairs={{0,8},{2,6},{4,0},{6,14},{8,16},{10,2},{12,4},{14,22},{16,24},{18,... | collective-permute-start | bytes 589832 | tf_op jit(solution)/shard_map/ppermute | solution.py:190
  16.4 8.6 %collective-permute-start.8 = (bf16[384,256]{1,0:T(8,128)(2,1)S(1)}, bf16[384,256]{1,0:T(8,128)(2,1)S(1)}, u32[]{:S(2)}, u32[]{:S(2)}) collective-permute-start(bf16[384,256]{1,0:T(8,128)(2,1)S(1)} %collective-permute-done.2), channel_id=1, source_target_pairs={{0,2},{2,0},{4,6},{6,4},{8,10},{10,8},{12,14},{14,12},{16,18},{18,... | collective-permute-start | bytes 589832 | tf_op jit(solution)/shard_map/ppermute | solution.py:171
  16.5 5.7 %collective-permute-start.4 = (bf16[384,256]{1,0:T(8,128)(2,1)S(1)}, bf16[384,256]{1,0:T(8,128)(2,1)S(1)}, u32[]{:S(2)}, u32[]{:S(2)}) collective-permute-start(bf16[384,256]{1,0:T(8,128)(2,1)S(1)} %collective-permute-done.2), channel_id=1, source_target_pairs={{0,8},{2,6},{4,0},{6,14},{8,16},{10,2},{12,4},{14,22},{16,24},{18,... | collective-permute-start | bytes 589832 | tf_op jit(solution)/shard_map/ppermute | solution.py:191
  19.9 13.7 %collective-permute-start.9 = (bf16[384,256]{1,0:T(8,128)(2,1)S(1)}, bf16[384,256]{1,0:T(8,128)(2,1)S(1)}, u32[]{:S(2)}, u32[]{:S(2)}) collective-permute-start(bf16[384,256]{1,0:T(8,128)(2,1)S(1)} %collective-permute-done.3), channel_id=1, source_target_pairs={{0,2},{2,0},{4,6},{6,4},{8,10},{10,8},{12,14},{14,12},{16,18},{18,... | collective-permute-start | bytes 589832 | tf_op jit(solution)/shard_map/ppermute | solution.py:171
  19.9 5.9 %collective-permute-start.5 = (bf16[384,256]{1,0:T(8,128)(2,1)S(1)}, bf16[384,256]{1,0:T(8,128)(2,1)S(1)}, u32[]{:S(2)}, u32[]{:S(2)}) collective-permute-start(bf16[384,256]{1,0:T(8,128)(2,1)S(1)} %collective-permute-done.3), channel_id=1, source_target_pairs={{0,8},{2,6},{4,0},{6,14},{8,16},{10,2},{12,4},{14,22},{16,24},{18,... | collective-permute-start | bytes 589832 | tf_op jit(solution)/shard_map/ppermute | solution.py:190
  22.2 5.7 %collective-permute-start.6 = (bf16[384,256]{1,0:T(8,128)(2,1)S(1)}, bf16[384,256]{1,0:T(8,128)(2,1)S(1)}, u32[]{:S(2)}, u32[]{:S(2)}) collective-permute-start(bf16[384,256]{1,0:T(8,128)(2,1)S(1)} %collective-permute-done.4), channel_id=1, source_target_pairs={{0,8},{2,6},{4,0},{6,14},{8,16},{10,2},{12,4},{14,22},{16,24},{18,... | collective-permute-start | bytes 589832 | tf_op jit(solution)/shard_map/ppermute | solution.py:191
  24.9 8.7 %collective-permute-start.10 = (bf16[384,256]{1,0:T(8,128)(2,1)S(1)}, bf16[384,256]{1,0:T(8,128)(2,1)S(1)}, u32[]{:S(2)}, u32[]{:S(2)}) collective-permute-start(bf16[384,256]{1,0:T(8,128)(2,1)S(1)} %collective-permute-done.4), channel_id=1, source_target_pairs={{0,2},{2,0},{4,6},{6,4},{8,10},{10,8},{12,14},{14,12},{16,18},{18,... | collective-permute-start | bytes 589832 | tf_op jit(solution)/shard_map/ppermute | solution.py:171
  27.9 5.7 %collective-permute-start.13 = (bf16[384,256]{1,0:T(8,128)(2,1)S(1)}, bf16[384,256]{1,0:T(8,128)(2,1)S(1)}, u32[]{:S(2)}, u32[]{:S(2)}) collective-permute-start(bf16[384,256]{1,0:T(8,128)(2,1)S(1)} %broadcast_select_fusion.1), channel_id=1, source_target_pairs={{0,8},{2,6},{4,0},{6,14},{8,16},{10,2},{12,4},{14,22},{16,24},{18,... | collective-permute-start | bytes 589832 | tf_op jit(solution)/shard_map/ppermute | solution.py:194
  29.9 3.8 %collective-permute-start.11 = (bf16[384,256]{1,0:T(8,128)(2,1)S(1)}, bf16[384,256]{1,0:T(8,128)(2,1)S(1)}, u32[]{:S(2)}, u32[]{:S(2)}) collective-permute-start(bf16[384,256]{1,0:T(8,128)(2,1)S(1)} %collective-permute-done.5), channel_id=1, source_target_pairs={{0,2},{2,0},{4,6},{6,4},{8,10},{10,8},{12,14},{14,12},{16,18},{18,... | collective-permute-start | bytes 589832 | tf_op jit(solution)/shard_map/ppermute | solution.py:171
  29.9 3.8 %collective-permute-start.12 = (bf16[384,256]{1,0:T(8,128)(2,1)S(1)}, bf16[384,256]{1,0:T(8,128)(2,1)S(1)}, u32[]{:S(2)}, u32[]{:S(2)}) collective-permute-start(bf16[384,256]{1,0:T(8,128)(2,1)S(1)} %collective-permute-done.6), channel_id=1, source_target_pairs={{0,2},{2,0},{4,6},{6,4},{8,10},{10,8},{12,14},{14,12},{16,18},{18,... | collective-permute-start | bytes 589832 | tf_op jit(solution)/shard_map/ppermute | solution.py:171
  33.6 1.4 %collective-permute-start.14 = (bf16[384,256]{1,0:T(8,128)(2,1)S(1)}, bf16[384,256]{1,0:T(8,128)(2,1)S(1)}, u32[]{:S(2)}, u32[]{:S(2)}) collective-permute-start(bf16[384,256]{1,0:T(8,128)(2,1)S(1)} %collective-permute-done.13), channel_id=1, source_target_pairs={{0,2},{2,0},{4,6},{6,4},{8,10},{10,8},{12,14},{14,12},{16,18},{18,... | collective-permute-start | bytes 589832 | tf_op jit(solution)/shard_map/ppermute | solution.py:171
  35.1 11.3 %collective-permute-start.15 = (bf16[8,2,48,256]{3,2,1,0:T(8,128)(2,1)S(1)}, bf16[8,2,48,256]{3,2,1,0:T(8,128)(2,1)S(1)}, u32[]{:S(2)}, u32[]{:S(2)}) collective-permute-start(bf16[8,2,48,256]{3,2,1,0:T(8,128)(2,1)S(1)} %bitcast_dynamic-update-slice_fusion), channel_id=1, source_target_pairs={{0,1},{1,0},{2,3},{3,2},{4,5},{5,4},{6,7},{7,6},{8,9},{9,8},{10,11... | collective-permute-start | bytes 1179656 | tf_op jit(solution)/shard_map/ppermute | solution.py:204

commit v2 on v1

v2 whole, which is shorter than its diff:
```python
import functools

import jax
import jax.numpy as jnp
from jax import lax
from jax.experimental import pallas as pl
from jax.experimental.pallas import tpu as pltpu
from jax.sharding import PartitionSpec as P

EPSILON = 1e-05
F32 = jnp.float32
BF16 = jnp.bfloat16
F8 = jnp.float8_e4m3fn


def norm_rows(values, gain, bias):
    average = jnp.mean(values, axis=-1, keepdims=True)
    centered = values - average
    variance = jnp.mean(centered * centered, axis=-1, keepdims=True)
    return centered * lax.rsqrt(variance + EPSILON) * gain + bias


def project_body(core_ref, x_ref, gain_ref, bias_ref, weight_ref, pbias_ref, out_ref):
    local, _, _ = x_ref.shape
    width = weight_ref.shape[1]
    group = 2 * local
    lanes = width * group
    first = core_ref[0] * local
    ch = lax.broadcasted_iota(jnp.int32, (width, lanes), 0)
    lane = lax.broadcasted_iota(jnp.int32, (width, lanes), 1)
    total = None
    for s in range(local):
        normed = norm_rows(x_ref[s].astype(F32), gain_ref[...], bias_ref[...]).astype(BF16)
        y = jnp.dot(normed, weight_ref[...], preferred_element_type=F32) + pbias_ref[...]
        spread = (lane == ch * group + (first + s)).astype(F32).astype(BF16)
        part = jnp.dot(y.astype(BF16), spread, preferred_element_type=F32)
        total = part if total is None else total + part
    half = lanes // 2
    out_ref[0] = total[:, :half].astype(BF16)
    out_ref[1] = total[:, half:].astype(BF16)


def project(core, x, gain, bias, weight, pbias):
    local, residues, _ = x.shape
    lanes = weight.shape[1] * local
    vmem = pl.BlockSpec(memory_space=pltpu.VMEM)
    return pl.pallas_call(
        project_body,
        in_specs=[pl.BlockSpec(memory_space=pltpu.SMEM)] + [vmem] * 5,
        out_specs=vmem,
        out_shape=jax.ShapeDtypeStruct((2, residues, lanes), BF16),
        compiler_params=pltpu.CompilerParams(vmem_limit_bytes=32 << 20),
    )(core, x, gain, bias, weight, pbias)


def power_of_two(largest):
    scale = jnp.ones_like(largest)
    inverse = jnp.ones_like(largest)
    for k in (32, 16, 8, 4, 2, 1):
        fits = largest * (scale * float(2**k)) <= 448.0
        scale = jnp.where(fits, scale * float(2**k), scale)
        inverse = jnp.where(fits, inverse * float(2.0**-k), inverse)
    return scale, inverse


def split_weight_body(total, w_ref, w8_ref, undo_ref, scr):
    half = w8_ref.shape[0] // 8
    zc = w_ref.shape[1]
    scr[...] = w_ref[...].astype(F32)
    scale, inverse = power_of_two(jnp.max(jnp.abs(scr[...]), axis=0, keepdims=True))
    undo_ref[...] = inverse * (1.0 / total)
    zero = jnp.zeros((4 * half, half * zc), w8_ref.dtype)
    w8_ref[4 * half :, : half * zc] = zero
    w8_ref[: 4 * half, half * zc :] = zero
    for d in range(2):
        for k in range(half):
            if d == 0:
                block = scr[pl.ds(k, half, stride=half), :]
            else:
                block = scr[k * half : (k + 1) * half, :]
            block = block * scale
            high = block.astype(w8_ref.dtype)
            low = (block - high.astype(F32)).astype(w8_ref.dtype)
            lanes = slice((d * half + k) * zc, (d * half + k + 1) * zc)
            row = d * 4 * half
            w8_ref[row : row + half, lanes] = high
            w8_ref[row + half : row + 2 * half, lanes] = high
            w8_ref[row + 2 * half : row + 3 * half, lanes] = low
            w8_ref[row + 3 * half : row + 4 * half, lanes] = low


def split_weight(w_out, half, total):
    zc = w_out.shape[1]
    vmem = pl.BlockSpec(memory_space=pltpu.VMEM)
    return pl.pallas_call(
        functools.partial(split_weight_body, total),
        in_specs=[vmem],
        out_specs=[vmem, vmem],
        out_shape=[
            jax.ShapeDtypeStruct((8 * half, 2 * half * zc), F8),
            jax.ShapeDtypeStruct((1, zc), F32),
        ],
        scratch_shapes=[pltpu.VMEM(w_out.shape, F32)],
        compiler_params=pltpu.CompilerParams(vmem_limit_bytes=32 << 20),
    )(w_out)


def prepare_rows(chips, group, row_refs, undo_ref, y_scr, lhs_scr, undo_scr):
    row_length = row_refs[0].shape[2]
    part = row_refs[0].shape[3]
    half = part // group
    lanes = 4 * half
    k = lax.broadcasted_iota(jnp.int32, (part, lanes), 0)
    lane = lax.broadcasted_iota(jnp.int32, (part, lanes), 1)
    offset = k - lax.rem(lane, half) * group
    count = chips * row_length
    for side in range(2):
        x = jnp.concatenate(
            [r[q, 1 - side] for r in row_refs for q in range(r.shape[0])], axis=0
        )
        for s in range(group):
            pick = jnp.where(offset == s, 1.0, 0.0).astype(BF16)
            y_scr[side, pl.ds(s, count, stride=group), :] = jnp.dot(
                x, pick, preferred_element_type=F32
            )
        largest = None
        for q in range(chips):
            y = y_scr[side, q * row_length * group : (q + 1) * row_length * group, :]
            m = jnp.max(jnp.abs(y).reshape(row_length, group, lanes), axis=1)
            largest = m if largest is None else jnp.maximum(largest, m)
        largest = jnp.max(largest, axis=-1, keepdims=True)
        scale, inverse = power_of_two(jnp.broadcast_to(largest, (row_length, lanes)))
        undo_scr[side] = inverse * undo_ref[...]
        spread = jnp.broadcast_to(scale[:, None, :], (row_length, group, lanes)).reshape(
            row_length * group, lanes
        )
        here = lax.broadcasted_iota(jnp.int32, (row_length * group, lanes), 1)
        is_high = lax.rem(lax.div(here, half), 2) == 0
        for q in range(chips):
            y = y_scr[side, q * row_length * group : (q + 1) * row_length * group, :] * spread
            high = y.astype(F8).astype(F32)
            both = jnp.where(is_high, high, y - high).astype(F8)
            lhs_scr[q, :, side * lanes : (side + 1) * lanes] = both


def pair_body(chips, here, group, row_parts, core_ref, *refs):
    row_refs = refs[:row_parts]
    refs = refs[row_parts:]
    own_ref, *col_refs = refs[: chips * 2 - 1]
    (w_ref, undo_ref, b_out_ref, gain_ref, bias_ref, w_up_ref, b_up_ref, w_down_ref, b_down_ref) = (
        refs[chips * 2 - 1 : chips * 2 + 8]
    )
    out_ref, col_scr, y_scr, lhs_scr, undo_scr, t_scr, z_scr = refs[chips * 2 + 8 :]
    part = own_ref.shape[2]
    zc = out_ref.shape[2]
    half = part // group
    step = pl.program_id(0)

    @pl.when(step == 0)
    def _():
        for d in range(2):
            col_scr[d, :, :part] = own_ref[d]
            for q in range(1, chips - 1):
                col_scr[d, :, q * part : (q + 1) * part] = col_refs[2 * (q - 1) + d][...]

        far = slice((chips - 1) * part, chips * part)
        far_here, far_there = col_refs[-2:]

        @pl.when(core_ref[0] == 0)
        def _():
            col_scr[0, :, far] = far_here[...]
            col_scr[1, :, far] = far_there[...]

        @pl.when(core_ref[0] != 0)
        def _():
            col_scr[0, :, far] = far_there[...]
            col_scr[1, :, far] = far_here[...]

        prepare_rows(chips, group, row_refs, undo_ref, y_scr, lhs_scr, undo_scr)

    rows = here * group
    lhs = lhs_scr[:, pl.ds(pl.multiple_of(step * rows, rows), rows), :].reshape(
        chips * rows, lhs_scr.shape[2]
    )
    for d in range(2):
        for bp in range(half // 2):
            lane = (d * half + 2 * bp) * zc
            t = jnp.dot(lhs, w_ref[:, lane : lane + 2 * zc], preferred_element_type=F32)
            t = t.reshape(chips * here, group, 2 * zc)
            t = jnp.concatenate([t[:, :, :zc], t[:, :, zc:]], axis=1).astype(BF16)
            t = t.reshape(chips, here, 2 * group, zc)
            for g in range(here):
                for q in range(chips):
                    k = q * part + bp * 2 * group
                    t_scr[d, g // 2, k : k + 2 * group, (g % 2) * zc : (g % 2 + 1) * zc] = t[q, g]
    for p in range(here // 2):
        for d in range(2):
            z_scr[d, p] = jnp.dot(col_scr[d], t_scr[d, p], preferred_element_type=F32)
    for g in range(here):
        lanes = slice((g % 2) * zc, (g % 2 + 1) * zc)
        undo = [undo_scr[d, pl.ds(step * here + g, 1), :] for d in range(2)]
        forward = z_scr[0, g // 2, :, lanes] * undo[0] + b_out_ref[...]
        mirror = z_scr[1, g // 2, :, lanes] * undo[1] + b_out_ref[...]
        pair = jnp.maximum(forward, 0.0) + jnp.maximum(mirror, 0.0)
        normed = norm_rows(pair, gain_ref[...], bias_ref[...]).astype(BF16)
        hidden = jnp.dot(normed, w_up_ref[...], preferred_element_type=F32) + b_up_ref[...]
        hidden = jnp.maximum(hidden, 0.0).astype(BF16)
        update = jnp.dot(hidden, w_down_ref[...], preferred_element_type=F32)
        out_ref[g] = (pair + update + b_down_ref[...]).astype(BF16)


def pair_kernel(core, group, rows, cols, rest):
    own = cols[0]
    _, column_length, part = own.shape
    chips = (len(cols) + 1) // 2
    row_length = rows[0].shape[2]
    zc = rest[2].shape[1]
    here = 4
    depth = chips * part
    lanes = 4 * part // group

    def whole(a):
        return pl.BlockSpec(a.shape, lambda i: (0,) * a.ndim)

    return pl.pallas_call(
        functools.partial(pair_body, chips, here, group, len(rows)),
        grid=(row_length // here,),
        in_specs=[pl.BlockSpec(memory_space=pltpu.SMEM)]
        + [whole(a) for a in (*rows, *cols, *rest)],
        out_specs=pl.BlockSpec((here, column_length, zc), lambda i: (i, 0, 0)),
        out_shape=jax.ShapeDtypeStruct((row_length, column_length, zc), BF16),
        scratch_shapes=[
            pltpu.VMEM((2, column_length, depth), BF16),
            pltpu.VMEM((2, chips * row_length * group, lanes), F32),
            pltpu.VMEM((chips, row_length * group, 2 * lanes), F8),
            pltpu.VMEM((2, row_length, zc), F32),
            pltpu.VMEM((2, here // 2, depth, 2 * zc), BF16),
            pltpu.VMEM((2, here // 2, column_length, 2 * zc), F32),
        ],
        compiler_params=pltpu.CompilerParams(vmem_limit_bytes=56 << 20),
    )(core, *rows, *cols, *rest)


def chip_ring(chips):
    order = list(range(0, chips, 2)) + list(range(chips - 1, 0, -2))
    after = {order[i]: order[(i + 1) % chips] for i in range(chips)}
    before = {v: k for k, v in after.items()}
    return [
        (2 * q + core, 2 * (after if core == 0 else before)[q] + core)
        for q in range(chips)
        for core in range(2)
    ]


def shards(
    alignment,
    alignment_norm_gain,
    alignment_norm_bias,
    projection_weight,
    projection_bias_pair,
    w_out,
    b_out,
    pair_gain,
    pair_bias,
    w_up,
    b_up,
    w_down,
    b_down,
):
    local, column_length, _ = alignment.shape
    width = projection_weight.shape[1]
    half = width // 2
    row_count = lax.axis_size("row")
    col_count = lax.axis_size("col")
    row_length = column_length * col_count // row_count
    chips = row_count // 2
    row_index = lax.axis_index("row")
    col_index = lax.axis_index("col")
    core = row_index % 2

    def swap(a):
        return lax.ppermute(a, "row", [(r, r ^ 1) for r in range(row_count)])

    ring = chip_ring(chips)

    weight = jnp.concatenate([projection_weight[:, half:], projection_weight[:, :half]], axis=1)
    pbias = jnp.concatenate([projection_bias_pair[half:], projection_bias_pair[:half]])
    mine = project(
        core.reshape(1),
        alignment,
        alignment_norm_gain[None],
        alignment_norm_bias[None],
        weight,
        pbias[None],
    )
    own = mine + swap(mine)

    per_col = column_length // row_length
    start = (row_index % per_col) * row_length
    source = row_index // per_col

    def exchange(pieces):
        block = jnp.stack(
            [
                jnp.stack([lax.dynamic_slice_in_dim(c, start, row_length, 0) for c in pair])
                for pair in pieces
            ]
        )
        if col_count == 2:
            there = lax.ppermute(block, "col", [(0, 1), (1, 0)])
            return jnp.where(source == col_index, block, there)
        return lax.dynamic_index_in_dim(lax.all_gather(block, "col"), source, 0, False)

    right, left = own[0], own[1]
    cols = [own]
    early = [(right, left)]
    late = []
    steps = chips // 2 - 1
    for d in range(steps):
        right = lax.ppermute(right, "row", ring)
        left = lax.ppermute(left, "row", ring)
        pieces = [(right, left), (swap(right), swap(left))]
        for pair in pieces:
            cols.extend(pair)
        (early if d < steps - 1 else late).extend(pieces)
    far = lax.ppermute(jnp.where(core == 0, right, left), "row", ring)
    far_other = swap(far)
    cols.extend([far, far_other])
    late.append((jnp.where(core == 0, far, far_other), jnp.where(core == 0, far_other, far)))
    rows = [exchange(early), exchange(late)]

    group = 2 * local
    w8, undo = split_weight(w_out, half, group * chips)
    rest = (w8, undo, b_out[None], pair_gain[None], pair_bias[None], w_up, b_up[None], w_down)
    return pair_kernel(core.reshape(1), group, rows, cols, rest + (b_down[None],))


def solution(mesh):
    return jax.shard_map(
        shards,
        mesh=mesh,
        in_specs=(P("row", "col", None),) + (P(),) * 12,
        out_specs=P("row", "col", None),
        check_vma=False,
    )
```

time: 100 us -> 91.2 us (0.912)
  other arithmetic: 7.01 us -> 1.77 us
  Pallas kernels: 51.6 us -> 48.7 us
  starting transfers between devices: 17.7 us -> 19 us
  waiting for transfers between devices: 14.8 us -> 13.6 us
    another operation x9 -> x6, other arithmetic: 5.57 us -> 0.06 us  [the longest x5 0.05 us: exchange(): jnp.stack([jnp.stack([lax.dynamic_slice_in_dim(c, start, row_length, 0) f...]
    ppermute x3, waiting for transfers between devices: 1.66 us -> 4.95 us  [shards(): right = lax.ppermute(right, 'row', ring)]
    ppermute x1 -> x2, waiting for transfers between devices: 6.28 us -> 3.43 us  [exchange(): there = lax.ppermute(block, 'col', [(0, 1), (1, 0)])]
    pallas_call x1 -> x2, Pallas kernels: 50.4 us -> 47.6 us  [the longest x1 47.1 us: pair_kernel(): pl.pallas_call(functools.partial(pair_body, chips, here, group, len(rows)...]
    unnamed x14 -> x44, local copies, waits for them, and re-layouts: 2.84 us -> 5.67 us
    reshape x2 -> x0, local copies, waits for them, and re-layouts: 2.1 us -> none  [the longest x1 2 us: shards(): rows = rows.reshape(row_length, chips * group, width)]
    ppermute x1, waiting for transfers between devices: 3.22 us -> 1.58 us  [shards(): far = lax.ppermute(jnp.where(core == 0, right, left), 'row', ring)]
    ppermute x1 -> x2, starting transfers between devices: 1.91 us -> 3.48 us  [exchange(): there = lax.ppermute(block, 'col', [(0, 1), (1, 0)])]
  transfers between devices with their start and end apart: 16 -> 17, of which waited for: 7 -> 7; matrix products, arithmetic and copies ran while one was open for 8% -> 1% of each run, Pallas kernels for 0% -> 1%
where the time goes in v2:
time: 91.2 us; the launch traced here: 90.8 us
  Pallas kernels  48.7 us (53%)
  starting transfers between devices  19 us (21%)
  waiting for transfers between devices  13.6 us (15%)
  local copies, waits for them, and re-layouts  7.35 us (8%)
  other arithmetic  1.77 us (2%)
    pallas_call x1, Pallas kernels, pair_kernel(): pl.pallas_call(functools.partial(pair_body, chips, here, group, len(rows)...  47.1 us
    ppermute x3, starting transfers between devices, shards(): right = lax.ppermute(right, 'row', ring)  6.81 us
    unnamed x44, local copies, waits for them, and re-layouts  5.67 us
    ppermute x3, starting transfers between devices, shards(): left = lax.ppermute(left, 'row', ring)  5.64 us
    ppermute x3, waiting for transfers between devices, shards(): right = lax.ppermute(right, 'row', ring)  4.95 us
    ppermute x2, starting transfers between devices, exchange(): there = lax.ppermute(block, 'col', [(0, 1), (1, 0)])  3.48 us
    ppermute x2, waiting for transfers between devices, exchange(): there = lax.ppermute(block, 'col', [(0, 1), (1, 0)])  3.43 us
    ppermute x3, waiting for transfers between devices, shards(): left = lax.ppermute(left, 'row', ring)  2.27 us
  transfers between devices with their start and end apart: 17, of which 7 were waited for; matrix products, arithmetic and copies ran while one was open for 1% of the time, Pallas kernels for 1%

profile of v2, /device:TPU:0, one launch (start us, length us, event | category | flops | bytes accessed | tf_op | source)
XLA Modules:
  0.0 90.8 jit_solution(14093136736472054232)
XLA Ops:
  0.0 0.8 fusion.6
  0.8 0.7 fusion.5
  1.5 0.1 copy.16
  1.7 0.1 copy.17
  1.8 0.1 maximum_bitcast_fusion.8.pbias_ref
  1.9 0.1 pad_maximum_fusion.1.weight_ref
  2.0 0.0 copy-start.1
  2.0 1.1 %copy-done.1 = bf16[4,384,256]{2,1,0:T(8,128)(2,1)S(1)} copy-done((bf16[4,384,256]{2,1,0:T(8,128)(2,1)S(1)}, bf16[4,384,256]{2,1,0:T(8,128)(2,1)}, u32[]{:S(2)}) %copy-start.1) | copy-done | bytes 786456
  3.1 0.7 copy-done.3
  3.8 0.7 copy-done.4
  4.5 1.2 %shard_map.127 = bf16[2,384,256]{2,1,0:T(8,128)(2,1)S(1)} custom-call(s32[1]{0:T(128)} %bitcast.core_ref, bf16[4,384,256]{2,1,0:T(8,128)(2,1)S(1)} %copy-done.1, f32[1,256]{1,0:T(1,128)S(1)} %bitcast.68, f32[1,256]{1,0:T(1,128)S(1)} %bitcast.69, bf16[256,64]{1,0:T(8,128)(2,1)S(1)} %pad_maximum_fusion.1.weight_ref, f32[1,64]{1,0:T(1,128)S(1)} %maximum_bitcast_fusion.8.pbias_ref), custom_call_target="tpu_custom_call" | custom-call | tf_op jit(solution)/shard_map/pallas_call | solution.py:47
  5.6 0.5 collective-permute-start
  6.2 0.9 %copy-done.2 = bf16[1024,128]{1,0:T(8,128)(2,1)S(1)} copy-done((bf16[1024,128]{1,0:T(8,128)(2,1)S(1)}, bf16[1024,128]{1,0:T(8,128)(2,1)}, u32[]{:S(2)}) %copy-start.2) | copy-done | bytes 262168
  7.1 0.5 shard_map.128
  7.6 1.4 %copy-done = f8e4m3fn[256,8192]{1,0:T(32,128)(4,1)} copy-done((f8e4m3fn[256,8192]{1,0:T(32,128)(4,1)}, f8e4m3fn[256,8192]{1,0:T(32,128)(4,1)S(1)}, u32[]{:S(2)}) %copy-start) | copy-done | bytes 2097176
  9.0 0.6 copy-done.5
  9.6 0.0 collective-permute-done
  9.6 0.1 add.13.refs_2_
  9.7 0.1 slice_bitcast_fusion.1
  9.7 2.7 %collective-permute-start.1 = (bf16[384,256]{1,0:T(8,128)(2,1)S(1)}, bf16[384,256]{1,0:T(8,128)(2,1)S(1)}, u32[]{:S(2)}, u32[]{:S(2)}) collective-permute-start(bf16[384,256]{1,0:T(8,128)(2,1)S(1)} %get-tuple-element.11), channel_id=1, source_target_pairs={{0,8},{2,6},{4,0},{6,14},{8,16},{10,2},{12,4},{14,22},{16,24},{18,... | collective-permute-start | bytes 589832 | tf_op jit(solution)/shard_map/ppermute | solution.py:320
  12.4 1.6 %collective-permute-start.2 = (bf16[384,256]{1,0:T(8,128)(2,1)S(1)}, bf16[384,256]{1,0:T(8,128)(2,1)S(1)}, u32[]{:S(2)}, u32[]{:S(2)}) collective-permute-start(bf16[384,256]{1,0:T(8,128)(2,1)S(1)} %get-tuple-element.12), channel_id=1, source_target_pairs={{0,8},{2,6},{4,0},{6,14},{8,16},{10,2},{12,4},{14,22},{16,24},{18,... | collective-permute-start | bytes 589832 | tf_op jit(solution)/shard_map/ppermute | solution.py:321
  14.0 2.0 %collective-permute-done.1.refs_3_ = bf16[384,256]{1,0:T(8,128)(2,1)S(1)} collective-permute-done((bf16[384,256]{1,0:T(8,128)(2,1)S(1)}, bf16[384,256]{1,0:T(8,128)(2,1)S(1)}, u32[]{:S(2)}, u32[]{:S(2)}) %collective-permute-start.1) | collective-permute-done | bytes 196640 | tf_op jit(solution)/shard_map/ppermute | solution.py:320
  16.0 2.1 %collective-permute-start.5 = (bf16[384,256]{1,0:T(8,128)(2,1)S(1)}, bf16[384,256]{1,0:T(8,128)(2,1)S(1)}, u32[]{:S(2)}, u32[]{:S(2)}) collective-permute-start(bf16[384,256]{1,0:T(8,128)(2,1)S(1)} %collective-permute-done.1.refs_3_), channel_id=1, source_target_pairs={{0,8},{2,6},{4,0},{6,14},{8,16},{10,2},{12,4},{14,22},{16,24},{18,... | collective-permute-start | bytes 589832 | tf_op jit(solution)/shard_map/ppermute | solution.py:320
  18.1 0.0 collective-permute-start.3
  18.1 0.0 collective-permute-done.2.refs_4_
  18.1 2.1 %collective-permute-start.6 = (bf16[384,256]{1,0:T(8,128)(2,1)S(1)}, bf16[384,256]{1,0:T(8,128)(2,1)S(1)}, u32[]{:S(2)}, u32[]{:S(2)}) collective-permute-start(bf16[384,256]{1,0:T(8,128)(2,1)S(1)} %collective-permute-done.2.refs_4_), channel_id=1, source_target_pairs={{0,8},{2,6},{4,0},{6,14},{8,16},{10,2},{12,4},{14,22},{16,24},{18,... | collective-permute-start | bytes 589832 | tf_op jit(solution)/shard_map/ppermute | solution.py:321
  20.2 0.0 collective-permute-start.4
  20.2 1.5 %collective-permute-done.5.refs_7_ = bf16[384,256]{1,0:T(8,128)(2,1)S(1)} collective-permute-done((bf16[384,256]{1,0:T(8,128)(2,1)S(1)}, bf16[384,256]{1,0:T(8,128)(2,1)S(1)}, u32[]{:S(2)}, u32[]{:S(2)}) %collective-permute-start.5) | collective-permute-done | bytes 196640 | tf_op jit(solution)/shard_map/ppermute | solution.py:320
  21.7 2.1 %collective-permute-start.10 = (bf16[384,256]{1,0:T(8,128)(2,1)S(1)}, bf16[384,256]{1,0:T(8,128)(2,1)S(1)}, u32[]{:S(2)}, u32[]{:S(2)}) collective-permute-start(bf16[384,256]{1,0:T(8,128)(2,1)S(1)} %collective-permute-done.5.refs_7_), channel_id=1, source_target_pairs={{0,8},{2,6},{4,0},{6,14},{8,16},{10,2},{12,4},{14,22},{16,24},{18,... | collective-permute-start | bytes 589832 | tf_op jit(solution)/shard_map/ppermute | solution.py:320
  23.8 0.0 collective-permute-start.7
  23.8 0.0 collective-permute-done.3.refs_5_
  23.8 0.0 collective-permute-done.4.refs_6_
  23.9 0.0 collective-permute-done.6.refs_8_
  23.9 2.0 %collective-permute-start.11 = (bf16[384,256]{1,0:T(8,128)(2,1)S(1)}, bf16[384,256]{1,0:T(8,128)(2,1)S(1)}, u32[]{:S(2)}, u32[]{:S(2)}) collective-permute-start(bf16[384,256]{1,0:T(8,128)(2,1)S(1)} %collective-permute-done.6.refs_8_), channel_id=1, source_target_pairs={{0,8},{2,6},{4,0},{6,14},{8,16},{10,2},{12,4},{14,22},{16,24},{18,... | collective-permute-start | bytes 589832 | tf_op jit(solution)/shard_map/ppermute | solution.py:321
  25.9 0.0 collective-permute-start.8
  25.9 1.5 %collective-permute-done.10.refs_11_ = bf16[384,256]{1,0:T(8,128)(2,1)S(1)} collective-permute-done((bf16[384,256]{1,0:T(8,128)(2,1)S(1)}, bf16[384,256]{1,0:T(8,128)(2,1)S(1)}, u32[]{:S(2)}, u32[]{:S(2)}) %collective-permute-start.10) | collective-permute-done | bytes 196640 | tf_op jit(solution)/shard_map/ppermute | solution.py:320
  27.4 2.2 %collective-permute-done.11.refs_12_ = bf16[384,256]{1,0:T(8,128)(2,1)S(1)} collective-permute-done((bf16[384,256]{1,0:T(8,128)(2,1)S(1)}, bf16[384,256]{1,0:T(8,128)(2,1)S(1)}, u32[]{:S(2)}, u32[]{:S(2)}) %collective-permute-start.11) | collective-permute-done | bytes 196640 | tf_op jit(solution)/shard_map/ppermute | solution.py:321
  29.6 2.0 %collective-permute-start.14 = (bf16[384,256]{1,0:T(8,128)(2,1)S(1)}, bf16[384,256]{1,0:T(8,128)(2,1)S(1)}, u32[]{:S(2)}, u32[]{:S(2)}) collective-permute-start(bf16[384,256]{1,0:T(8,128)(2,1)S(1)} %broadcast_select_fusion.1), channel_id=1, source_target_pairs={{0,8},{2,6},{4,0},{6,14},{8,16},{10,2},{12,4},{14,22},{16,24},{18,... | collective-permute-start | bytes 589832 | tf_op jit(solution)/shard_map/ppermute | solution.py:326
  31.6 0.0 collective-permute-done.7.refs_9_
  31.6 0.0 collective-permute-done.8.refs_10_
  31.7 1.6 %collective-permute-start.9 = (bf16[5,2,48,256]{3,2,1,0:T(8,128)(2,1)S(1)}, bf16[5,2,48,256]{3,2,1,0:T(8,128)(2,1)S(1)}, u32[]{:S(2)}, u32[]{:S(2)}) collective-permute-start(bf16[5,2,48,256]{3,2,1,0:T(8,128)(2,1)S(1)} %fusion.4), channel_id=1, source_target_pairs={{0,1},{1,0},{2,3},{3,2},{4,5},{5,4},{6,7},{7,6},{8,9},{9,8},{10,11... | collective-permute-start | bytes 737288 | tf_op jit(solution)/shard_map/ppermute | solution.py:310
  33.2 0.0 collective-permute-start.12
  33.2 0.5 collective-permute-start.13
  33.8 1.6 %collective-permute-done.14.refs_15_ = bf16[384,256]{1,0:T(8,128)(2,1)S(1)} collective-permute-done((bf16[384,256]{1,0:T(8,128)(2,1)S(1)}, bf16[384,256]{1,0:T(8,128)(2,1)S(1)}, u32[]{:S(2)}, u32[]{:S(2)}) %collective-permute-start.14) | collective-permute-done | bytes 196640 | tf_op jit(solution)/shard_map/ppermute | solution.py:326
  35.4 0.0 collective-permute-start.15
  35.4 0.0 collective-permute-done.12.refs_13_
  35.4 0.0 collective-permute-done.13.refs_14_
  35.4 1.3 %collective-permute-done.15.refs_16_ = bf16[384,256]{1,0:T(8,128)(2,1)S(1)} collective-permute-done((bf16[384,256]{1,0:T(8,128)(2,1)S(1)}, bf16[384,256]{1,0:T(8,128)(2,1)S(1)}, u32[]{:S(2)}, u32[]{:S(2)}) %collective-permute-start.15) | collective-permute-done | bytes 196640 | tf_op jit(solution)/shard_map/ppermute | solution.py:282
  36.9 1.9 %collective-permute-start.16 = (bf16[3,2,48,256]{3,2,1,0:T(8,128)(2,1)S(1)}, bf16[3,2,48,256]{3,2,1,0:T(8,128)(2,1)S(1)}, u32[]{:S(2)}, u32[]{:S(2)}) collective-permute-start(bf16[3,2,48,256]{3,2,1,0:T(8,128)(2,1)S(1)} %pad_maximum_fusion), channel_id=1, source_target_pairs={{0,1},{1,0},{2,3},{3,2},{4,5},{5,4},{6,7},{7,6},{8,9},{9,8},{10,11... | collective-permute-start | bytes 442376 | tf_op jit(solution)/shard_map/ppermute | solution.py:310
  38.8 0.0 collective-permute-done.9
  38.8 0.7 broadcast_select_fusion.refs_0_
  39.5 3.4 %collective-permute-done.16 = bf16[3,2,48,256]{3,2,1,0:T(8,128)(2,1)S(1)} collective-permute-done((bf16[3,2,48,256]{3,2,1,0:T(8,128)(2,1)S(1)}, bf16[3,2,48,256]{3,2,1,0:T(8,128)(2,1)S(1)}, u32[]{:S(2)}, u32[]{:S(2)}) %collective-permute-start.16) | collective-permute-done | bytes 147488 | tf_op jit(solution)/shard_map/ppermute | solution.py:310
  42.9 0.7 broadcast_select_fusion.2.refs_1_
  43.6 0.0 copy-done.6
  43.6 0.0 copy-done.12
  43.6 0.0 copy-done.14
  43.6 0.0 copy-done.13
  43.6 0.0 copy-done.7
  43.7 0.0 copy-done.8
  43.7 0.0 copy-done.15
  43.7 0.0 copy-done.16
  43.7 0.0 copy-done.17
  43.7 0.0 copy-done.18
  43.7 47.1 %shard_map.129 = bf16[48,384,128]{2,1,0:T(8,128)(2,1)} custom-call(s32[1]{0:T(128)} %bitcast.core_ref, bf16[5,2,48,256]{3,2,1,0:T(8,128)(2,1)} %broadcast_select_fusion.refs_0_, bf16[3,2,48,256]{3,2,1,0:T(8,128)(2,1)} %broadcast_select_fusion.2.refs_1_, bf16[2,384,256]{2,1,0:T(8,128)(2,1)} %copy-done.6, bf16[384,256]{1,0:T(8,128)(2,1)} %copy-done.9, ...), custom_call_target="tpu_custom_call" | custom-call | tf_op jit(solution)/shard_map/pallas_call | solution.py:225
  (49 shorter events, 0.2 us)
Async XLA Ops:
  2.0 1.1 %copy-start.1 = (bf16[4,384,256]{2,1,0:T(8,128)(2,1)S(1)}, bf16[4,384,256]{2,1,0:T(8,128)(2,1)}, u32[]{:S(2)}) copy-start(bf16[4,384,256]{2,1,0:T(8,128)(2,1)} %x_ref.1) | copy-start | bytes 2359300
  3.1 0.7 copy-start.3
  3.8 0.7 copy-start.4
  5.6 3.9 %collective-permute-start = (bf16[2,384,256]{2,1,0:T(8,128)(2,1)S(1)}, bf16[2,384,256]{2,1,0:T(8,128)(2,1)S(1)}, u32[]{:S(2)}, u32[]{:S(2)}) collective-permute-start(bf16[2,384,256]{2,1,0:T(8,128)(2,1)S(1)} %shard_map.127), channel_id=1, source_target_pairs={{0,2},{2,0},{4,6},{6,4},{8,10},{10,8},{12,14},{14,12},{16,18},{18,... | collective-permute-start | bytes 1179656 | tf_op jit(solution)/shard_map/ppermute | solution.py:282
  6.2 0.9 %copy-start.2 = (bf16[1024,128]{1,0:T(8,128)(2,1)S(1)}, bf16[1024,128]{1,0:T(8,128)(2,1)}, u32[]{:S(2)}) copy-start(bf16[1024,128]{1,0:T(8,128)(2,1)} %w_ref.1) | copy-start | bytes 786436
  7.6 1.4 %copy-start = (f8e4m3fn[256,8192]{1,0:T(32,128)(4,1)}, f8e4m3fn[256,8192]{1,0:T(32,128)(4,1)S(1)}, u32[]{:S(2)}) copy-start(f8e4m3fn[256,8192]{1,0:T(32,128)(4,1)S(1)} %get-tuple-element.7.refs_17_) | copy-start | bytes 6291460
  9.0 0.6 copy-start.5
  9.7 33.9 %copy-start.6 = (bf16[2,384,256]{2,1,0:T(8,128)(2,1)}, bf16[2,384,256]{2,1,0:T(8,128)(2,1)S(1)}, u32[]{:S(2)}) copy-start(bf16[2,384,256]{2,1,0:T(8,128)(2,1)S(1)} %add.13.refs_2_) | copy-start | bytes 1179652
  9.7 6.3 %collective-permute-start.1 = (bf16[384,256]{1,0:T(8,128)(2,1)S(1)}, bf16[384,256]{1,0:T(8,128)(2,1)S(1)}, u32[]{:S(2)}, u32[]{:S(2)}) collective-permute-start(bf16[384,256]{1,0:T(8,128)(2,1)S(1)} %get-tuple-element.11), channel_id=1, source_target_pairs={{0,8},{2,6},{4,0},{6,14},{8,16},{10,2},{12,4},{14,22},{16,24},{18,... | collective-permute-start | bytes 589832 | tf_op jit(solution)/shard_map/ppermute | solution.py:320
  12.4 5.7 %collective-permute-start.2 = (bf16[384,256]{1,0:T(8,128)(2,1)S(1)}, bf16[384,256]{1,0:T(8,128)(2,1)S(1)}, u32[]{:S(2)}, u32[]{:S(2)}) collective-permute-start(bf16[384,256]{1,0:T(8,128)(2,1)S(1)} %get-tuple-element.12), channel_id=1, source_target_pairs={{0,8},{2,6},{4,0},{6,14},{8,16},{10,2},{12,4},{14,22},{16,24},{18,... | collective-permute-start | bytes 589832 | tf_op jit(solution)/shard_map/ppermute | solution.py:321
  16.0 27.6 %copy-start.9 = (bf16[384,256]{1,0:T(8,128)(2,1)}, bf16[384,256]{1,0:T(8,128)(2,1)S(1)}, u32[]{:S(2)}) copy-start(bf16[384,256]{1,0:T(8,128)(2,1)S(1)} %collective-permute-done.1.refs_3_) | copy-start | bytes 589828
  16.0 5.7 %collective-permute-start.5 = (bf16[384,256]{1,0:T(8,128)(2,1)S(1)}, bf16[384,256]{1,0:T(8,128)(2,1)S(1)}, u32[]{:S(2)}, u32[]{:S(2)}) collective-permute-start(bf16[384,256]{1,0:T(8,128)(2,1)S(1)} %collective-permute-done.1.refs_3_), channel_id=1, source_target_pairs={{0,8},{2,6},{4,0},{6,14},{8,16},{10,2},{12,4},{14,22},{16,24},{18,... | collective-permute-start | bytes 589832 | tf_op jit(solution)/shard_map/ppermute | solution.py:320
  18.1 5.7 %collective-permute-start.3 = (bf16[384,256]{1,0:T(8,128)(2,1)S(1)}, bf16[384,256]{1,0:T(8,128)(2,1)S(1)}, u32[]{:S(2)}, u32[]{:S(2)}) collective-permute-start(bf16[384,256]{1,0:T(8,128)(2,1)S(1)} %collective-permute-done.1.refs_3_), channel_id=1, source_target_pairs={{0,2},{2,0},{4,6},{6,4},{8,10},{10,8},{12,14},{14,12},{16,18},{18,... | collective-permute-start | bytes 589832 | tf_op jit(solution)/shard_map/ppermute | solution.py:282
  18.1 25.5 %copy-start.10 = (bf16[384,256]{1,0:T(8,128)(2,1)}, bf16[384,256]{1,0:T(8,128)(2,1)S(1)}, u32[]{:S(2)}) copy-start(bf16[384,256]{1,0:T(8,128)(2,1)S(1)} %collective-permute-done.2.refs_4_) | copy-start | bytes 589828
  18.1 5.7 %collective-permute-start.6 = (bf16[384,256]{1,0:T(8,128)(2,1)S(1)}, bf16[384,256]{1,0:T(8,128)(2,1)S(1)}, u32[]{:S(2)}, u32[]{:S(2)}) collective-permute-start(bf16[384,256]{1,0:T(8,128)(2,1)S(1)} %collective-permute-done.2.refs_4_), channel_id=1, source_target_pairs={{0,8},{2,6},{4,0},{6,14},{8,16},{10,2},{12,4},{14,22},{16,24},{18,... | collective-permute-start | bytes 589832 | tf_op jit(solution)/shard_map/ppermute | solution.py:321
  20.2 3.6 %collective-permute-start.4 = (bf16[384,256]{1,0:T(8,128)(2,1)S(1)}, bf16[384,256]{1,0:T(8,128)(2,1)S(1)}, u32[]{:S(2)}, u32[]{:S(2)}) collective-permute-start(bf16[384,256]{1,0:T(8,128)(2,1)S(1)} %collective-permute-done.2.refs_4_), channel_id=1, source_target_pairs={{0,2},{2,0},{4,6},{6,4},{8,10},{10,8},{12,14},{14,12},{16,18},{18,... | collective-permute-start | bytes 589832 | tf_op jit(solution)/shard_map/ppermute | solution.py:282
  21.7 21.9 %copy-start.11 = (bf16[384,256]{1,0:T(8,128)(2,1)}, bf16[384,256]{1,0:T(8,128)(2,1)S(1)}, u32[]{:S(2)}) copy-start(bf16[384,256]{1,0:T(8,128)(2,1)S(1)} %collective-permute-done.5.refs_7_) | copy-start | bytes 589828
  21.7 5.7 %collective-permute-start.10 = (bf16[384,256]{1,0:T(8,128)(2,1)S(1)}, bf16[384,256]{1,0:T(8,128)(2,1)S(1)}, u32[]{:S(2)}, u32[]{:S(2)}) collective-permute-start(bf16[384,256]{1,0:T(8,128)(2,1)S(1)} %collective-permute-done.5.refs_7_), channel_id=1, source_target_pairs={{0,8},{2,6},{4,0},{6,14},{8,16},{10,2},{12,4},{14,22},{16,24},{18,... | collective-permute-start | bytes 589832 | tf_op jit(solution)/shard_map/ppermute | solution.py:320
  23.8 7.9 %collective-permute-start.7 = (bf16[384,256]{1,0:T(8,128)(2,1)S(1)}, bf16[384,256]{1,0:T(8,128)(2,1)S(1)}, u32[]{:S(2)}, u32[]{:S(2)}) collective-permute-start(bf16[384,256]{1,0:T(8,128)(2,1)S(1)} %collective-permute-done.5.refs_7_), channel_id=1, source_target_pairs={{0,2},{2,0},{4,6},{6,4},{8,10},{10,8},{12,14},{14,12},{16,18},{18,... | collective-permute-start | bytes 589832 | tf_op jit(solution)/shard_map/ppermute | solution.py:282
  23.8 19.9 %copy-start.12 = (bf16[384,256]{1,0:T(8,128)(2,1)}, bf16[384,256]{1,0:T(8,128)(2,1)S(1)}, u32[]{:S(2)}) copy-start(bf16[384,256]{1,0:T(8,128)(2,1)S(1)} %collective-permute-done.3.refs_5_) | copy-start | bytes 589828
  23.8 19.8 %copy-start.14 = (bf16[384,256]{1,0:T(8,128)(2,1)}, bf16[384,256]{1,0:T(8,128)(2,1)S(1)}, u32[]{:S(2)}) copy-start(bf16[384,256]{1,0:T(8,128)(2,1)S(1)} %collective-permute-done.4.refs_6_) | copy-start | bytes 589828
  23.9 19.8 %copy-start.13 = (bf16[384,256]{1,0:T(8,128)(2,1)}, bf16[384,256]{1,0:T(8,128)(2,1)S(1)}, u32[]{:S(2)}) copy-start(bf16[384,256]{1,0:T(8,128)(2,1)S(1)} %collective-permute-done.6.refs_8_) | copy-start | bytes 589828
  23.9 5.7 %collective-permute-start.11 = (bf16[384,256]{1,0:T(8,128)(2,1)S(1)}, bf16[384,256]{1,0:T(8,128)(2,1)S(1)}, u32[]{:S(2)}, u32[]{:S(2)}) collective-permute-start(bf16[384,256]{1,0:T(8,128)(2,1)S(1)} %collective-permute-done.6.refs_8_), channel_id=1, source_target_pairs={{0,8},{2,6},{4,0},{6,14},{8,16},{10,2},{12,4},{14,22},{16,24},{18,... | collective-permute-start | bytes 589832 | tf_op jit(solution)/shard_map/ppermute | solution.py:321
  25.9 5.8 %collective-permute-start.8 = (bf16[384,256]{1,0:T(8,128)(2,1)S(1)}, bf16[384,256]{1,0:T(8,128)(2,1)S(1)}, u32[]{:S(2)}, u32[]{:S(2)}) collective-permute-start(bf16[384,256]{1,0:T(8,128)(2,1)S(1)} %collective-permute-done.6.refs_8_), channel_id=1, source_target_pairs={{0,2},{2,0},{4,6},{6,4},{8,10},{10,8},{12,14},{14,12},{16,18},{18,... | collective-permute-start | bytes 589832 | tf_op jit(solution)/shard_map/ppermute | solution.py:282
  27.4 16.3 %copy-start.7 = (bf16[384,256]{1,0:T(8,128)(2,1)}, bf16[384,256]{1,0:T(8,128)(2,1)S(1)}, u32[]{:S(2)}) copy-start(bf16[384,256]{1,0:T(8,128)(2,1)S(1)} %collective-permute-done.10.refs_11_) | copy-start | bytes 589828
  29.6 14.1 %copy-start.8 = (bf16[384,256]{1,0:T(8,128)(2,1)}, bf16[384,256]{1,0:T(8,128)(2,1)S(1)}, u32[]{:S(2)}) copy-start(bf16[384,256]{1,0:T(8,128)(2,1)S(1)} %collective-permute-done.11.refs_12_) | copy-start | bytes 589828
  29.6 5.7 %collective-permute-start.14 = (bf16[384,256]{1,0:T(8,128)(2,1)S(1)}, bf16[384,256]{1,0:T(8,128)(2,1)S(1)}, u32[]{:S(2)}, u32[]{:S(2)}) collective-permute-start(bf16[384,256]{1,0:T(8,128)(2,1)S(1)} %broadcast_select_fusion.1), channel_id=1, source_target_pairs={{0,8},{2,6},{4,0},{6,14},{8,16},{10,2},{12,4},{14,22},{16,24},{18,... | collective-permute-start | bytes 589832 | tf_op jit(solution)/shard_map/ppermute | solution.py:326
  31.6 12.1 %copy-start.15 = (bf16[384,256]{1,0:T(8,128)(2,1)}, bf16[384,256]{1,0:T(8,128)(2,1)S(1)}, u32[]{:S(2)}) copy-start(bf16[384,256]{1,0:T(8,128)(2,1)S(1)} %collective-permute-done.7.refs_9_) | copy-start | bytes 589828
  31.6 12.0 %copy-start.16 = (bf16[384,256]{1,0:T(8,128)(2,1)}, bf16[384,256]{1,0:T(8,128)(2,1)S(1)}, u32[]{:S(2)}) copy-start(bf16[384,256]{1,0:T(8,128)(2,1)S(1)} %collective-permute-done.8.refs_10_) | copy-start | bytes 589828
  31.7 7.1 %collective-permute-start.9 = (bf16[5,2,48,256]{3,2,1,0:T(8,128)(2,1)S(1)}, bf16[5,2,48,256]{3,2,1,0:T(8,128)(2,1)S(1)}, u32[]{:S(2)}, u32[]{:S(2)}) collective-permute-start(bf16[5,2,48,256]{3,2,1,0:T(8,128)(2,1)S(1)} %fusion.4), channel_id=1, source_target_pairs={{0,1},{1,0},{2,3},{3,2},{4,5},{5,4},{6,7},{7,6},{8,9},{9,8},{10,11... | collective-permute-start | bytes 737288 | tf_op jit(solution)/shard_map/ppermute | solution.py:310
  33.2 2.1 %collective-permute-start.12 = (bf16[384,256]{1,0:T(8,128)(2,1)S(1)}, bf16[384,256]{1,0:T(8,128)(2,1)S(1)}, u32[]{:S(2)}, u32[]{:S(2)}) collective-permute-start(bf16[384,256]{1,0:T(8,128)(2,1)S(1)} %collective-permute-done.10.refs_11_), channel_id=1, source_target_pairs={{0,2},{2,0},{4,6},{6,4},{8,10},{10,8},{12,14},{14,12},{16,18},{18,... | collective-permute-start | bytes 589832 | tf_op jit(solution)/shard_map/ppermute | solution.py:282
  33.2 2.1 %collective-permute-start.13 = (bf16[384,256]{1,0:T(8,128)(2,1)S(1)}, bf16[384,256]{1,0:T(8,128)(2,1)S(1)}, u32[]{:S(2)}, u32[]{:S(2)}) collective-permute-start(bf16[384,256]{1,0:T(8,128)(2,1)S(1)} %collective-permute-done.11.refs_12_), channel_id=1, source_target_pairs={{0,2},{2,0},{4,6},{6,4},{8,10},{10,8},{12,14},{14,12},{16,18},{18,... | collective-permute-start | bytes 589832 | tf_op jit(solution)/shard_map/ppermute | solution.py:282
  35.3 8.3 %copy-start.17 = (bf16[384,256]{1,0:T(8,128)(2,1)}, bf16[384,256]{1,0:T(8,128)(2,1)S(1)}, u32[]{:S(2)}) copy-start(bf16[384,256]{1,0:T(8,128)(2,1)S(1)} %collective-permute-done.14.refs_15_) | copy-start | bytes 589828
  35.4 1.4 %collective-permute-start.15 = (bf16[384,256]{1,0:T(8,128)(2,1)S(1)}, bf16[384,256]{1,0:T(8,128)(2,1)S(1)}, u32[]{:S(2)}, u32[]{:S(2)}) collective-permute-start(bf16[384,256]{1,0:T(8,128)(2,1)S(1)} %collective-permute-done.14.refs_15_), channel_id=1, source_target_pairs={{0,2},{2,0},{4,6},{6,4},{8,10},{10,8},{12,14},{14,12},{16,18},{18,... | collective-permute-start | bytes 589832 | tf_op jit(solution)/shard_map/ppermute | solution.py:282
  35.4 8.3 %copy-start.18 = (bf16[384,256]{1,0:T(8,128)(2,1)}, bf16[384,256]{1,0:T(8,128)(2,1)S(1)}, u32[]{:S(2)}) copy-start(bf16[384,256]{1,0:T(8,128)(2,1)S(1)} %collective-permute-done.12.refs_13_) | copy-start | bytes 589828
  35.4 8.3 %copy-start.19 = (bf16[384,256]{1,0:T(8,128)(2,1)}, bf16[384,256]{1,0:T(8,128)(2,1)S(1)}, u32[]{:S(2)}) copy-start(bf16[384,256]{1,0:T(8,128)(2,1)S(1)} %collective-permute-done.13.refs_14_) | copy-start | bytes 589828
  36.8 6.9 %copy-start.20 = (bf16[384,256]{1,0:T(8,128)(2,1)}, bf16[384,256]{1,0:T(8,128)(2,1)S(1)}, u32[]{:S(2)}) copy-start(bf16[384,256]{1,0:T(8,128)(2,1)S(1)} %collective-permute-done.15.refs_16_) | copy-start | bytes 589828
  36.9 6.1 %collective-permute-start.16 = (bf16[3,2,48,256]{3,2,1,0:T(8,128)(2,1)S(1)}, bf16[3,2,48,256]{3,2,1,0:T(8,128)(2,1)S(1)}, u32[]{:S(2)}, u32[]{:S(2)}) collective-permute-start(bf16[3,2,48,256]{3,2,1,0:T(8,128)(2,1)S(1)} %pad_maximum_fusion), channel_id=1, source_target_pairs={{0,1},{1,0},{2,3},{3,2},{4,5},{5,4},{6,7},{7,6},{8,9},{9,8},{10,11... | collective-permute-start | bytes 442376 | tf_op jit(solution)/shard_map/ppermute | solution.py:310

commit v3 on v2

--- a/solution.py
+++ b/solution.py
@@ -1,4 +1,5 @@
 import functools
+import math
 
 import jax
 import jax.numpy as jnp
@@ -26,7 +27,7 @@
     group = 2 * local
     lanes = width * group
     first = core_ref[0] * local
-    ch = lax.broadcasted_iota(jnp.int32, (width, lanes), 0)
+    ch = lax.rem(lax.broadcasted_iota(jnp.int32, (width, lanes), 0) + width // 2, width)
     lane = lax.broadcasted_iota(jnp.int32, (width, lanes), 1)
     total = None
     for s in range(local):
@@ -105,9 +106,9 @@
     )(w_out)
 
 
-def prepare_rows(chips, group, row_refs, undo_ref, y_scr, lhs_scr, undo_scr):
-    row_length = row_refs[0].shape[2]
-    part = row_refs[0].shape[3]
+def prepare_rows(chips, group, x_scr, undo_ref, y_scr, lhs_scr, undo_scr):
+    row_length = x_scr.shape[1] // chips
+    part = x_scr.shape[2]
     half = part // group
     lanes = 4 * half
     k = lax.broadcasted_iota(jnp.int32, (part, lanes), 0)
@@ -115,9 +116,7 @@
     offset = k - lax.rem(lane, half) * group
     count = chips * row_length
     for side in range(2):
-        x = jnp.concatenate(
-            [r[q, 1 - side] for r in row_refs for q in range(r.shape[0])], axis=0
-        )
+        x = x_scr[1 - side]
         for s in range(group):
             pick = jnp.where(offset == s, 1.0, 0.0).astype(BF16)
             y_scr[side, pl.ds(s, count, stride=group), :] = jnp.dot(
@@ -143,14 +142,14 @@
             lhs_scr[q, :, side * lanes : (side + 1) * lanes] = both
 
 
-def pair_body(chips, here, group, row_parts, core_ref, *refs):
-    row_refs = refs[:row_parts]
-    refs = refs[row_parts:]
+def pair_body(chips, here, group, row_parts, place_ref, *refs):
+    here_refs, there_refs = refs[:row_parts], refs[row_parts : 2 * row_parts]
+    refs = refs[2 * row_parts :]
     own_ref, *col_refs = refs[: chips * 2 - 1]
     (w_ref, undo_ref, b_out_ref, gain_ref, bias_ref, w_up_ref, b_up_ref, w_down_ref, b_down_ref) = (
         refs[chips * 2 - 1 : chips * 2 + 8]
     )
-    out_ref, col_scr, y_scr, lhs_scr, undo_scr, t_scr, z_scr = refs[chips * 2 + 8 :]
+    out_ref, col_scr, x_scr, y_scr, lhs_scr, undo_scr, t_scr, z_scr = refs[chips * 2 + 8 :]
     part = own_ref.shape[2]
     zc = out_ref.shape[2]
     half = part // group
@@ -166,17 +165,31 @@
         far = slice((chips - 1) * part, chips * part)
         far_here, far_there = col_refs[-2:]
 
-        @pl.when(core_ref[0] == 0)
+        @pl.when(place_ref[0] == 0)
         def _():
             col_scr[0, :, far] = far_here[...]
             col_scr[1, :, far] = far_there[...]
 
-        @pl.when(core_ref[0] != 0)
+        @pl.when(place_ref[0] != 0)
         def _():
             col_scr[0, :, far] = far_there[...]
             col_scr[1, :, far] = far_here[...]
 
-        prepare_rows(chips, group, row_refs, undo_ref, y_scr, lhs_scr, undo_scr)
+        def take(row_refs):
+            blocks = [(r, q) for r in row_refs for q in range(r.shape[0])]
+            for i, (r, q) in enumerate(blocks):
+                for side in range(2):
+                    x_scr[side, i * r.shape[2] : (i + 1) * r.shape[2], :] = r[q, side]
+
+        @pl.when(place_ref[1] != 0)
+        def _():
+            take(here_refs)
+
+        @pl.when(place_ref[1] == 0)
+        def _():
+            take(there_refs)
+
+        prepare_rows(chips, group, x_scr, undo_ref, y_scr, lhs_scr, undo_scr)
 
     rows = here * group
     lhs = lhs_scr[:, pl.ds(pl.multiple_of(step * rows, rows), rows), :].reshape(
@@ -209,13 +222,13 @@
         out_ref[g] = (pair + update + b_down_ref[...]).astype(BF16)
 
 
-def pair_kernel(core, group, rows, cols, rest):
+def pair_kernel(place, group, rows_here, rows_there, cols, rest):
     own = cols[0]
     _, column_length, part = own.shape
     chips = (len(cols) + 1) // 2
-    row_length = rows[0].shape[2]
+    row_length = rows_here[0].shape[2]
     zc = rest[2].shape[1]
-    here = 4
+    here = math.gcd(row_length, 8)
     depth = chips * part
     lanes = 4 * part // group
 
@@ -223,14 +236,15 @@
         return pl.BlockSpec(a.shape, lambda i: (0,) * a.ndim)
 
     return pl.pallas_call(
-        functools.partial(pair_body, chips, here, group, len(rows)),
+        functools.partial(pair_body, chips, here, group, len(rows_here)),
         grid=(row_length // here,),
         in_specs=[pl.BlockSpec(memory_space=pltpu.SMEM)]
-        + [whole(a) for a in (*rows, *cols, *rest)],
+        + [whole(a) for a in (*rows_here, *rows_there, *cols, *rest)],
         out_specs=pl.BlockSpec((here, column_length, zc), lambda i: (i, 0, 0)),
         out_shape=jax.ShapeDtypeStruct((row_length, column_length, zc), BF16),
         scratch_shapes=[
             pltpu.VMEM((2, column_length, depth), BF16),
+            pltpu.VMEM((2, chips * row_length, part), BF16),
             pltpu.VMEM((2, chips * row_length * group, lanes), F32),
             pltpu.VMEM((chips, row_length * group, 2 * lanes), F8),
             pltpu.VMEM((2, row_length, zc), F32),
@@ -238,7 +252,7 @@
             pltpu.VMEM((2, here // 2, column_length, 2 * zc), F32),
         ],
         compiler_params=pltpu.CompilerParams(vmem_limit_bytes=56 << 20),
-    )(core, *rows, *cols, *rest)
+    )(place, *rows_here, *rows_there, *cols, *rest)
 
 
 def chip_ring(chips):
@@ -283,15 +297,13 @@
 
     ring = chip_ring(chips)
 
-    weight = jnp.concatenate([projection_weight[:, half:], projection_weight[:, :half]], axis=1)
-    pbias = jnp.concatenate([projection_bias_pair[half:], projection_bias_pair[:half]])
     mine = project(
         core.reshape(1),
         alignment,
         alignment_norm_gain[None],
         alignment_norm_bias[None],
-        weight,
-        pbias[None],
+        projection_weight,
+        projection_bias_pair[None],
     )
     own = mine + swap(mine)
 
@@ -299,22 +311,33 @@
     start = (row_index % per_col) * row_length
     source = row_index // per_col
 
-    def exchange(pieces):
-        block = jnp.stack(
+    def cut(pieces, first):
+        return jnp.stack(
             [
-                jnp.stack([lax.dynamic_slice_in_dim(c, start, row_length, 0) for c in pair])
+                jnp.stack([lax.dynamic_slice_in_dim(c, first, row_length, 0) for c in pair])
                 for pair in pieces
             ]
         )
+
+    def exchange(pieces):
+        block = cut(pieces, start)
         if col_count == 2:
-            there = lax.ppermute(block, "col", [(0, 1), (1, 0)])
-            return jnp.where(source == col_index, block, there)
-        return lax.dynamic_index_in_dim(lax.all_gather(block, "col"), source, 0, False)
+            return block, lax.ppermute(block, "col", [(0, 1), (1, 0)])
+        block = lax.dynamic_index_in_dim(lax.all_gather(block, "col"), source, 0, False)
+        return block, block
 
     right, left = own[0], own[1]
     cols = [own]
     early = [(right, left)]
-    late = []
+    if col_count == 2:
+        opposite = [row_count - 2 - r + 2 * (r % 2) for r in range(row_count)]
+        target = row_count - 2 - row_index + 2 * core
+        far_there = lax.ppermute(
+            cut(early, (target % per_col) * row_length),
+            ("row", "col"),
+            [(2 * r + t // per_col, 2 * t + 1 - t // per_col) for r, t in enumerate(opposite)],
+        )
+    rows = []
     steps = chips // 2 - 1
     for d in range(steps):
         right = lax.ppermute(right, "row", ring)
@@ -322,17 +345,34 @@
         pieces = [(right, left), (swap(right), swap(left))]
         for pair in pieces:
             cols.extend(pair)
-        (early if d < steps - 1 else late).extend(pieces)
+        early.extend(pieces)
+        if d >= steps - 2:
+            rows.append(exchange(early))
+            early = []
+        if d == 0:
+            params = (w_out, b_out, pair_gain, pair_bias, w_up, b_up, w_down, b_down)
+            *params, right, left = lax.optimization_barrier((*params, right, left))
     far = lax.ppermute(jnp.where(core == 0, right, left), "row", ring)
     far_other = swap(far)
     cols.extend([far, far_other])
-    late.append((jnp.where(core == 0, far, far_other), jnp.where(core == 0, far_other, far)))
-    rows = [exchange(early), exchange(late)]
+    a = lax.dynamic_slice_in_dim(far, start, row_length, 0)
+    b = lax.dynamic_slice_in_dim(far_other, start, row_length, 0)
+    far_pair = (jnp.where(core == 0, a, b), jnp.where(core == 0, b, a))
+    if col_count == 2:
+        rows.append((jnp.stack(far_pair)[None], far_there))
+    else:
+        block = lax.all_gather(jnp.stack(far_pair)[None], "col")
+        block = lax.dynamic_index_in_dim(block, source, 0, False)
+        rows.append((block, block))
 
     group = 2 * local
+    w_out, b_out, pair_gain, pair_bias, w_up, b_up, w_down, b_down = params
     w8, undo = split_weight(w_out, half, group * chips)
     rest = (w8, undo, b_out[None], pair_gain[None], pair_bias[None], w_up, b_up[None], w_down)
-    return pair_kernel(core.reshape(1), group, rows, cols, rest + (b_down[None],))
+    place = jnp.stack([core, (source == col_index).astype(core.dtype)])
+    return pair_kernel(
+        place, group, [r[0] for r in rows], [r[1] for r in rows], cols, rest + (b_down[None],)
+    )
 
 
 def solution(mesh):

time: 91.2 us -> 89.8 us (0.985)
  Pallas kernels: 48.7 us -> 46.9 us
    ppermute x3, waiting for transfers between devices: 2.27 us -> 4.21 us  [shards(): left = lax.ppermute(left, 'row', ring)]
    pallas_call x1, Pallas kernels: 47.1 us -> 45.2 us  [pair_kernel(): pl.pallas_call(functools.partial(pair_body, chips, here, group, len(rows_...]
    unnamed x44 -> x55, local copies, waits for them, and re-layouts: 5.67 us -> 7.41 us
    slice x2 -> x0, local copies, waits for them, and re-layouts: 1.54 us -> none  [the longest x1 0.8 us: shards(): projection_bias_pair[half:]]
    select_n x2 -> x0, other arithmetic: 1.4 us -> none  [exchange(): return jnp.where(source == col_index, block, there)]
    ppermute x2 -> x3, starting transfers between devices: 3.48 us -> 4.82 us  [the longest x2 4.16 us: exchange(): return (block, lax.ppermute(block, 'col', [(0, 1), (1, 0)]))]
    ppermute x3, waiting for transfers between devices: 4.95 us -> 3.63 us  [shards(): right = lax.ppermute(right, 'row', ring)]
    ppermute x3, starting transfers between devices: 5.64 us -> 4.73 us  [shards(): left = lax.ppermute(left, 'row', ring)]
  transfers between devices with their start and end apart: 17 -> 18, of which waited for: 7 -> 7; matrix products, arithmetic and copies ran while one was open for 1% -> 2% of each run, Pallas kernels for 1% -> 1%
where the time goes in v3:
time: 89.8 us; the launch traced here: 89.5 us
  Pallas kernels  46.9 us (52%)
  starting transfers between devices  19.7 us (22%)
  waiting for transfers between devices  13.3 us (15%)
  local copies, waits for them, and re-layouts  7.55 us (8%)
  other arithmetic  1.48 us (2%)
    pallas_call x1, Pallas kernels, pair_kernel(): pl.pallas_call(functools.partial(pair_body, chips, here, group, len(rows_...  45.2 us
    unnamed x55, local copies, waits for them, and re-layouts  7.41 us
    ppermute x3, starting transfers between devices, shards(): right = lax.ppermute(right, 'row', ring)  6.7 us
    ppermute x3, starting transfers between devices, shards(): left = lax.ppermute(left, 'row', ring)  4.73 us
    ppermute x3, waiting for transfers between devices, shards(): left = lax.ppermute(left, 'row', ring)  4.21 us
    ppermute x2, starting transfers between devices, exchange(): return (block, lax.ppermute(block, 'col', [(0, 1), (1, 0)]))  4.16 us
    ppermute x3, waiting for transfers between devices, shards(): right = lax.ppermute(right, 'row', ring)  3.63 us
    ppermute x2, waiting for transfers between devices, exchange(): return (block, lax.ppermute(block, 'col', [(0, 1), (1, 0)]))  2.71 us
  transfers between devices with their start and end apart: 18, of which 7 were waited for; matrix products, arithmetic and copies ran while one was open for 2% of the time, Pallas kernels for 1%

profile of v3, /device:TPU:0, one launch (start us, length us, event | category | flops | bytes accessed | tf_op | source)
XLA Modules:
  0.0 89.5 jit_solution(17649820464405950960)
XLA Ops:
  0.0 0.9 copy.14.weight_ref
  0.9 0.0 copy-start.1
  0.9 1.1 %copy-done.1 = bf16[4,384,256]{2,1,0:T(8,128)(2,1)S(1)} copy-done((bf16[4,384,256]{2,1,0:T(8,128)(2,1)S(1)}, bf16[4,384,256]{2,1,0:T(8,128)(2,1)}, u32[]{:S(2)}) %copy-start.1) | copy-done | bytes 786456
  2.0 0.7 copy-done.3
  2.7 0.7 copy-done.4
  3.4 0.7 copy-done.5
  4.0 1.2 %shard_map.127 = bf16[2,384,256]{2,1,0:T(8,128)(2,1)S(1)} custom-call(s32[1]{0:T(128)} %bitcast.core_ref, bf16[4,384,256]{2,1,0:T(8,128)(2,1)S(1)} %copy-done.1, f32[1,256]{1,0:T(1,128)S(1)} %bitcast.70, f32[1,256]{1,0:T(1,128)S(1)} %bitcast.71, bf16[256,64]{1,0:T(8,128)(2,1)S(1)} %copy.14.weight_ref, f32[1,64]{1,0:T(1,128)S(1)} %bitcast.72), custom_call_target="tpu_custom_call" | custom-call | tf_op jit(solution)/shard_map/pallas_call | solution.py:48
  5.2 0.5 collective-permute-start
  5.7 0.6 pad_add_fusion.place_ref
  6.3 0.8 collective-permute-done
  7.1 0.1 add.20.refs_6_
  7.2 0.1 slice_bitcast_fusion.1
  7.3 3.0 %collective-permute-start.1 = (bf16[384,256]{1,0:T(8,128)(2,1)S(1)}, bf16[384,256]{1,0:T(8,128)(2,1)S(1)}, u32[]{:S(2)}, u32[]{:S(2)}) collective-permute-start(bf16[384,256]{1,0:T(8,128)(2,1)S(1)} %get-tuple-element.31), channel_id=1, source_target_pairs={{0,8},{2,6},{4,0},{6,14},{8,16},{10,2},{12,4},{14,22},{16,24},{18,... | collective-permute-start | bytes 589832 | tf_op jit(solution)/shard_map/ppermute | solution.py:343
  10.3 1.6 %collective-permute-start.2 = (bf16[384,256]{1,0:T(8,128)(2,1)S(1)}, bf16[384,256]{1,0:T(8,128)(2,1)S(1)}, u32[]{:S(2)}, u32[]{:S(2)}) collective-permute-start(bf16[384,256]{1,0:T(8,128)(2,1)S(1)} %get-tuple-element.32), channel_id=1, source_target_pairs={{0,8},{2,6},{4,0},{6,14},{8,16},{10,2},{12,4},{14,22},{16,24},{18,... | collective-permute-start | bytes 589832 | tf_op jit(solution)/shard_map/ppermute | solution.py:344
  11.9 0.7 collective-permute-start.17
  12.5 1.3 %collective-permute-done.1.refs_7_ = bf16[384,256]{1,0:T(8,128)(2,1)S(1)} collective-permute-done((bf16[384,256]{1,0:T(8,128)(2,1)S(1)}, bf16[384,256]{1,0:T(8,128)(2,1)S(1)}, u32[]{:S(2)}, u32[]{:S(2)}) %collective-permute-start.1) | collective-permute-done | bytes 196640 | tf_op jit(solution)/shard_map/ppermute | solution.py:343
  13.8 2.1 %collective-permute-done.2.refs_8_ = bf16[384,256]{1,0:T(8,128)(2,1)S(1)} collective-permute-done((bf16[384,256]{1,0:T(8,128)(2,1)S(1)}, bf16[384,256]{1,0:T(8,128)(2,1)S(1)}, u32[]{:S(2)}, u32[]{:S(2)}) %collective-permute-start.2) | collective-permute-done | bytes 196640 | tf_op jit(solution)/shard_map/ppermute | solution.py:344
  16.0 2.1 %collective-permute-start.5 = (bf16[384,256]{1,0:T(8,128)(2,1)S(1)}, bf16[384,256]{1,0:T(8,128)(2,1)S(1)}, u32[]{:S(2)}, u32[]{:S(2)}) collective-permute-start(bf16[384,256]{1,0:T(8,128)(2,1)S(1)} %collective-permute-done.1.refs_7_), channel_id=1, source_target_pairs={{0,8},{2,6},{4,0},{6,14},{8,16},{10,2},{12,4},{14,22},{16,24},{18,... | collective-permute-start | bytes 589832 | tf_op jit(solution)/shard_map/ppermute | solution.py:343
  18.0 1.6 %collective-permute-start.6 = (bf16[384,256]{1,0:T(8,128)(2,1)S(1)}, bf16[384,256]{1,0:T(8,128)(2,1)S(1)}, u32[]{:S(2)}, u32[]{:S(2)}) collective-permute-start(bf16[384,256]{1,0:T(8,128)(2,1)S(1)} %collective-permute-done.2.refs_8_), channel_id=1, source_target_pairs={{0,8},{2,6},{4,0},{6,14},{8,16},{10,2},{12,4},{14,22},{16,24},{18,... | collective-permute-start | bytes 589832 | tf_op jit(solution)/shard_map/ppermute | solution.py:344
  19.6 0.9 %copy-done.2 = bf16[1024,128]{1,0:T(8,128)(2,1)S(1)} copy-done((bf16[1024,128]{1,0:T(8,128)(2,1)S(1)}, bf16[1024,128]{1,0:T(8,128)(2,1)}, u32[]{:S(2)}) %copy-start.2) | copy-done | bytes 262168
  20.6 0.5 shard_map.128
  21.1 1.3 %copy-done = f8e4m3fn[256,8192]{1,0:T(32,128)(4,1)} copy-done((f8e4m3fn[256,8192]{1,0:T(32,128)(4,1)}, f8e4m3fn[256,8192]{1,0:T(32,128)(4,1)S(1)}, u32[]{:S(2)}) %copy-start) | copy-done | bytes 2097176
  22.4 0.6 copy-done.6
  23.0 0.0 collective-permute-start.3
  23.0 0.5 collective-permute-start.4
  23.5 0.0 collective-permute-done.5.refs_11_
  23.5 1.6 %collective-permute-start.9 = (bf16[384,256]{1,0:T(8,128)(2,1)S(1)}, bf16[384,256]{1,0:T(8,128)(2,1)S(1)}, u32[]{:S(2)}, u32[]{:S(2)}) collective-permute-start(bf16[384,256]{1,0:T(8,128)(2,1)S(1)} %collective-permute-done.5.refs_11_), channel_id=1, source_target_pairs={{0,8},{2,6},{4,0},{6,14},{8,16},{10,2},{12,4},{14,22},{16,24},{18,... | collective-permute-start | bytes 589832 | tf_op jit(solution)/shard_map/ppermute | solution.py:343
  25.2 0.0 collective-permute-done.3.refs_9_
  25.2 0.1 collective-permute-start.7
  25.3 0.0 collective-permute-done.4.refs_10_
  25.3 0.0 copy-start.17
  25.3 0.0 collective-permute-done.6.refs_12_
  25.3 1.6 %collective-permute-start.10 = (bf16[384,256]{1,0:T(8,128)(2,1)S(1)}, bf16[384,256]{1,0:T(8,128)(2,1)S(1)}, u32[]{:S(2)}, u32[]{:S(2)}) collective-permute-start(bf16[384,256]{1,0:T(8,128)(2,1)S(1)} %collective-permute-done.6.refs_12_), channel_id=1, source_target_pairs={{0,8},{2,6},{4,0},{6,14},{8,16},{10,2},{12,4},{14,22},{16,24},{18,... | collective-permute-start | bytes 589832 | tf_op jit(solution)/shard_map/ppermute | solution.py:344
  26.9 0.0 collective-permute-start.8
  26.9 2.3 %collective-permute-done.9.refs_15_ = bf16[384,256]{1,0:T(8,128)(2,1)S(1)} collective-permute-done((bf16[384,256]{1,0:T(8,128)(2,1)S(1)}, bf16[384,256]{1,0:T(8,128)(2,1)S(1)}, u32[]{:S(2)}, u32[]{:S(2)}) %collective-permute-start.9) | collective-permute-done | bytes 196640 | tf_op jit(solution)/shard_map/ppermute | solution.py:343
  29.3 2.1 %collective-permute-done.10.refs_16_ = bf16[384,256]{1,0:T(8,128)(2,1)S(1)} collective-permute-done((bf16[384,256]{1,0:T(8,128)(2,1)S(1)}, bf16[384,256]{1,0:T(8,128)(2,1)S(1)}, u32[]{:S(2)}, u32[]{:S(2)}) %collective-permute-start.10) | collective-permute-done | bytes 196640 | tf_op jit(solution)/shard_map/ppermute | solution.py:344
  31.4 1.8 %collective-permute-start.13 = (bf16[384,256]{1,0:T(8,128)(2,1)S(1)}, bf16[384,256]{1,0:T(8,128)(2,1)S(1)}, u32[]{:S(2)}, u32[]{:S(2)}) collective-permute-start(bf16[384,256]{1,0:T(8,128)(2,1)S(1)} %broadcast_select_fusion), channel_id=1, source_target_pairs={{0,8},{2,6},{4,0},{6,14},{8,16},{10,2},{12,4},{14,22},{16,24},{18,... | collective-permute-start | bytes 589832 | tf_op jit(solution)/shard_map/ppermute | solution.py:355
  33.2 0.0 collective-permute-done.7.refs_13_
  33.2 0.0 collective-permute-done.8.refs_14_
  33.3 0.0 copy-start.11
  33.3 1.6 %collective-permute-start.15 = (bf16[5,2,48,256]{3,2,1,0:T(8,128)(2,1)S(1)}, bf16[5,2,48,256]{3,2,1,0:T(8,128)(2,1)S(1)}, u32[]{:S(2)}, u32[]{:S(2)}) collective-permute-start(bf16[5,2,48,256]{3,2,1,0:T(8,128)(2,1)S(1)} %fusion.4.refs_0_), channel_id=1, source_target_pairs={{0,1},{1,0},{2,3},{3,2},{4,5},{5,4},{6,7},{7,6},{8,9},{9,8},{10,11... | collective-permute-start | bytes 737288 | tf_op jit(solution)/shard_map/ppermute | solution.py:325
  34.8 0.0 collective-permute-start.11
  34.8 0.5 collective-permute-start.12
  35.4 1.9 %collective-permute-done.13.refs_19_ = bf16[384,256]{1,0:T(8,128)(2,1)S(1)} collective-permute-done((bf16[384,256]{1,0:T(8,128)(2,1)S(1)}, bf16[384,256]{1,0:T(8,128)(2,1)S(1)}, u32[]{:S(2)}, u32[]{:S(2)}) %collective-permute-start.13) | collective-permute-done | bytes 196640 | tf_op jit(solution)/shard_map/ppermute | solution.py:355
  37.3 0.0 collective-permute-start.14
  37.3 0.0 collective-permute-done.11.refs_17_
  37.3 0.0 collective-permute-done.12.refs_18_
  37.4 0.0 copy-start.10
  37.4 2.6 %collective-permute-start.16 = (bf16[2,2,48,256]{3,2,1,0:T(8,128)(2,1)S(1)}, bf16[2,2,48,256]{3,2,1,0:T(8,128)(2,1)S(1)}, u32[]{:S(2)}, u32[]{:S(2)}) collective-permute-start(bf16[2,2,48,256]{3,2,1,0:T(8,128)(2,1)S(1)} %pad_maximum_fusion.refs_1_), channel_id=1, source_target_pairs={{0,1},{1,0},{2,3},{3,2},{4,5},{5,4},{6,7},{7,6},{8,9},{9,8},{10,11... | collective-permute-start | bytes 294920 | tf_op jit(solution)/shard_map/ppermute | solution.py:325
  40.0 0.0 collective-permute-done.14.refs_20_
  40.1 0.7 maximum_bitcast_fusion.7.refs_2_
  40.7 0.0 collective-permute-done.17.refs_5_
  40.8 0.0 collective-permute-done.15.refs_3_
  40.8 0.0 copy-start.24
  40.8 2.7 %collective-permute-done.16.refs_4_ = bf16[2,2,48,256]{3,2,1,0:T(8,128)(2,1)S(1)} collective-permute-done((bf16[2,2,48,256]{3,2,1,0:T(8,128)(2,1)S(1)}, bf16[2,2,48,256]{3,2,1,0:T(8,128)(2,1)S(1)}, u32[]{:S(2)}, u32[]{:S(2)}) %collective-permute-start.16) | collective-permute-done | bytes 98336 | tf_op jit(solution)/shard_map/ppermute | solution.py:325
  43.5 0.0 copy-done.12
  43.5 0.0 copy-done.14
  43.5 0.0 copy-done.16
  43.5 0.0 copy-done.17
  43.5 0.0 copy-done.15
  43.5 0.0 copy-done.8
  43.5 0.0 copy-done.9
  43.6 0.5 copy-done.25
  44.1 45.2 %shard_map.129 = bf16[48,384,128]{2,1,0:T(8,128)(2,1)} custom-call(s32[2]{0:T(128)} %pad_add_fusion.place_ref, bf16[5,2,48,256]{3,2,1,0:T(8,128)(2,1)} %copy-done.11, bf16[2,2,48,256]{3,2,1,0:T(8,128)(2,1)} %copy-done.10, bf16[1,2,48,256]{3,2,1,0:T(8,128)(2,1)} %maximum_bitcast_fusion.7.refs_2_, bf16[5,2,48,256]{3,2,1,0:T(8,128)(2,1)} %copy-done.24, ...), custom_call_target="tpu_custom_call" | custom-call | tf_op jit(solution)/shard_map/pallas_call | solution.py:238
  (58 shorter events, 0.3 us)
Async XLA Ops:
  0.9 1.1 %copy-start.1 = (bf16[4,384,256]{2,1,0:T(8,128)(2,1)S(1)}, bf16[4,384,256]{2,1,0:T(8,128)(2,1)}, u32[]{:S(2)}) copy-start(bf16[4,384,256]{2,1,0:T(8,128)(2,1)} %x_ref.1) | copy-start | bytes 2359300
  2.0 0.7 copy-start.3
  2.7 0.7 copy-start.4
  3.4 0.7 copy-start.5
  5.2 1.9 %collective-permute-start = (bf16[2,384,256]{2,1,0:T(8,128)(2,1)S(1)}, bf16[2,384,256]{2,1,0:T(8,128)(2,1)S(1)}, u32[]{:S(2)}, u32[]{:S(2)}) collective-permute-start(bf16[2,384,256]{2,1,0:T(8,128)(2,1)S(1)} %shard_map.127), channel_id=1, source_target_pairs={{0,2},{2,0},{4,6},{6,4},{8,10},{10,8},{12,14},{14,12},{16,18},{18,... | collective-permute-start | bytes 1179656 | tf_op jit(solution)/shard_map/ppermute | solution.py:296
  7.2 36.3 %copy-start.7 = (bf16[2,384,256]{2,1,0:T(8,128)(2,1)}, bf16[2,384,256]{2,1,0:T(8,128)(2,1)S(1)}, u32[]{:S(2)}) copy-start(bf16[2,384,256]{2,1,0:T(8,128)(2,1)S(1)} %add.20.refs_6_) | copy-start | bytes 1179652
  7.3 6.6 %collective-permute-start.1 = (bf16[384,256]{1,0:T(8,128)(2,1)S(1)}, bf16[384,256]{1,0:T(8,128)(2,1)S(1)}, u32[]{:S(2)}, u32[]{:S(2)}) collective-permute-start(bf16[384,256]{1,0:T(8,128)(2,1)S(1)} %get-tuple-element.31), channel_id=1, source_target_pairs={{0,8},{2,6},{4,0},{6,14},{8,16},{10,2},{12,4},{14,22},{16,24},{18,... | collective-permute-start | bytes 589832 | tf_op jit(solution)/shard_map/ppermute | solution.py:343
  10.3 5.7 %collective-permute-start.2 = (bf16[384,256]{1,0:T(8,128)(2,1)S(1)}, bf16[384,256]{1,0:T(8,128)(2,1)S(1)}, u32[]{:S(2)}, u32[]{:S(2)}) collective-permute-start(bf16[384,256]{1,0:T(8,128)(2,1)S(1)} %get-tuple-element.32), channel_id=1, source_target_pairs={{0,8},{2,6},{4,0},{6,14},{8,16},{10,2},{12,4},{14,22},{16,24},{18,... | collective-permute-start | bytes 589832 | tf_op jit(solution)/shard_map/ppermute | solution.py:344
  11.9 28.9 %collective-permute-start.17 = (bf16[1,2,48,256]{3,2,1,0:T(8,128)(2,1)S(1)}, bf16[1,2,48,256]{3,2,1,0:T(8,128)(2,1)S(1)}, u32[]{:S(2)}, u32[]{:S(2)}) collective-permute-start(bf16[1,2,48,256]{3,2,1,0:T(8,128)(2,1)S(1)} %maximum_bitcast_fusion.8), channel_id=1, source_target_pairs={{1,28},{3,30},{5,24},{7,26},{9,20},{11,22},{13,16},{15,18},{16,13}... | collective-permute-start | bytes 147464 | tf_op jit(solution)/shard_map/ppermute | solution.py:335
  13.8 29.6 %copy-start.12 = (bf16[384,256]{1,0:T(8,128)(2,1)}, bf16[384,256]{1,0:T(8,128)(2,1)S(1)}, u32[]{:S(2)}) copy-start(bf16[384,256]{1,0:T(8,128)(2,1)S(1)} %collective-permute-done.1.refs_7_) | copy-start | bytes 589828
  16.0 27.5 %copy-start.13 = (bf16[384,256]{1,0:T(8,128)(2,1)}, bf16[384,256]{1,0:T(8,128)(2,1)S(1)}, u32[]{:S(2)}) copy-start(bf16[384,256]{1,0:T(8,128)(2,1)S(1)} %collective-permute-done.2.refs_8_) | copy-start | bytes 589828
  16.0 7.6 %collective-permute-start.5 = (bf16[384,256]{1,0:T(8,128)(2,1)S(1)}, bf16[384,256]{1,0:T(8,128)(2,1)S(1)}, u32[]{:S(2)}, u32[]{:S(2)}) collective-permute-start(bf16[384,256]{1,0:T(8,128)(2,1)S(1)} %collective-permute-done.1.refs_7_), channel_id=1, source_target_pairs={{0,8},{2,6},{4,0},{6,14},{8,16},{10,2},{12,4},{14,22},{16,24},{18,... | collective-permute-start | bytes 589832 | tf_op jit(solution)/shard_map/ppermute | solution.py:343
  18.0 7.3 %collective-permute-start.6 = (bf16[384,256]{1,0:T(8,128)(2,1)S(1)}, bf16[384,256]{1,0:T(8,128)(2,1)S(1)}, u32[]{:S(2)}, u32[]{:S(2)}) collective-permute-start(bf16[384,256]{1,0:T(8,128)(2,1)S(1)} %collective-permute-done.2.refs_8_), channel_id=1, source_target_pairs={{0,8},{2,6},{4,0},{6,14},{8,16},{10,2},{12,4},{14,22},{16,24},{18,... | collective-permute-start | bytes 589832 | tf_op jit(solution)/shard_map/ppermute | solution.py:344
  19.6 0.9 %copy-start.2 = (bf16[1024,128]{1,0:T(8,128)(2,1)S(1)}, bf16[1024,128]{1,0:T(8,128)(2,1)}, u32[]{:S(2)}) copy-start(bf16[1024,128]{1,0:T(8,128)(2,1)} %w_ref) | copy-start | bytes 786436
  21.1 1.3 %copy-start = (f8e4m3fn[256,8192]{1,0:T(32,128)(4,1)}, f8e4m3fn[256,8192]{1,0:T(32,128)(4,1)S(1)}, u32[]{:S(2)}) copy-start(f8e4m3fn[256,8192]{1,0:T(32,128)(4,1)S(1)} %get-tuple-element.20.refs_21_) | copy-start | bytes 6291460
  22.4 0.6 copy-start.6
  23.0 2.2 %collective-permute-start.3 = (bf16[384,256]{1,0:T(8,128)(2,1)S(1)}, bf16[384,256]{1,0:T(8,128)(2,1)S(1)}, u32[]{:S(2)}, u32[]{:S(2)}) collective-permute-start(bf16[384,256]{1,0:T(8,128)(2,1)S(1)} %collective-permute-done.1.refs_7_), channel_id=1, source_target_pairs={{0,2},{2,0},{4,6},{6,4},{8,10},{10,8},{12,14},{14,12},{16,18},{18,... | collective-permute-start | bytes 589832 | tf_op jit(solution)/shard_map/ppermute | solution.py:296
  23.0 2.3 %collective-permute-start.4 = (bf16[384,256]{1,0:T(8,128)(2,1)S(1)}, bf16[384,256]{1,0:T(8,128)(2,1)S(1)}, u32[]{:S(2)}, u32[]{:S(2)}) collective-permute-start(bf16[384,256]{1,0:T(8,128)(2,1)S(1)} %collective-permute-done.2.refs_8_), channel_id=1, source_target_pairs={{0,2},{2,0},{4,6},{6,4},{8,10},{10,8},{12,14},{14,12},{16,18},{18,... | collective-permute-start | bytes 589832 | tf_op jit(solution)/shard_map/ppermute | solution.py:296
  23.5 20.0 %copy-start.14 = (bf16[384,256]{1,0:T(8,128)(2,1)}, bf16[384,256]{1,0:T(8,128)(2,1)S(1)}, u32[]{:S(2)}) copy-start(bf16[384,256]{1,0:T(8,128)(2,1)S(1)} %collective-permute-done.5.refs_11_) | copy-start | bytes 589828
  23.5 5.7 %collective-permute-start.9 = (bf16[384,256]{1,0:T(8,128)(2,1)S(1)}, bf16[384,256]{1,0:T(8,128)(2,1)S(1)}, u32[]{:S(2)}, u32[]{:S(2)}) collective-permute-start(bf16[384,256]{1,0:T(8,128)(2,1)S(1)} %collective-permute-done.5.refs_11_), channel_id=1, source_target_pairs={{0,8},{2,6},{4,0},{6,14},{8,16},{10,2},{12,4},{14,22},{16,24},{18,... | collective-permute-start | bytes 589832 | tf_op jit(solution)/shard_map/ppermute | solution.py:343
  25.2 18.3 %copy-start.16 = (bf16[384,256]{1,0:T(8,128)(2,1)}, bf16[384,256]{1,0:T(8,128)(2,1)S(1)}, u32[]{:S(2)}) copy-start(bf16[384,256]{1,0:T(8,128)(2,1)S(1)} %collective-permute-done.3.refs_9_) | copy-start | bytes 589828
  25.2 8.0 %collective-permute-start.7 = (bf16[384,256]{1,0:T(8,128)(2,1)S(1)}, bf16[384,256]{1,0:T(8,128)(2,1)S(1)}, u32[]{:S(2)}, u32[]{:S(2)}) collective-permute-start(bf16[384,256]{1,0:T(8,128)(2,1)S(1)} %collective-permute-done.5.refs_11_), channel_id=1, source_target_pairs={{0,2},{2,0},{4,6},{6,4},{8,10},{10,8},{12,14},{14,12},{16,18},{18,... | collective-permute-start | bytes 589832 | tf_op jit(solution)/shard_map/ppermute | solution.py:296
  25.3 18.2 %copy-start.17 = (bf16[384,256]{1,0:T(8,128)(2,1)}, bf16[384,256]{1,0:T(8,128)(2,1)S(1)}, u32[]{:S(2)}) copy-start(bf16[384,256]{1,0:T(8,128)(2,1)S(1)} %collective-permute-done.4.refs_10_) | copy-start | bytes 589828
  25.3 18.2 %copy-start.15 = (bf16[384,256]{1,0:T(8,128)(2,1)}, bf16[384,256]{1,0:T(8,128)(2,1)S(1)}, u32[]{:S(2)}) copy-start(bf16[384,256]{1,0:T(8,128)(2,1)S(1)} %collective-permute-done.6.refs_12_) | copy-start | bytes 589828
  25.3 6.0 %collective-permute-start.10 = (bf16[384,256]{1,0:T(8,128)(2,1)S(1)}, bf16[384,256]{1,0:T(8,128)(2,1)S(1)}, u32[]{:S(2)}, u32[]{:S(2)}) collective-permute-start(bf16[384,256]{1,0:T(8,128)(2,1)S(1)} %collective-permute-done.6.refs_12_), channel_id=1, source_target_pairs={{0,8},{2,6},{4,0},{6,14},{8,16},{10,2},{12,4},{14,22},{16,24},{18,... | collective-permute-start | bytes 589832 | tf_op jit(solution)/shard_map/ppermute | solution.py:344
  26.9 6.3 %collective-permute-start.8 = (bf16[384,256]{1,0:T(8,128)(2,1)S(1)}, bf16[384,256]{1,0:T(8,128)(2,1)S(1)}, u32[]{:S(2)}, u32[]{:S(2)}) collective-permute-start(bf16[384,256]{1,0:T(8,128)(2,1)S(1)} %collective-permute-done.6.refs_12_), channel_id=1, source_target_pairs={{0,2},{2,0},{4,6},{6,4},{8,10},{10,8},{12,14},{14,12},{16,18},{18,... | collective-permute-start | bytes 589832 | tf_op jit(solution)/shard_map/ppermute | solution.py:296
  29.3 14.3 %copy-start.8 = (bf16[384,256]{1,0:T(8,128)(2,1)}, bf16[384,256]{1,0:T(8,128)(2,1)S(1)}, u32[]{:S(2)}) copy-start(bf16[384,256]{1,0:T(8,128)(2,1)S(1)} %collective-permute-done.9.refs_15_) | copy-start | bytes 589828
  31.4 12.2 %copy-start.9 = (bf16[384,256]{1,0:T(8,128)(2,1)}, bf16[384,256]{1,0:T(8,128)(2,1)S(1)}, u32[]{:S(2)}) copy-start(bf16[384,256]{1,0:T(8,128)(2,1)S(1)} %collective-permute-done.10.refs_16_) | copy-start | bytes 589828
  31.4 5.9 %collective-permute-start.13 = (bf16[384,256]{1,0:T(8,128)(2,1)S(1)}, bf16[384,256]{1,0:T(8,128)(2,1)S(1)}, u32[]{:S(2)}, u32[]{:S(2)}) collective-permute-start(bf16[384,256]{1,0:T(8,128)(2,1)S(1)} %broadcast_select_fusion), channel_id=1, source_target_pairs={{0,8},{2,6},{4,0},{6,14},{8,16},{10,2},{12,4},{14,22},{16,24},{18,... | collective-permute-start | bytes 589832 | tf_op jit(solution)/shard_map/ppermute | solution.py:355
  33.2 10.3 %copy-start.18 = (bf16[384,256]{1,0:T(8,128)(2,1)}, bf16[384,256]{1,0:T(8,128)(2,1)S(1)}, u32[]{:S(2)}) copy-start(bf16[384,256]{1,0:T(8,128)(2,1)S(1)} %collective-permute-done.7.refs_13_) | copy-start | bytes 589828
  33.2 10.3 %copy-start.19 = (bf16[384,256]{1,0:T(8,128)(2,1)}, bf16[384,256]{1,0:T(8,128)(2,1)S(1)}, u32[]{:S(2)}) copy-start(bf16[384,256]{1,0:T(8,128)(2,1)S(1)} %collective-permute-done.8.refs_14_) | copy-start | bytes 589828
  33.3 10.3 %copy-start.11 = (bf16[5,2,48,256]{3,2,1,0:T(8,128)(2,1)}, bf16[5,2,48,256]{3,2,1,0:T(8,128)(2,1)S(1)}, u32[]{:S(2)}) copy-start(bf16[5,2,48,256]{3,2,1,0:T(8,128)(2,1)S(1)} %fusion.4.refs_0_) | copy-start | bytes 737284
  33.3 7.5 %collective-permute-start.15 = (bf16[5,2,48,256]{3,2,1,0:T(8,128)(2,1)S(1)}, bf16[5,2,48,256]{3,2,1,0:T(8,128)(2,1)S(1)}, u32[]{:S(2)}, u32[]{:S(2)}) collective-permute-start(bf16[5,2,48,256]{3,2,1,0:T(8,128)(2,1)S(1)} %fusion.4.refs_0_), channel_id=1, source_target_pairs={{0,1},{1,0},{2,3},{3,2},{4,5},{5,4},{6,7},{7,6},{8,9},{9,8},{10,11... | collective-permute-start | bytes 737288 | tf_op jit(solution)/shard_map/ppermute | solution.py:325
  34.8 2.5 %collective-permute-start.11 = (bf16[384,256]{1,0:T(8,128)(2,1)S(1)}, bf16[384,256]{1,0:T(8,128)(2,1)S(1)}, u32[]{:S(2)}, u32[]{:S(2)}) collective-permute-start(bf16[384,256]{1,0:T(8,128)(2,1)S(1)} %collective-permute-done.9.refs_15_), channel_id=1, source_target_pairs={{0,2},{2,0},{4,6},{6,4},{8,10},{10,8},{12,14},{14,12},{16,18},{18,... | collective-permute-start | bytes 589832 | tf_op jit(solution)/shard_map/ppermute | solution.py:296
  34.8 2.5 %collective-permute-start.12 = (bf16[384,256]{1,0:T(8,128)(2,1)S(1)}, bf16[384,256]{1,0:T(8,128)(2,1)S(1)}, u32[]{:S(2)}, u32[]{:S(2)}) collective-permute-start(bf16[384,256]{1,0:T(8,128)(2,1)S(1)} %collective-permute-done.10.refs_16_), channel_id=1, source_target_pairs={{0,2},{2,0},{4,6},{6,4},{8,10},{10,8},{12,14},{14,12},{16,18},{18,... | collective-permute-start | bytes 589832 | tf_op jit(solution)/shard_map/ppermute | solution.py:296
  37.3 6.3 %copy-start.20 = (bf16[384,256]{1,0:T(8,128)(2,1)}, bf16[384,256]{1,0:T(8,128)(2,1)S(1)}, u32[]{:S(2)}) copy-start(bf16[384,256]{1,0:T(8,128)(2,1)S(1)} %collective-permute-done.13.refs_19_) | copy-start | bytes 589828
  37.3 2.7 %collective-permute-start.14 = (bf16[384,256]{1,0:T(8,128)(2,1)S(1)}, bf16[384,256]{1,0:T(8,128)(2,1)S(1)}, u32[]{:S(2)}, u32[]{:S(2)}) collective-permute-start(bf16[384,256]{1,0:T(8,128)(2,1)S(1)} %collective-permute-done.13.refs_19_), channel_id=1, source_target_pairs={{0,2},{2,0},{4,6},{6,4},{8,10},{10,8},{12,14},{14,12},{16,18},{18,... | collective-permute-start | bytes 589832 | tf_op jit(solution)/shard_map/ppermute | solution.py:296
  37.3 6.3 %copy-start.21 = (bf16[384,256]{1,0:T(8,128)(2,1)}, bf16[384,256]{1,0:T(8,128)(2,1)S(1)}, u32[]{:S(2)}) copy-start(bf16[384,256]{1,0:T(8,128)(2,1)S(1)} %collective-permute-done.11.refs_17_) | copy-start | bytes 589828
  37.3 6.3 %copy-start.22 = (bf16[384,256]{1,0:T(8,128)(2,1)}, bf16[384,256]{1,0:T(8,128)(2,1)S(1)}, u32[]{:S(2)}) copy-start(bf16[384,256]{1,0:T(8,128)(2,1)S(1)} %collective-permute-done.12.refs_18_) | copy-start | bytes 589828
  37.4 6.2 %copy-start.10 = (bf16[2,2,48,256]{3,2,1,0:T(8,128)(2,1)}, bf16[2,2,48,256]{3,2,1,0:T(8,128)(2,1)S(1)}, u32[]{:S(2)}) copy-start(bf16[2,2,48,256]{3,2,1,0:T(8,128)(2,1)S(1)} %pad_maximum_fusion.refs_1_) | copy-start | bytes 294916
  37.4 6.0 %collective-permute-start.16 = (bf16[2,2,48,256]{3,2,1,0:T(8,128)(2,1)S(1)}, bf16[2,2,48,256]{3,2,1,0:T(8,128)(2,1)S(1)}, u32[]{:S(2)}, u32[]{:S(2)}) collective-permute-start(bf16[2,2,48,256]{3,2,1,0:T(8,128)(2,1)S(1)} %pad_maximum_fusion.refs_1_), channel_id=1, source_target_pairs={{0,1},{1,0},{2,3},{3,2},{4,5},{5,4},{6,7},{7,6},{8,9},{9,8},{10,11... | collective-permute-start | bytes 294920 | tf_op jit(solution)/shard_map/ppermute | solution.py:325
  40.0 3.6 %copy-start.23 = (bf16[384,256]{1,0:T(8,128)(2,1)}, bf16[384,256]{1,0:T(8,128)(2,1)S(1)}, u32[]{:S(2)}) copy-start(bf16[384,256]{1,0:T(8,128)(2,1)S(1)} %collective-permute-done.14.refs_20_) | copy-start | bytes 589828
  40.7 2.9 %copy-start.26 = (bf16[1,2,48,256]{3,2,1,0:T(8,128)(2,1)}, bf16[1,2,48,256]{3,2,1,0:T(8,128)(2,1)S(1)}, u32[]{:S(2)}) copy-start(bf16[1,2,48,256]{3,2,1,0:T(8,128)(2,1)S(1)} %collective-permute-done.17.refs_5_) | copy-start | bytes 147460
  40.8 2.9 %copy-start.24 = (bf16[5,2,48,256]{3,2,1,0:T(8,128)(2,1)}, bf16[5,2,48,256]{3,2,1,0:T(8,128)(2,1)S(1)}, u32[]{:S(2)}) copy-start(bf16[5,2,48,256]{3,2,1,0:T(8,128)(2,1)S(1)} %collective-permute-done.15.refs_3_) | copy-start | bytes 737284
  43.5 0.6 copy-start.25

commit v4 on v3

--- a/solution.py
+++ b/solution.py
@@ -23,7 +23,7 @@
 
 def project_body(core_ref, x_ref, gain_ref, bias_ref, weight_ref, pbias_ref, out_ref):
     local, _, _ = x_ref.shape
-    width = weight_ref.shape[1]
+    width = weight_ref.shape[0]
     group = 2 * local
     lanes = width * group
     first = core_ref[0] * local
@@ -32,7 +32,10 @@
     total = None
     for s in range(local):
         normed = norm_rows(x_ref[s].astype(F32), gain_ref[...], bias_ref[...]).astype(BF16)
-        y = jnp.dot(normed, weight_ref[...], preferred_element_type=F32) + pbias_ref[...]
+        y = lax.dot_general(
+            normed, weight_ref[...], (((1,), (1,)), ((), ())), preferred_element_type=F32
+        )
+        y = y + pbias_ref[...]
         spread = (lane == ch * group + (first + s)).astype(F32).astype(BF16)
         part = jnp.dot(y.astype(BF16), spread, preferred_element_type=F32)
         total = part if total is None else total + part
@@ -41,15 +44,21 @@
     out_ref[1] = total[:, half:].astype(BF16)
 
 
+def whole(a):
+    return pl.BlockSpec(a.shape, lambda i: (0,) * len(a.shape))
+
+
 def project(core, x, gain, bias, weight, pbias):
     local, residues, _ = x.shape
-    lanes = weight.shape[1] * local
-    vmem = pl.BlockSpec(memory_space=pltpu.VMEM)
+    lanes = weight.shape[0] * local
+    out = jax.ShapeDtypeStruct((2, residues, lanes), BF16)
     return pl.pallas_call(
         project_body,
-        in_specs=[pl.BlockSpec(memory_space=pltpu.SMEM)] + [vmem] * 5,
-        out_specs=vmem,
-        out_shape=jax.ShapeDtypeStruct((2, residues, lanes), BF16),
+        grid=(1,),
+        in_specs=[pl.BlockSpec(memory_space=pltpu.SMEM)]
+        + [whole(a) for a in (x, gain, bias, weight, pbias)],
+        out_specs=whole(out),
+        out_shape=out,
         compiler_params=pltpu.CompilerParams(vmem_limit_bytes=32 << 20),
     )(core, x, gain, bias, weight, pbias)
 
@@ -92,15 +101,16 @@
 
 def split_weight(w_out, half, total):
     zc = w_out.shape[1]
-    vmem = pl.BlockSpec(memory_space=pltpu.VMEM)
+    outs = [
+        jax.ShapeDtypeStruct((8 * half, 2 * half * zc), F8),
+        jax.ShapeDtypeStruct((1, zc), F32),
+    ]
     return pl.pallas_call(
         functools.partial(split_weight_body, total),
-        in_specs=[vmem],
-        out_specs=[vmem, vmem],
-        out_shape=[
-            jax.ShapeDtypeStruct((8 * half, 2 * half * zc), F8),
-            jax.ShapeDtypeStruct((1, zc), F32),
-        ],
+        grid=(1,),
+        in_specs=[whole(w_out)],
+        out_specs=[whole(a) for a in outs],
+        out_shape=outs,
         scratch_shapes=[pltpu.VMEM(w_out.shape, F32)],
         compiler_params=pltpu.CompilerParams(vmem_limit_bytes=32 << 20),
     )(w_out)
@@ -232,9 +242,6 @@
     depth = chips * part
     lanes = 4 * part // group
 
-    def whole(a):
-        return pl.BlockSpec(a.shape, lambda i: (0,) * a.ndim)
-
     return pl.pallas_call(
         functools.partial(pair_body, chips, here, group, len(rows_here)),
         grid=(row_length // here,),
@@ -255,14 +262,16 @@
     )(place, *rows_here, *rows_there, *cols, *rest)
 
 
-def chip_ring(chips):
-    order = list(range(0, chips, 2)) + list(range(chips - 1, 0, -2))
-    after = {order[i]: order[(i + 1) % chips] for i in range(chips)}
-    before = {v: k for k, v in after.items()}
+def ring_order(chips):
+    return list(range(0, chips, 2)) + list(range(chips - 1, 0, -2))
+
+
+def ring_source(chips, steps):
+    order = ring_order(chips)
+    place = {q: i for i, q in enumerate(order)}
     return [
-        (2 * q + core, 2 * (after if core == 0 else before)[q] + core)
-        for q in range(chips)
-        for core in range(2)
+        2 * order[(place[r // 2] + (steps if r % 2 else -steps)) % chips] + r % 2
+        for r in range(2 * chips)
     ]
 
 
@@ -295,14 +304,14 @@
     def swap(a):
         return lax.ppermute(a, "row", [(r, r ^ 1) for r in range(row_count)])
 
-    ring = chip_ring(chips)
+    ring = [(src, r) for r, src in enumerate(ring_source(chips, 1))]
 
     mine = project(
         core.reshape(1),
         alignment,
         alignment_norm_gain[None],
         alignment_norm_bias[None],
-        projection_weight,
+        projection_weight.T,
         projection_bias_pair[None],
     )
     own = mine + swap(mine)
@@ -329,27 +338,29 @@
     right, left = own[0], own[1]
     cols = [own]
     early = [(right, left)]
+    steps = chips // 2 - 1
+
+    def direct(hops):
+        sources = ring_source(chips, hops)
+        targets = [sources.index(r) for r in range(row_count)]
+        first = jnp.array([t % per_col * row_length for t in targets], jnp.int32)[row_index]
+        pairs = [(2 * r + t // per_col, 2 * t + 1 - t // per_col) for r, t in enumerate(targets)]
+        return lax.ppermute(cut([(right, left)], first), ("row", "col"), pairs)
+
     if col_count == 2:
-        opposite = [row_count - 2 - r + 2 * (r % 2) for r in range(row_count)]
-        target = row_count - 2 - row_index + 2 * core
-        far_there = lax.ppermute(
-            cut(early, (target % per_col) * row_length),
-            ("row", "col"),
-            [(2 * r + t // per_col, 2 * t + 1 - t // per_col) for r, t in enumerate(opposite)],
-        )
+        straight = [direct(steps), direct(-steps), direct(steps + 1)]
     rows = []
-    steps = chips // 2 - 1
     for d in range(steps):
         right = lax.ppermute(right, "row", ring)
         left = lax.ppermute(left, "row", ring)
         pieces = [(right, left), (swap(right), swap(left))]
         for pair in pieces:
             cols.extend(pair)
-        early.extend(pieces)
-        if d >= steps - 2:
+        if d < steps - 1:
+            early.extend(pieces)
+        if d == steps - 2:
             rows.append(exchange(early))
-            early = []
-        if d == 0:
+        if d == steps - 1:
             params = (w_out, b_out, pair_gain, pair_bias, w_up, b_up, w_down, b_down)
             *params, right, left = lax.optimization_barrier((*params, right, left))
     far = lax.ppermute(jnp.where(core == 0, right, left), "row", ring)
@@ -358,11 +369,14 @@
     a = lax.dynamic_slice_in_dim(far, start, row_length, 0)
     b = lax.dynamic_slice_in_dim(far_other, start, row_length, 0)
     far_pair = (jnp.where(core == 0, a, b), jnp.where(core == 0, b, a))
+    pieces = pieces + [far_pair]
+    last = cut(pieces[:2], start)
     if col_count == 2:
-        rows.append((jnp.stack(far_pair)[None], far_there))
+        rows.extend([(last[:1], straight[0]), (last[1:], straight[1])])
+        rows.append((jnp.stack(far_pair)[None], straight[2]))
     else:
-        block = lax.all_gather(jnp.stack(far_pair)[None], "col")
-        block = lax.dynamic_index_in_dim(block, source, 0, False)
+        last = jnp.concatenate([last, jnp.stack(far_pair)[None]])
+        block = lax.dynamic_index_in_dim(lax.all_gather(last, "col"), source, 0, False)
         rows.append((block, block))
 
     group = 2 * local

time: 89.8 us -> 110 us (1.22)
  starting transfers between devices: 19.7 us -> 34.6 us
  between operations: 0.6 us -> 6.08 us
  waiting for transfers between devices: 13.3 us -> 8.67 us
  local copies, waits for them, and re-layouts: 7.55 us -> 10.3 us
  other arithmetic: 1.48 us -> 2.76 us
    ppermute x3, starting transfers between devices: 6.7 us -> 12.7 us  [shards(): right = lax.ppermute(right, 'row', ring)]
    ppermute x3, starting transfers between devices: 4.73 us -> 9.54 us  [shards(): left = lax.ppermute(left, 'row', ring)]
    dynamic_slice x0 -> x3, local copies, waits for them, and re-layouts: none -> 3.8 us  [direct(): jnp.array([t % per_col * row_length for t in targets], jnp.int32)[row_index]]
    ppermute x3, waiting for transfers between devices: 3.63 us -> 1.12 us  [shards(): right = lax.ppermute(right, 'row', ring)]
    ppermute x2 -> x1, starting transfers between devices: 4.16 us -> 6.58 us  [exchange(): return (block, lax.ppermute(block, 'col', [(0, 1), (1, 0)]))]
    ppermute x1, waiting for transfers between devices: 1.94 us -> 0.01 us  [shards(): far = lax.ppermute(jnp.where(core == 0, right, left), 'row', ring)]
    ppermute x3, waiting for transfers between devices: 4.21 us -> 2.71 us  [shards(): left = lax.ppermute(left, 'row', ring)]
    ppermute x1 -> x3, starting transfers between devices: 0.66 us -> 2.16 us  [direct(): return lax.ppermute(cut([(right, left)], first), ('row', 'col'), pairs)]
  transfers between devices with their start and end apart: 18 -> 19, of which waited for: 7 -> 6; matrix products, arithmetic and copies ran while one was open for 2% -> 6% of each run, Pallas kernels for 1% -> 0%
where the time goes in v4:
time: 110 us; the launch traced here: 109 us
  Pallas kernels  46.9 us (43%)
  starting transfers between devices  34.6 us (31%)
  local copies, waits for them, and re-layouts  10.3 us (9%)
  waiting for transfers between devices  8.67 us (8%)
  between operations  6.08 us (6%)
  other arithmetic  2.76 us (3%)
    pallas_call x1, Pallas kernels, pair_kernel(): pl.pallas_call(functools.partial(pair_body, chips, here, group, len(rows_...  45.2 us
    ppermute x3, starting transfers between devices, shards(): right = lax.ppermute(right, 'row', ring)  12.7 us
    ppermute x3, starting transfers between devices, shards(): left = lax.ppermute(left, 'row', ring)  9.54 us
    ppermute x1, starting transfers between devices, exchange(): return (block, lax.ppermute(block, 'col', [(0, 1), (1, 0)]))  6.58 us
    unnamed x56, local copies, waits for them, and re-layouts  6.34 us
    dynamic_slice x3, local copies, waits for them, and re-layouts, direct(): jnp.array([t % per_col * row_length for t in targets], jnp.int32)[row_index]  3.8 us
    ppermute x1, waiting for transfers between devices, exchange(): return (block, lax.ppermute(block, 'col', [(0, 1), (1, 0)]))  3.79 us
    ppermute x3, waiting for transfers between devices, shards(): left = lax.ppermute(left, 'row', ring)  2.71 us
  transfers between devices with their start and end apart: 19, of which 6 were waited for; matrix products, arithmetic and copies ran while one was open for 6% of the time, Pallas kernels for 0%

profile of v4, /device:TPU:0, one launch (start us, length us, event | category | flops | bytes accessed | tf_op | source)
XLA Modules:
  0.0 109.3 jit_solution(7342540936151730037)
XLA Ops:
  0.0 1.1 %copy-done.1 = bf16[4,384,256]{2,1,0:T(8,128)(2,1)S(1)} copy-done((bf16[4,384,256]{2,1,0:T(8,128)(2,1)S(1)}, bf16[4,384,256]{2,1,0:T(8,128)(2,1)}, u32[]{:S(2)}) %copy-start.1) | copy-done | bytes 786456
  1.1 0.8 copy-done.3
  1.9 0.7 copy-done.4
  2.6 0.7 copy-done.5
  3.3 0.7 copy-done.6
  3.9 1.2 %shard_map.154 = bf16[2,384,256]{2,1,0:T(8,128)(2,1)S(1)} custom-call(s32[1]{0:T(128)} %bitcast.core_ref, bf16[4,384,256]{2,1,0:T(8,128)(2,1)S(1)} %copy-done.1, f32[1,256]{1,0:T(1,128)S(1)} %bitcast.79, f32[1,256]{1,0:T(1,128)S(1)} %bitcast.80, bf16[64,256]{1,0:T(8,128)(2,1)S(1)} %bitcast.78, f32[1,64]{1,0:T(1,128)S(1)} %bitcast.81), custom_call_target="tpu_custom_call" | custom-call | tf_op jit(solution)/shard_map/pallas_call | solution.py:55
  5.1 0.5 collective-permute-start
  5.6 1.3 %dynamic_slice.97 = s32[1]{0:T(128)} dynamic-slice(s32[16]{0:T(128)} %constant.66.clone, s32[]{:T(128)S(6)} %select_n.79), dynamic_slice_sizes={1} | dynamic-slice | bytes 12 | tf_op jit(solution)/shard_map/dynamic_slice | solution.py:346
  8.1 1.3 %dynamic_slice.94 = s32[1]{0:T(128)} dynamic-slice(s32[16]{0:T(128)} %constant.65.clone, s32[]{:T(128)S(6)} %select_n.79), dynamic_slice_sizes={1} | dynamic-slice | bytes 12 | tf_op jit(solution)/shard_map/dynamic_slice | solution.py:346
  10.7 1.2 %dynamic_slice.91 = s32[1]{0:T(128)} dynamic-slice(s32[16]{0:T(128)} %constant.64.clone, s32[]{:T(128)S(6)} %select_n.79), dynamic_slice_sizes={1} | dynamic-slice | bytes 12 | tf_op jit(solution)/shard_map/dynamic_slice | solution.py:346
  14.9 0.6 pad_add_fusion.place_ref
  15.5 0.0 collective-permute-done
  15.5 0.1 add.21.refs_8_
  15.6 0.0 copy-start.8
  15.6 0.1 slice_bitcast_fusion.1
  15.7 0.7 collective-permute-start.16
  16.4 0.7 collective-permute-start.17
  17.1 7.0 %collective-permute-start.1 = (bf16[384,256]{1,0:T(8,128)(2,1)S(1)}, bf16[384,256]{1,0:T(8,128)(2,1)S(1)}, u32[]{:S(2)}, u32[]{:S(2)}) collective-permute-start(bf16[384,256]{1,0:T(8,128)(2,1)S(1)} %get-tuple-element.31), channel_id=1, source_target_pairs={{4,0},{10,2},{12,4},{2,6},{0,8},{18,10},{20,12},{6,14},{8,16},{26,... | collective-permute-start | bytes 589832 | tf_op jit(solution)/shard_map/ppermute | solution.py:354
  24.1 4.5 %collective-permute-start.2 = (bf16[384,256]{1,0:T(8,128)(2,1)S(1)}, bf16[384,256]{1,0:T(8,128)(2,1)S(1)}, u32[]{:S(2)}, u32[]{:S(2)}) collective-permute-start(bf16[384,256]{1,0:T(8,128)(2,1)S(1)} %get-tuple-element.32), channel_id=1, source_target_pairs={{4,0},{10,2},{12,4},{2,6},{0,8},{18,10},{20,12},{6,14},{8,16},{26,... | collective-permute-start | bytes 589832 | tf_op jit(solution)/shard_map/ppermute | solution.py:355
  28.5 0.0 collective-permute-done.1.refs_9_
  28.6 0.0 copy-start.12
  28.6 3.2 %collective-permute-start.5 = (bf16[384,256]{1,0:T(8,128)(2,1)S(1)}, bf16[384,256]{1,0:T(8,128)(2,1)S(1)}, u32[]{:S(2)}, u32[]{:S(2)}) collective-permute-start(bf16[384,256]{1,0:T(8,128)(2,1)S(1)} %collective-permute-done.1.refs_9_), channel_id=1, source_target_pairs={{4,0},{10,2},{12,4},{2,6},{0,8},{18,10},{20,12},{6,14},{8,16},{26,... | collective-permute-start | bytes 589832 | tf_op jit(solution)/shard_map/ppermute | solution.py:354
  31.7 0.0 collective-permute-start.3
  31.7 0.0 collective-permute-done.2.refs_10_
  31.7 0.0 copy-start.13
  31.7 2.5 %collective-permute-start.6 = (bf16[384,256]{1,0:T(8,128)(2,1)S(1)}, bf16[384,256]{1,0:T(8,128)(2,1)S(1)}, u32[]{:S(2)}, u32[]{:S(2)}) collective-permute-start(bf16[384,256]{1,0:T(8,128)(2,1)S(1)} %collective-permute-done.2.refs_10_), channel_id=1, source_target_pairs={{4,0},{10,2},{12,4},{2,6},{0,8},{18,10},{20,12},{6,14},{8,16},{26,... | collective-permute-start | bytes 589832 | tf_op jit(solution)/shard_map/ppermute | solution.py:355
  34.3 0.6 collective-permute-done.5.refs_13_
  34.9 0.0 collective-permute-start.4
  34.9 0.0 collective-permute-done.3.refs_11_
  34.9 0.0 copy-start.15
  34.9 2.5 %collective-permute-start.9 = (bf16[384,256]{1,0:T(8,128)(2,1)S(1)}, bf16[384,256]{1,0:T(8,128)(2,1)S(1)}, u32[]{:S(2)}, u32[]{:S(2)}) collective-permute-start(bf16[384,256]{1,0:T(8,128)(2,1)S(1)} %collective-permute-done.5.refs_13_), channel_id=1, source_target_pairs={{4,0},{10,2},{12,4},{2,6},{0,8},{18,10},{20,12},{6,14},{8,16},{26,... | collective-permute-start | bytes 589832 | tf_op jit(solution)/shard_map/ppermute | solution.py:354
  37.5 0.0 collective-permute-done.4.refs_12_
  37.5 0.1 collective-permute-start.7
  37.6 0.0 collective-permute-done.6.refs_14_
  37.6 0.0 copy-start.16
  37.6 2.5 %collective-permute-start.10 = (bf16[384,256]{1,0:T(8,128)(2,1)S(1)}, bf16[384,256]{1,0:T(8,128)(2,1)S(1)}, u32[]{:S(2)}, u32[]{:S(2)}) collective-permute-start(bf16[384,256]{1,0:T(8,128)(2,1)S(1)} %collective-permute-done.6.refs_14_), channel_id=1, source_target_pairs={{4,0},{10,2},{12,4},{2,6},{0,8},{18,10},{20,12},{6,14},{8,16},{26,... | collective-permute-start | bytes 589832 | tf_op jit(solution)/shard_map/ppermute | solution.py:355
  40.2 0.5 collective-permute-done.9.refs_17_
  40.7 0.1 collective-permute-start.8
  40.8 2.7 %collective-permute-done.10.refs_18_ = bf16[384,256]{1,0:T(8,128)(2,1)S(1)} collective-permute-done((bf16[384,256]{1,0:T(8,128)(2,1)S(1)}, bf16[384,256]{1,0:T(8,128)(2,1)S(1)}, u32[]{:S(2)}, u32[]{:S(2)}) %collective-permute-start.10) | collective-permute-done | bytes 196640 | tf_op jit(solution)/shard_map/ppermute | solution.py:355
  43.5 2.4 %collective-permute-start.13 = (bf16[384,256]{1,0:T(8,128)(2,1)S(1)}, bf16[384,256]{1,0:T(8,128)(2,1)S(1)}, u32[]{:S(2)}, u32[]{:S(2)}) collective-permute-start(bf16[384,256]{1,0:T(8,128)(2,1)S(1)} %broadcast_select_fusion), channel_id=1, source_target_pairs={{4,0},{10,2},{12,4},{2,6},{0,8},{18,10},{20,12},{6,14},{8,16},{26,... | collective-permute-start | bytes 589832 | tf_op jit(solution)/shard_map/ppermute | solution.py:366
  45.9 0.5 shard_map.155
  46.4 1.3 %copy-done = f8e4m3fn[256,8192]{1,0:T(32,128)(4,1)} copy-done((f8e4m3fn[256,8192]{1,0:T(32,128)(4,1)}, f8e4m3fn[256,8192]{1,0:T(32,128)(4,1)S(1)}, u32[]{:S(2)}) %copy-start) | copy-done | bytes 2097176
  47.8 0.5 copy-done.7
  48.3 0.0 collective-permute-done.7.refs_15_
  48.3 0.0 copy-start.18
  48.3 0.1 collective-permute-start.11
  48.4 0.6 maximum_bitcast_fusion.5.refs_1_
  49.0 0.0 collective-permute-done.8.refs_16_
  49.0 0.5 collective-permute-start.12
  49.5 0.3 collective-permute-done.11.refs_19_
  49.8 0.8 collective-permute-start.18
  50.7 0.0 collective-permute-done.13.refs_21_
  50.7 6.6 %collective-permute-start.15 = (bf16[5,2,48,256]{3,2,1,0:T(8,128)(2,1)S(1)}, bf16[5,2,48,256]{3,2,1,0:T(8,128)(2,1)S(1)}, u32[]{:S(2)}, u32[]{:S(2)}) collective-permute-start(bf16[5,2,48,256]{3,2,1,0:T(8,128)(2,1)S(1)} %fusion.4.refs_0_), channel_id=1, source_target_pairs={{0,1},{1,0},{2,3},{3,2},{4,5},{5,4},{6,7},{7,6},{8,9},{9,8},{10,11... | collective-permute-start | bytes 737288 | tf_op jit(solution)/shard_map/ppermute | solution.py:334
  57.3 0.0 collective-permute-done.12.refs_20_
  57.3 0.0 collective-permute-start.14
  57.3 0.7 maximum_bitcast_fusion.6.refs_2_
  58.0 0.7 collective-permute-done.14.refs_22_
  58.7 0.7 maximum_bitcast_fusion.7.refs_3_
  59.4 0.0 collective-permute-done.16.refs_5_
  59.4 0.0 collective-permute-done.17.refs_6_
  59.4 0.0 collective-permute-done.18.refs_7_
  59.5 3.8 %collective-permute-done.15.refs_4_ = bf16[5,2,48,256]{3,2,1,0:T(8,128)(2,1)S(1)} collective-permute-done((bf16[5,2,48,256]{3,2,1,0:T(8,128)(2,1)S(1)}, bf16[5,2,48,256]{3,2,1,0:T(8,128)(2,1)S(1)}, u32[]{:S(2)}, u32[]{:S(2)}) %collective-permute-start.15) | collective-permute-done | bytes 245792 | tf_op jit(solution)/shard_map/ppermute | solution.py:334
  63.4 0.5 copy-done.24
  63.9 45.2 %shard_map.156 = bf16[48,384,128]{2,1,0:T(8,128)(2,1)} custom-call(s32[2]{0:T(128)} %pad_add_fusion.place_ref, bf16[5,2,48,256]{3,2,1,0:T(8,128)(2,1)} %copy-done.11, bf16[1,2,48,256]{3,2,1,0:T(8,128)(2,1)} %maximum_bitcast_fusion.5.refs_1_, bf16[1,2,48,256]{3,2,1,0:T(8,128)(2,1)} %maximum_bitcast_fusion.6.refs_2_, ...), custom_call_target="tpu_custom_call" | custom-call | tf_op jit(solution)/shard_map/pallas_call | solution.py:245
  (65 shorter events, 0.3 us)
Async XLA Ops:
  0.0 1.1 %copy-start.1 = (bf16[4,384,256]{2,1,0:T(8,128)(2,1)S(1)}, bf16[4,384,256]{2,1,0:T(8,128)(2,1)}, u32[]{:S(2)}) copy-start(bf16[4,384,256]{2,1,0:T(8,128)(2,1)} %x_ref.1) | copy-start | bytes 2359300
  1.1 0.8 copy-start.3
  1.9 0.7 copy-start.4
  2.6 0.7 copy-start.5
  3.3 0.7 copy-start.6
  3.9 42.0 %copy-start.2 = (bf16[1024,128]{1,0:T(8,128)(2,1)S(1)}, bf16[1024,128]{1,0:T(8,128)(2,1)}, u32[]{:S(2)}) copy-start(bf16[1024,128]{1,0:T(8,128)(2,1)} %w_ref) | copy-start | bytes 786436
  5.1 10.4 %collective-permute-start = (bf16[2,384,256]{2,1,0:T(8,128)(2,1)S(1)}, bf16[2,384,256]{2,1,0:T(8,128)(2,1)S(1)}, u32[]{:S(2)}, u32[]{:S(2)}) collective-permute-start(bf16[2,384,256]{2,1,0:T(8,128)(2,1)S(1)} %shard_map.154), channel_id=1, source_target_pairs={{0,2},{2,0},{4,6},{6,4},{8,10},{10,8},{12,14},{14,12},{16,18},{18,... | collective-permute-start | bytes 1179656 | tf_op jit(solution)/shard_map/ppermute | solution.py:305
  15.6 47.7 %copy-start.8 = (bf16[2,384,256]{2,1,0:T(8,128)(2,1)}, bf16[2,384,256]{2,1,0:T(8,128)(2,1)S(1)}, u32[]{:S(2)}) copy-start(bf16[2,384,256]{2,1,0:T(8,128)(2,1)S(1)} %add.21.refs_8_) | copy-start | bytes 1179652
  15.7 43.7 %collective-permute-start.16 = (bf16[1,2,48,256]{3,2,1,0:T(8,128)(2,1)S(1)}, bf16[1,2,48,256]{3,2,1,0:T(8,128)(2,1)S(1)}, u32[]{:S(2)}, u32[]{:S(2)}) collective-permute-start(bf16[1,2,48,256]{3,2,1,0:T(8,128)(2,1)S(1)} %maximum_bitcast_fusion.8), channel_id=1, source_target_pairs={{1,24},{3,22},{5,16},{7,30},{9,28},{10,15},{12,9},{15,26},{17,20},... | collective-permute-start | bytes 147464 | tf_op jit(solution)/shard_map/ppermute | solution.py:348
  16.4 43.0 %collective-permute-start.17 = (bf16[1,2,48,256]{3,2,1,0:T(8,128)(2,1)S(1)}, bf16[1,2,48,256]{3,2,1,0:T(8,128)(2,1)S(1)}, u32[]{:S(2)}, u32[]{:S(2)}) collective-permute-start(bf16[1,2,48,256]{3,2,1,0:T(8,128)(2,1)S(1)} %maximum_bitcast_fusion.9), channel_id=1, source_target_pairs={{1,20},{3,26},{5,28},{7,18},{8,13},{11,30},{13,24},{14,11},{16,5},... | collective-permute-start | bytes 147464 | tf_op jit(solution)/shard_map/ppermute | solution.py:348
  17.1 11.5 %collective-permute-start.1 = (bf16[384,256]{1,0:T(8,128)(2,1)S(1)}, bf16[384,256]{1,0:T(8,128)(2,1)S(1)}, u32[]{:S(2)}, u32[]{:S(2)}) collective-permute-start(bf16[384,256]{1,0:T(8,128)(2,1)S(1)} %get-tuple-element.31), channel_id=1, source_target_pairs={{4,0},{10,2},{12,4},{2,6},{0,8},{18,10},{20,12},{6,14},{8,16},{26,... | collective-permute-start | bytes 589832 | tf_op jit(solution)/shard_map/ppermute | solution.py:354
  24.1 7.7 %collective-permute-start.2 = (bf16[384,256]{1,0:T(8,128)(2,1)S(1)}, bf16[384,256]{1,0:T(8,128)(2,1)S(1)}, u32[]{:S(2)}, u32[]{:S(2)}) collective-permute-start(bf16[384,256]{1,0:T(8,128)(2,1)S(1)} %get-tuple-element.32), channel_id=1, source_target_pairs={{4,0},{10,2},{12,4},{2,6},{0,8},{18,10},{20,12},{6,14},{8,16},{26,... | collective-permute-start | bytes 589832 | tf_op jit(solution)/shard_map/ppermute | solution.py:355
  28.6 34.7 %copy-start.12 = (bf16[384,256]{1,0:T(8,128)(2,1)}, bf16[384,256]{1,0:T(8,128)(2,1)S(1)}, u32[]{:S(2)}) copy-start(bf16[384,256]{1,0:T(8,128)(2,1)S(1)} %collective-permute-done.1.refs_9_) | copy-start | bytes 589828
  28.6 6.3 %collective-permute-start.5 = (bf16[384,256]{1,0:T(8,128)(2,1)S(1)}, bf16[384,256]{1,0:T(8,128)(2,1)S(1)}, u32[]{:S(2)}, u32[]{:S(2)}) collective-permute-start(bf16[384,256]{1,0:T(8,128)(2,1)S(1)} %collective-permute-done.1.refs_9_), channel_id=1, source_target_pairs={{4,0},{10,2},{12,4},{2,6},{0,8},{18,10},{20,12},{6,14},{8,16},{26,... | collective-permute-start | bytes 589832 | tf_op jit(solution)/shard_map/ppermute | solution.py:354
  31.7 3.2 %collective-permute-start.3 = (bf16[384,256]{1,0:T(8,128)(2,1)S(1)}, bf16[384,256]{1,0:T(8,128)(2,1)S(1)}, u32[]{:S(2)}, u32[]{:S(2)}) collective-permute-start(bf16[384,256]{1,0:T(8,128)(2,1)S(1)} %collective-permute-done.1.refs_9_), channel_id=1, source_target_pairs={{0,2},{2,0},{4,6},{6,4},{8,10},{10,8},{12,14},{14,12},{16,18},{18,... | collective-permute-start | bytes 589832 | tf_op jit(solution)/shard_map/ppermute | solution.py:305
  31.7 31.5 %copy-start.13 = (bf16[384,256]{1,0:T(8,128)(2,1)}, bf16[384,256]{1,0:T(8,128)(2,1)S(1)}, u32[]{:S(2)}) copy-start(bf16[384,256]{1,0:T(8,128)(2,1)S(1)} %collective-permute-done.2.refs_10_) | copy-start | bytes 589828
  31.7 5.9 %collective-permute-start.6 = (bf16[384,256]{1,0:T(8,128)(2,1)S(1)}, bf16[384,256]{1,0:T(8,128)(2,1)S(1)}, u32[]{:S(2)}, u32[]{:S(2)}) collective-permute-start(bf16[384,256]{1,0:T(8,128)(2,1)S(1)} %collective-permute-done.2.refs_10_), channel_id=1, source_target_pairs={{4,0},{10,2},{12,4},{2,6},{0,8},{18,10},{20,12},{6,14},{8,16},{26,... | collective-permute-start | bytes 589832 | tf_op jit(solution)/shard_map/ppermute | solution.py:355
  34.9 28.4 %copy-start.14 = (bf16[384,256]{1,0:T(8,128)(2,1)}, bf16[384,256]{1,0:T(8,128)(2,1)S(1)}, u32[]{:S(2)}) copy-start(bf16[384,256]{1,0:T(8,128)(2,1)S(1)} %collective-permute-done.5.refs_13_) | copy-start | bytes 589828
  34.9 2.6 %collective-permute-start.4 = (bf16[384,256]{1,0:T(8,128)(2,1)S(1)}, bf16[384,256]{1,0:T(8,128)(2,1)S(1)}, u32[]{:S(2)}, u32[]{:S(2)}) collective-permute-start(bf16[384,256]{1,0:T(8,128)(2,1)S(1)} %collective-permute-done.2.refs_10_), channel_id=1, source_target_pairs={{0,2},{2,0},{4,6},{6,4},{8,10},{10,8},{12,14},{14,12},{16,18},{18,... | collective-permute-start | bytes 589832 | tf_op jit(solution)/shard_map/ppermute | solution.py:305
  34.9 28.4 %copy-start.15 = (bf16[384,256]{1,0:T(8,128)(2,1)}, bf16[384,256]{1,0:T(8,128)(2,1)S(1)}, u32[]{:S(2)}) copy-start(bf16[384,256]{1,0:T(8,128)(2,1)S(1)} %collective-permute-done.3.refs_11_) | copy-start | bytes 589828
  34.9 5.7 %collective-permute-start.9 = (bf16[384,256]{1,0:T(8,128)(2,1)S(1)}, bf16[384,256]{1,0:T(8,128)(2,1)S(1)}, u32[]{:S(2)}, u32[]{:S(2)}) collective-permute-start(bf16[384,256]{1,0:T(8,128)(2,1)S(1)} %collective-permute-done.5.refs_13_), channel_id=1, source_target_pairs={{4,0},{10,2},{12,4},{2,6},{0,8},{18,10},{20,12},{6,14},{8,16},{26,... | collective-permute-start | bytes 589832 | tf_op jit(solution)/shard_map/ppermute | solution.py:354
  37.5 25.8 %copy-start.17 = (bf16[384,256]{1,0:T(8,128)(2,1)}, bf16[384,256]{1,0:T(8,128)(2,1)S(1)}, u32[]{:S(2)}) copy-start(bf16[384,256]{1,0:T(8,128)(2,1)S(1)} %collective-permute-done.4.refs_12_) | copy-start | bytes 589828
  37.5 10.8 %collective-permute-start.7 = (bf16[384,256]{1,0:T(8,128)(2,1)S(1)}, bf16[384,256]{1,0:T(8,128)(2,1)S(1)}, u32[]{:S(2)}, u32[]{:S(2)}) collective-permute-start(bf16[384,256]{1,0:T(8,128)(2,1)S(1)} %collective-permute-done.5.refs_13_), channel_id=1, source_target_pairs={{0,2},{2,0},{4,6},{6,4},{8,10},{10,8},{12,14},{14,12},{16,18},{18,... | collective-permute-start | bytes 589832 | tf_op jit(solution)/shard_map/ppermute | solution.py:305
  37.6 25.7 %copy-start.16 = (bf16[384,256]{1,0:T(8,128)(2,1)}, bf16[384,256]{1,0:T(8,128)(2,1)S(1)}, u32[]{:S(2)}) copy-start(bf16[384,256]{1,0:T(8,128)(2,1)S(1)} %collective-permute-done.6.refs_14_) | copy-start | bytes 589828
  37.6 5.9 %collective-permute-start.10 = (bf16[384,256]{1,0:T(8,128)(2,1)S(1)}, bf16[384,256]{1,0:T(8,128)(2,1)S(1)}, u32[]{:S(2)}, u32[]{:S(2)}) collective-permute-start(bf16[384,256]{1,0:T(8,128)(2,1)S(1)} %collective-permute-done.6.refs_14_), channel_id=1, source_target_pairs={{4,0},{10,2},{12,4},{2,6},{0,8},{18,10},{20,12},{6,14},{8,16},{26,... | collective-permute-start | bytes 589832 | tf_op jit(solution)/shard_map/ppermute | solution.py:355
  40.7 22.6 %copy-start.9 = (bf16[384,256]{1,0:T(8,128)(2,1)}, bf16[384,256]{1,0:T(8,128)(2,1)S(1)}, u32[]{:S(2)}) copy-start(bf16[384,256]{1,0:T(8,128)(2,1)S(1)} %collective-permute-done.9.refs_17_) | copy-start | bytes 589828
  40.7 8.3 %collective-permute-start.8 = (bf16[384,256]{1,0:T(8,128)(2,1)S(1)}, bf16[384,256]{1,0:T(8,128)(2,1)S(1)}, u32[]{:S(2)}, u32[]{:S(2)}) collective-permute-start(bf16[384,256]{1,0:T(8,128)(2,1)S(1)} %collective-permute-done.6.refs_14_), channel_id=1, source_target_pairs={{0,2},{2,0},{4,6},{6,4},{8,10},{10,8},{12,14},{14,12},{16,18},{18,... | collective-permute-start | bytes 589832 | tf_op jit(solution)/shard_map/ppermute | solution.py:305
  43.5 19.8 %copy-start.10 = (bf16[384,256]{1,0:T(8,128)(2,1)}, bf16[384,256]{1,0:T(8,128)(2,1)S(1)}, u32[]{:S(2)}) copy-start(bf16[384,256]{1,0:T(8,128)(2,1)S(1)} %collective-permute-done.10.refs_18_) | copy-start | bytes 589828
  43.5 7.2 %collective-permute-start.13 = (bf16[384,256]{1,0:T(8,128)(2,1)S(1)}, bf16[384,256]{1,0:T(8,128)(2,1)S(1)}, u32[]{:S(2)}, u32[]{:S(2)}) collective-permute-start(bf16[384,256]{1,0:T(8,128)(2,1)S(1)} %broadcast_select_fusion), channel_id=1, source_target_pairs={{4,0},{10,2},{12,4},{2,6},{0,8},{18,10},{20,12},{6,14},{8,16},{26,... | collective-permute-start | bytes 589832 | tf_op jit(solution)/shard_map/ppermute | solution.py:366
  46.4 1.3 %copy-start = (f8e4m3fn[256,8192]{1,0:T(32,128)(4,1)}, f8e4m3fn[256,8192]{1,0:T(32,128)(4,1)S(1)}, u32[]{:S(2)}) copy-start(f8e4m3fn[256,8192]{1,0:T(32,128)(4,1)S(1)} %get-tuple-element.20.refs_23_) | copy-start | bytes 6291460
  47.8 0.5 copy-start.7
  48.3 15.0 %copy-start.18 = (bf16[384,256]{1,0:T(8,128)(2,1)}, bf16[384,256]{1,0:T(8,128)(2,1)S(1)}, u32[]{:S(2)}) copy-start(bf16[384,256]{1,0:T(8,128)(2,1)S(1)} %collective-permute-done.7.refs_15_) | copy-start | bytes 589828
  48.3 1.5 %collective-permute-start.11 = (bf16[384,256]{1,0:T(8,128)(2,1)S(1)}, bf16[384,256]{1,0:T(8,128)(2,1)S(1)}, u32[]{:S(2)}, u32[]{:S(2)}) collective-permute-start(bf16[384,256]{1,0:T(8,128)(2,1)S(1)} %collective-permute-done.9.refs_17_), channel_id=1, source_target_pairs={{0,2},{2,0},{4,6},{6,4},{8,10},{10,8},{12,14},{14,12},{16,18},{18,... | collective-permute-start | bytes 589832 | tf_op jit(solution)/shard_map/ppermute | solution.py:305
  49.0 14.3 %copy-start.19 = (bf16[384,256]{1,0:T(8,128)(2,1)}, bf16[384,256]{1,0:T(8,128)(2,1)S(1)}, u32[]{:S(2)}) copy-start(bf16[384,256]{1,0:T(8,128)(2,1)S(1)} %collective-permute-done.8.refs_16_) | copy-start | bytes 589828
  49.0 8.3 %collective-permute-start.12 = (bf16[384,256]{1,0:T(8,128)(2,1)S(1)}, bf16[384,256]{1,0:T(8,128)(2,1)S(1)}, u32[]{:S(2)}, u32[]{:S(2)}) collective-permute-start(bf16[384,256]{1,0:T(8,128)(2,1)S(1)} %collective-permute-done.10.refs_18_), channel_id=1, source_target_pairs={{0,2},{2,0},{4,6},{6,4},{8,10},{10,8},{12,14},{14,12},{16,18},{18,... | collective-permute-start | bytes 589832 | tf_op jit(solution)/shard_map/ppermute | solution.py:305
  49.5 13.8 %copy-start.11 = (bf16[5,2,48,256]{3,2,1,0:T(8,128)(2,1)}, bf16[5,2,48,256]{3,2,1,0:T(8,128)(2,1)S(1)}, u32[]{:S(2)}) copy-start(bf16[5,2,48,256]{3,2,1,0:T(8,128)(2,1)S(1)} %fusion.4.refs_0_) | copy-start | bytes 737284
  49.8 13.6 %copy-start.21 = (bf16[384,256]{1,0:T(8,128)(2,1)}, bf16[384,256]{1,0:T(8,128)(2,1)S(1)}, u32[]{:S(2)}) copy-start(bf16[384,256]{1,0:T(8,128)(2,1)S(1)} %collective-permute-done.11.refs_19_) | copy-start | bytes 589828
  49.8 9.6 %collective-permute-start.18 = (bf16[1,2,48,256]{3,2,1,0:T(8,128)(2,1)S(1)}, bf16[1,2,48,256]{3,2,1,0:T(8,128)(2,1)S(1)}, u32[]{:S(2)}, u32[]{:S(2)}) collective-permute-start(bf16[1,2,48,256]{3,2,1,0:T(8,128)(2,1)S(1)} %maximum_bitcast_fusion.10), channel_id=1, source_target_pairs={{1,28},{3,30},{5,24},{7,26},{9,20},{11,22},{13,16},{15,18},{16,13}... | collective-permute-start | bytes 147464 | tf_op jit(solution)/shard_map/ppermute | solution.py:348
  50.7 12.7 %copy-start.20 = (bf16[384,256]{1,0:T(8,128)(2,1)}, bf16[384,256]{1,0:T(8,128)(2,1)S(1)}, u32[]{:S(2)}) copy-start(bf16[384,256]{1,0:T(8,128)(2,1)S(1)} %collective-permute-done.13.refs_21_) | copy-start | bytes 589828
  50.7 12.6 %collective-permute-start.15 = (bf16[5,2,48,256]{3,2,1,0:T(8,128)(2,1)S(1)}, bf16[5,2,48,256]{3,2,1,0:T(8,128)(2,1)S(1)}, u32[]{:S(2)}, u32[]{:S(2)}) collective-permute-start(bf16[5,2,48,256]{3,2,1,0:T(8,128)(2,1)S(1)} %fusion.4.refs_0_), channel_id=1, source_target_pairs={{0,1},{1,0},{2,3},{3,2},{4,5},{5,4},{6,7},{7,6},{8,9},{9,8},{10,11... | collective-permute-start | bytes 737288 | tf_op jit(solution)/shard_map/ppermute | solution.py:334
  57.3 6.1 %copy-start.22 = (bf16[384,256]{1,0:T(8,128)(2,1)}, bf16[384,256]{1,0:T(8,128)(2,1)S(1)}, u32[]{:S(2)}) copy-start(bf16[384,256]{1,0:T(8,128)(2,1)S(1)} %collective-permute-done.12.refs_20_) | copy-start | bytes 589828
  57.3 1.4 %collective-permute-start.14 = (bf16[384,256]{1,0:T(8,128)(2,1)S(1)}, bf16[384,256]{1,0:T(8,128)(2,1)S(1)}, u32[]{:S(2)}, u32[]{:S(2)}) collective-permute-start(bf16[384,256]{1,0:T(8,128)(2,1)S(1)} %collective-permute-done.13.refs_21_), channel_id=1, source_target_pairs={{0,2},{2,0},{4,6},{6,4},{8,10},{10,8},{12,14},{14,12},{16,18},{18,... | collective-permute-start | bytes 589832 | tf_op jit(solution)/shard_map/ppermute | solution.py:305
  58.7 4.7 %copy-start.23 = (bf16[384,256]{1,0:T(8,128)(2,1)}, bf16[384,256]{1,0:T(8,128)(2,1)S(1)}, u32[]{:S(2)}) copy-start(bf16[384,256]{1,0:T(8,128)(2,1)S(1)} %collective-permute-done.14.refs_22_) | copy-start | bytes 589828
  59.4 4.0 %copy-start.25 = (bf16[1,2,48,256]{3,2,1,0:T(8,128)(2,1)}, bf16[1,2,48,256]{3,2,1,0:T(8,128)(2,1)S(1)}, u32[]{:S(2)}) copy-start(bf16[1,2,48,256]{3,2,1,0:T(8,128)(2,1)S(1)} %collective-permute-done.16.refs_5_) | copy-start | bytes 147460
  59.4 4.0 %copy-start.26 = (bf16[1,2,48,256]{3,2,1,0:T(8,128)(2,1)}, bf16[1,2,48,256]{3,2,1,0:T(8,128)(2,1)S(1)}, u32[]{:S(2)}) copy-start(bf16[1,2,48,256]{3,2,1,0:T(8,128)(2,1)S(1)} %collective-permute-done.17.refs_6_) | copy-start | bytes 147460
  59.5 4.0 %copy-start.27 = (bf16[1,2,48,256]{3,2,1,0:T(8,128)(2,1)}, bf16[1,2,48,256]{3,2,1,0:T(8,128)(2,1)S(1)}, u32[]{:S(2)}) copy-start(bf16[1,2,48,256]{3,2,1,0:T(8,128)(2,1)S(1)} %collective-permute-done.18.refs_7_) | copy-start | bytes 147460
  63.3 0.7 copy-start.24

commit v5 on v4

--- a/solution.py
+++ b/solution.py
@@ -21,7 +21,14 @@
     return centered * lax.rsqrt(variance + EPSILON) * gain + bias
 
 
-def project_body(core_ref, x_ref, gain_ref, bias_ref, weight_ref, pbias_ref, out_ref):
+def project_body(core_ref, *refs):
+    x_ref, gain_ref, bias_ref, weight_ref, pbias_ref = refs[6:11]
+    out_ref, sems = refs[5], refs[11]
+    copies = [pltpu.make_async_copy(refs[i], refs[6 + i], sems.at[i]) for i in range(5)]
+    for copy in copies:
+        copy.start()
+    for copy in copies:
+        copy.wait()
     local, _, _ = x_ref.shape
     width = weight_ref.shape[0]
     group = 2 * local
@@ -51,16 +58,17 @@
 def project(core, x, gain, bias, weight, pbias):
     local, residues, _ = x.shape
     lanes = weight.shape[0] * local
-    out = jax.ShapeDtypeStruct((2, residues, lanes), BF16)
+    operands = (x, gain, bias, weight, pbias)
     return pl.pallas_call(
         project_body,
-        grid=(1,),
         in_specs=[pl.BlockSpec(memory_space=pltpu.SMEM)]
-        + [whole(a) for a in (x, gain, bias, weight, pbias)],
-        out_specs=whole(out),
-        out_shape=out,
+        + [pl.BlockSpec(memory_space=pltpu.HBM)] * 5,
+        out_specs=pl.BlockSpec(memory_space=pltpu.VMEM),
+        out_shape=jax.ShapeDtypeStruct((2, residues, lanes), BF16),
+        scratch_shapes=[pltpu.VMEM(a.shape, a.dtype) for a in operands]
+        + [pltpu.SemaphoreType.DMA((5,))],
         compiler_params=pltpu.CompilerParams(vmem_limit_bytes=32 << 20),
-    )(core, x, gain, bias, weight, pbias)
+    )(core, *operands)
 
 
 def power_of_two(largest):
@@ -73,7 +81,7 @@
     return scale, inverse
 
 
-def split_weight_body(total, w_ref, w8_ref, undo_ref, scr):
+def split_weight(total, w_ref, w8_ref, undo_ref, scr):
     half = w8_ref.shape[0] // 8
     zc = w_ref.shape[1]
     scr[...] = w_ref[...].astype(F32)
@@ -97,23 +105,6 @@
             w8_ref[row + half : row + 2 * half, lanes] = high
             w8_ref[row + 2 * half : row + 3 * half, lanes] = low
             w8_ref[row + 3 * half : row + 4 * half, lanes] = low
-
-
-def split_weight(w_out, half, total):
-    zc = w_out.shape[1]
-    outs = [
-        jax.ShapeDtypeStruct((8 * half, 2 * half * zc), F8),
-        jax.ShapeDtypeStruct((1, zc), F32),
-    ]
-    return pl.pallas_call(
-        functools.partial(split_weight_body, total),
-        grid=(1,),
-        in_specs=[whole(w_out)],
-        out_specs=[whole(a) for a in outs],
-        out_shape=outs,
-        scratch_shapes=[pltpu.VMEM(w_out.shape, F32)],
-        compiler_params=pltpu.CompilerParams(vmem_limit_bytes=32 << 20),
-    )(w_out)
 
 
 def prepare_rows(chips, group, x_scr, undo_ref, y_scr, lhs_scr, undo_scr):
@@ -153,13 +144,13 @@
 
 
 def pair_body(chips, here, group, row_parts, place_ref, *refs):
-    here_refs, there_refs = refs[:row_parts], refs[row_parts : 2 * row_parts]
-    refs = refs[2 * row_parts :]
+    there_refs = refs[:row_parts]
+    refs = refs[row_parts:]
     own_ref, *col_refs = refs[: chips * 2 - 1]
-    (w_ref, undo_ref, b_out_ref, gain_ref, bias_ref, w_up_ref, b_up_ref, w_down_ref, b_down_ref) = (
-        refs[chips * 2 - 1 : chips * 2 + 8]
+    (w_out_ref, b_out_ref, gain_ref, bias_ref, w_up_ref, b_up_ref, w_down_ref, b_down_ref) = (
+        refs[chips * 2 - 1 : chips * 2 + 7]
     )
-    out_ref, col_scr, x_scr, y_scr, lhs_scr, undo_scr, t_scr, z_scr = refs[chips * 2 + 8 :]
+    out_ref, col_scr, x_scr, y_scr, lhs_scr, undo_scr, t_scr, z_scr, w_ref, undo_ref, w_scr = refs[chips * 2 + 7 :]
     part = own_ref.shape[2]
     zc = out_ref.shape[2]
     half = part // group
@@ -185,20 +176,25 @@
             col_scr[0, :, far] = far_there[...]
             col_scr[1, :, far] = far_here[...]
 
-        def take(row_refs):
-            blocks = [(r, q) for r in row_refs for q in range(r.shape[0])]
+        row_length = x_scr.shape[1] // chips
+
+        @pl.when(place_ref[1] != 0)
+        def _():
+            first = pl.multiple_of(place_ref[2] * row_length, row_length)
+            for side in range(2):
+                for q in range(chips):
+                    x_scr[side, q * row_length : (q + 1) * row_length, :] = col_scr[
+                        side, pl.ds(first, row_length), q * part : (q + 1) * part
+                    ]
+
+        @pl.when(place_ref[1] == 0)
+        def _():
+            blocks = [(r, q) for r in there_refs for q in range(r.shape[0])]
             for i, (r, q) in enumerate(blocks):
                 for side in range(2):
-                    x_scr[side, i * r.shape[2] : (i + 1) * r.shape[2], :] = r[q, side]
-
-        @pl.when(place_ref[1] != 0)
-        def _():
-            take(here_refs)
-
-        @pl.when(place_ref[1] == 0)
-        def _():
-            take(there_refs)
-
+                    x_scr[side, i * row_length : (i + 1) * row_length, :] = r[q, side]
+
+        split_weight(chips * group, w_out_ref, w_ref, undo_ref, w_scr)
         prepare_rows(chips, group, x_scr, undo_ref, y_scr, lhs_scr, undo_scr)
 
     rows = here * group
@@ -232,21 +228,21 @@
         out_ref[g] = (pair + update + b_down_ref[...]).astype(BF16)
 
 
-def pair_kernel(place, group, rows_here, rows_there, cols, rest):
+def pair_kernel(place, group, rows, cols, rest):
     own = cols[0]
     _, column_length, part = own.shape
     chips = (len(cols) + 1) // 2
-    row_length = rows_here[0].shape[2]
-    zc = rest[2].shape[1]
+    row_length = rows[0].shape[2]
+    zc = rest[1].shape[1]
     here = math.gcd(row_length, 8)
     depth = chips * part
     lanes = 4 * part // group
 
     return pl.pallas_call(
-        functools.partial(pair_body, chips, here, group, len(rows_here)),
+        functools.partial(pair_body, chips, here, group, len(rows)),
         grid=(row_length // here,),
         in_specs=[pl.BlockSpec(memory_space=pltpu.SMEM)]
-        + [whole(a) for a in (*rows_here, *rows_there, *cols, *rest)],
+        + [whole(a) for a in (*rows, *cols, *rest)],
         out_specs=pl.BlockSpec((here, column_length, zc), lambda i: (i, 0, 0)),
         out_shape=jax.ShapeDtypeStruct((row_length, column_length, zc), BF16),
         scratch_shapes=[
@@ -257,20 +253,23 @@
             pltpu.VMEM((2, row_length, zc), F32),
             pltpu.VMEM((2, here // 2, depth, 2 * zc), BF16),
             pltpu.VMEM((2, here // 2, column_length, 2 * zc), F32),
+            pltpu.VMEM((2 * lanes, 2 * part // group * zc), F8),
+            pltpu.VMEM((1, zc), F32),
+            pltpu.VMEM(rest[0].shape, F32),
         ],
         compiler_params=pltpu.CompilerParams(vmem_limit_bytes=56 << 20),
-    )(place, *rows_here, *rows_there, *cols, *rest)
+    )(place, *rows, *cols, *rest)
 
 
 def ring_order(chips):
     return list(range(0, chips, 2)) + list(range(chips - 1, 0, -2))
 
 
-def ring_source(chips, steps):
+def ring_source(chips):
     order = ring_order(chips)
     place = {q: i for i, q in enumerate(order)}
     return [
-        2 * order[(place[r // 2] + (steps if r % 2 else -steps)) % chips] + r % 2
+        2 * order[(place[r // 2] + (1 if r % 2 else -1)) % chips] + r % 2
         for r in range(2 * chips)
     ]
 
@@ -304,7 +303,7 @@
     def swap(a):
         return lax.ppermute(a, "row", [(r, r ^ 1) for r in range(row_count)])
 
-    ring = [(src, r) for r, src in enumerate(ring_source(chips, 1))]
+    ring = [(src, r) for r, src in enumerate(ring_source(chips))]
 
     mine = project(
         core.reshape(1),
@@ -320,73 +319,55 @@
     start = (row_index % per_col) * row_length
     source = row_index // per_col
 
-    def cut(pieces, first):
-        return jnp.stack(
-            [
-                jnp.stack([lax.dynamic_slice_in_dim(c, first, row_length, 0) for c in pair])
-                for pair in pieces
-            ]
-        )
-
-    def exchange(pieces):
-        block = cut(pieces, start)
-        if col_count == 2:
-            return block, lax.ppermute(block, "col", [(0, 1), (1, 0)])
-        block = lax.dynamic_index_in_dim(lax.all_gather(block, "col"), source, 0, False)
-        return block, block
+    def cut(pair, first, count):
+        return jnp.stack([lax.dynamic_slice_in_dim(c, first, count, 0) for c in pair])
+
+    def across(block):
+        return lax.ppermute(block, "col", [(0, 1), (1, 0)])
 
     right, left = own[0], own[1]
     cols = [own]
-    early = [(right, left)]
     steps = chips // 2 - 1
-
-    def direct(hops):
-        sources = ring_source(chips, hops)
-        targets = [sources.index(r) for r in range(row_count)]
-        first = jnp.array([t % per_col * row_length for t in targets], jnp.int32)[row_index]
-        pairs = [(2 * r + t // per_col, 2 * t + 1 - t // per_col) for r, t in enumerate(targets)]
-        return lax.ppermute(cut([(right, left)], first), ("row", "col"), pairs)
-
-    if col_count == 2:
-        straight = [direct(steps), direct(-steps), direct(steps + 1)]
-    rows = []
+    two = col_count == 2
+    if two:
+        targets = [row_count - 2 - r + 2 * (r % 2) for r in range(row_count)]
+        first = (row_count - 2 - row_index + 2 * core) % per_col * row_length
+        far_rows = lax.ppermute(
+            lax.dynamic_slice_in_dim(own, first, row_length, 1),
+            ("row", "col"),
+            [(2 * r + t // per_col, 2 * t + 1 - t // per_col) for r, t in enumerate(targets)],
+        )
+    blocks = [cut((right, left), start, row_length)]
     for d in range(steps):
         right = lax.ppermute(right, "row", ring)
         left = lax.ppermute(left, "row", ring)
-        pieces = [(right, left), (swap(right), swap(left))]
-        for pair in pieces:
-            cols.extend(pair)
-        if d < steps - 1:
-            early.extend(pieces)
-        if d == steps - 2:
-            rows.append(exchange(early))
-        if d == steps - 1:
-            params = (w_out, b_out, pair_gain, pair_bias, w_up, b_up, w_down, b_down)
-            *params, right, left = lax.optimization_barrier((*params, right, left))
+        other = (swap(right), swap(left))
+        cols.extend([right, left, *other])
+        if d < steps - 1 or not two:
+            blocks.extend([cut(pair, start, row_length) for pair in ((right, left), other)])
+        if d == steps - 2 and two:
+            rows = [across(jnp.stack(blocks))]
     far = lax.ppermute(jnp.where(core == 0, right, left), "row", ring)
+    if two:
+        both = across(cut((right, left), start - core * row_length, 2 * row_length))
+        far, both = lax.optimization_barrier((far, both))
+        kept = lax.dynamic_slice_in_dim(both, core * row_length, row_length, 1)
+        given = lax.dynamic_slice_in_dim(both, (1 - core) * row_length, row_length, 1)
+        rows.extend([kept[None], swap(given)[None], far_rows[None]])
     far_other = swap(far)
     cols.extend([far, far_other])
-    a = lax.dynamic_slice_in_dim(far, start, row_length, 0)
-    b = lax.dynamic_slice_in_dim(far_other, start, row_length, 0)
-    far_pair = (jnp.where(core == 0, a, b), jnp.where(core == 0, b, a))
-    pieces = pieces + [far_pair]
-    last = cut(pieces[:2], start)
-    if col_count == 2:
-        rows.extend([(last[:1], straight[0]), (last[1:], straight[1])])
-        rows.append((jnp.stack(far_pair)[None], straight[2]))
-    else:
-        last = jnp.concatenate([last, jnp.stack(far_pair)[None]])
-        block = lax.dynamic_index_in_dim(lax.all_gather(last, "col"), source, 0, False)
-        rows.append((block, block))
-
-    group = 2 * local
-    w_out, b_out, pair_gain, pair_bias, w_up, b_up, w_down, b_down = params
-    w8, undo = split_weight(w_out, half, group * chips)
-    rest = (w8, undo, b_out[None], pair_gain[None], pair_bias[None], w_up, b_up[None], w_down)
-    place = jnp.stack([core, (source == col_index).astype(core.dtype)])
-    return pair_kernel(
-        place, group, [r[0] for r in rows], [r[1] for r in rows], cols, rest + (b_down[None],)
-    )
+    is_here = (source == col_index).astype(core.dtype)
+    if not two:
+        a = lax.dynamic_slice_in_dim(far, start, row_length, 0)
+        b = lax.dynamic_slice_in_dim(far_other, start, row_length, 0)
+        blocks.append(jnp.stack([jnp.where(core == 0, a, b), jnp.where(core == 0, b, a)]))
+        gathered = lax.all_gather(jnp.stack(blocks), "col")
+        rows = [lax.dynamic_index_in_dim(gathered, source, 0, False)]
+        is_here = jnp.zeros_like(is_here)
+
+    place = jnp.stack([core, is_here, row_index % per_col])
+    rest = (w_out, b_out[None], pair_gain[None], pair_bias[None], w_up, b_up[None], w_down)
+    return pair_kernel(place, 2 * local, rows, cols, rest + (b_down[None],))
 
 
 def solution(mesh):

time: 110 us -> 87.7 us (0.80)
  the two profiles are of different devices: /device:TPU:0 before, /device:TPU:3 now
where the time goes in v5:
time: 87.7 us; the launch traced here: 87.4 us
  Pallas kernels  46.4 us (53%)
  starting transfers between devices  27.7 us (32%)
  waiting for transfers between devices  6.68 us (8%)
  local copies, waits for them, and re-layouts  5.36 us (6%)
    pallas_call x1, Pallas kernels, pair_kernel(): pl.pallas_call(functools.partial(pair_body, chips, here, group, len(rows)...  45.1 us
    ppermute x9, starting transfers between devices, swap(): return lax.ppermute(a, 'row', [(r, r ^ 1) for r in range(row_count)])  13.8 us
    ppermute x1, starting transfers between devices, shards(): lax.ppermute(lax.dynamic_slice_in_dim(own, first, row_length, 1), ('row',...  6.33 us
    unnamed x46, local copies, waits for them, and re-layouts  4.6 us
    ppermute x3, starting transfers between devices, shards(): right = lax.ppermute(right, 'row', ring)  3.65 us
    ppermute x3, waiting for transfers between devices, shards(): left = lax.ppermute(left, 'row', ring)  2.82 us
    ppermute x3, waiting for transfers between devices, shards(): right = lax.ppermute(right, 'row', ring)  2.27 us
    ppermute x3, starting transfers between devices, shards(): left = lax.ppermute(left, 'row', ring)  2.05 us
  transfers between devices with their start and end apart: 19, of which 4 were waited for; matrix products, arithmetic and copies ran while one was open for 2% of the time, Pallas kernels for 0%

profile of v5, /device:TPU:3, one launch (start us, length us, event | category | flops | bytes accessed | tf_op | source)
XLA Modules:
  0.0 87.4 jit_solution(2905696430130094559)
XLA Ops:
  0.0 1.1 %copy-done = bf16[4,384,256]{2,1,0:T(8,128)(2,1)S(1)} copy-done((bf16[4,384,256]{2,1,0:T(8,128)(2,1)S(1)}, bf16[4,384,256]{2,1,0:T(8,128)(2,1)}, u32[]{:S(2)}) %copy-start) | copy-done | bytes 786456
  1.1 0.8 copy-done.1
  1.9 0.7 copy-done.2
  2.6 0.7 copy-done.3
  3.3 0.7 copy-done.4
  3.9 1.3 %shard_map.127 = bf16[2,384,256]{2,1,0:T(8,128)(2,1)S(1)} custom-call(s32[1]{0:T(128)} %bitcast.core_ref, bf16[4,384,256]{2,1,0:T(8,128)(2,1)S(1)} %copy-done, f32[1,256]{1,0:T(1,128)S(1)} %bitcast.61, f32[1,256]{1,0:T(1,128)S(1)} %bitcast.62, bf16[64,256]{1,0:T(8,128)(2,1)S(1)} %bitcast.60, f32[1,64]{1,0:T(1,128)S(1)} %bitcast.63), custom_call_target="tpu_custom_call" | custom-call | tf_op jit(solution)/shard_map/pallas_call | solution.py:62
  5.3 0.7 collective-permute-start
  6.0 1.3 %collective-permute-done = bf16[2,384,256]{2,1,0:T(8,128)(2,1)S(1)} collective-permute-done((bf16[2,384,256]{2,1,0:T(8,128)(2,1)S(1)}, bf16[2,384,256]{2,1,0:T(8,128)(2,1)S(1)}, u32[]{:S(2)}, u32[]{:S(2)}) %collective-permute-start) | collective-permute-done | bytes 393248 | tf_op jit(solution)/shard_map/ppermute | solution.py:304
  7.3 0.1 add.45.refs_4_
  7.4 0.0 copy-start.5
  7.4 0.1 slice_bitcast_fusion.1
  7.5 1.3 %collective-permute-start.1 = (bf16[384,256]{1,0:T(8,128)(2,1)S(1)}, bf16[384,256]{1,0:T(8,128)(2,1)S(1)}, u32[]{:S(2)}, u32[]{:S(2)}) collective-permute-start(bf16[384,256]{1,0:T(8,128)(2,1)S(1)} %get-tuple-element.9), channel_id=1, source_target_pairs={{4,0},{10,2},{12,4},{2,6},{0,8},{18,10},{20,12},{6,14},{8,16},{26,... | collective-permute-start | bytes 589832 | tf_op jit(solution)/shard_map/ppermute | solution.py:342
  8.8 1.3 %collective-permute-start.2 = (bf16[384,256]{1,0:T(8,128)(2,1)S(1)}, bf16[384,256]{1,0:T(8,128)(2,1)S(1)}, u32[]{:S(2)}, u32[]{:S(2)}) collective-permute-start(bf16[384,256]{1,0:T(8,128)(2,1)S(1)} %get-tuple-element.10), channel_id=1, source_target_pairs={{4,0},{10,2},{12,4},{2,6},{0,8},{18,10},{20,12},{6,14},{8,16},{26,... | collective-permute-start | bytes 589832 | tf_op jit(solution)/shard_map/ppermute | solution.py:343
  10.1 2.3 %collective-permute-done.1.refs_5_ = bf16[384,256]{1,0:T(8,128)(2,1)S(1)} collective-permute-done((bf16[384,256]{1,0:T(8,128)(2,1)S(1)}, bf16[384,256]{1,0:T(8,128)(2,1)S(1)}, u32[]{:S(2)}, u32[]{:S(2)}) %collective-permute-start.1) | collective-permute-done | bytes 196640 | tf_op jit(solution)/shard_map/ppermute | solution.py:342
  12.4 1.2 %collective-permute-start.5 = (bf16[384,256]{1,0:T(8,128)(2,1)S(1)}, bf16[384,256]{1,0:T(8,128)(2,1)S(1)}, u32[]{:S(2)}, u32[]{:S(2)}) collective-permute-start(bf16[384,256]{1,0:T(8,128)(2,1)S(1)} %collective-permute-done.1.refs_5_), channel_id=1, source_target_pairs={{4,0},{10,2},{12,4},{2,6},{0,8},{18,10},{20,12},{6,14},{8,16},{26,... | collective-permute-start | bytes 589832 | tf_op jit(solution)/shard_map/ppermute | solution.py:342
  13.6 1.6 %collective-permute-start.3 = (bf16[384,256]{1,0:T(8,128)(2,1)S(1)}, bf16[384,256]{1,0:T(8,128)(2,1)S(1)}, u32[]{:S(2)}, u32[]{:S(2)}) collective-permute-start(bf16[384,256]{1,0:T(8,128)(2,1)S(1)} %collective-permute-done.1.refs_5_), channel_id=1, source_target_pairs={{0,2},{2,0},{4,6},{6,4},{8,10},{10,8},{12,14},{14,12},{16,18},{18,... | collective-permute-start | bytes 589832 | tf_op jit(solution)/shard_map/ppermute | solution.py:304
  15.2 0.0 collective-permute-done.2.refs_6_
  15.2 0.5 collective-permute-start.6
  15.7 1.6 %collective-permute-start.4 = (bf16[384,256]{1,0:T(8,128)(2,1)S(1)}, bf16[384,256]{1,0:T(8,128)(2,1)S(1)}, u32[]{:S(2)}, u32[]{:S(2)}) collective-permute-start(bf16[384,256]{1,0:T(8,128)(2,1)S(1)} %collective-permute-done.2.refs_6_), channel_id=1, source_target_pairs={{0,2},{2,0},{4,6},{6,4},{8,10},{10,8},{12,14},{14,12},{16,18},{18,... | collective-permute-start | bytes 589832 | tf_op jit(solution)/shard_map/ppermute | solution.py:304
  17.3 0.0 collective-permute-done.5.refs_9_
  17.3 0.0 copy-start.10
  17.3 1.1 %collective-permute-start.10 = (bf16[384,256]{1,0:T(8,128)(2,1)S(1)}, bf16[384,256]{1,0:T(8,128)(2,1)S(1)}, u32[]{:S(2)}, u32[]{:S(2)}) collective-permute-start(bf16[384,256]{1,0:T(8,128)(2,1)S(1)} %collective-permute-done.5.refs_9_), channel_id=1, source_target_pairs={{4,0},{10,2},{12,4},{2,6},{0,8},{18,10},{20,12},{6,14},{8,16},{26,... | collective-permute-start | bytes 589832 | tf_op jit(solution)/shard_map/ppermute | solution.py:342
  18.4 2.4 %collective-permute-start.7 = (bf16[384,256]{1,0:T(8,128)(2,1)S(1)}, bf16[384,256]{1,0:T(8,128)(2,1)S(1)}, u32[]{:S(2)}, u32[]{:S(2)}) collective-permute-start(bf16[384,256]{1,0:T(8,128)(2,1)S(1)} %collective-permute-done.5.refs_9_), channel_id=1, source_target_pairs={{0,2},{2,0},{4,6},{6,4},{8,10},{10,8},{12,14},{14,12},{16,18},{18,... | collective-permute-start | bytes 589832 | tf_op jit(solution)/shard_map/ppermute | solution.py:304
  20.9 0.0 collective-permute-done.3.refs_7_
  20.9 0.0 collective-permute-done.4.refs_8_
  20.9 0.0 copy-start.13
  20.9 0.0 collective-permute-done.6.refs_10_
  21.0 0.0 copy-start.12
  21.0 0.2 collective-permute-start.11
  21.2 1.8 %collective-permute-start.8 = (bf16[384,256]{1,0:T(8,128)(2,1)S(1)}, bf16[384,256]{1,0:T(8,128)(2,1)S(1)}, u32[]{:S(2)}, u32[]{:S(2)}) collective-permute-start(bf16[384,256]{1,0:T(8,128)(2,1)S(1)} %collective-permute-done.6.refs_10_), channel_id=1, source_target_pairs={{0,2},{2,0},{4,6},{6,4},{8,10},{10,8},{12,14},{14,12},{16,18},{18,... | collective-permute-start | bytes 589832 | tf_op jit(solution)/shard_map/ppermute | solution.py:304
  23.0 0.0 collective-permute-done.10.refs_13_
  23.0 0.0 copy-start.6
  23.0 2.8 %collective-permute-done.11.refs_14_ = bf16[384,256]{1,0:T(8,128)(2,1)S(1)} collective-permute-done((bf16[384,256]{1,0:T(8,128)(2,1)S(1)}, bf16[384,256]{1,0:T(8,128)(2,1)S(1)}, u32[]{:S(2)}, u32[]{:S(2)}) %collective-permute-start.11) | collective-permute-done | bytes 196640 | tf_op jit(solution)/shard_map/ppermute | solution.py:343
  25.9 0.3 collective-permute-start.13
  26.2 0.1 collective-permute-start.12
  26.3 0.0 collective-permute-done.7.refs_11_
  26.3 0.0 copy-start.14
  26.3 0.0 collective-permute-done.8.refs_12_
  26.3 0.0 copy-start.15
  26.4 1.4 %collective-permute-start.9 = (bf16[5,2,48,256]{3,2,1,0:T(8,128)(2,1)S(1)}, bf16[5,2,48,256]{3,2,1,0:T(8,128)(2,1)S(1)}, u32[]{:S(2)}, u32[]{:S(2)}) collective-permute-start(bf16[5,2,48,256]{3,2,1,0:T(8,128)(2,1)S(1)} %fusion.4), channel_id=1, source_target_pairs={{0,1},{1,0},{2,3},{3,2},{4,5},{5,4},{6,7},{7,6},{8,9},{9,8},{10,11... | collective-permute-start | bytes 737288 | tf_op jit(solution)/shard_map/ppermute | solution.py:326
  27.8 6.3 %collective-permute-start.15 = (bf16[2,48,256]{2,1,0:T(8,128)(2,1)S(1)}, bf16[2,48,256]{2,1,0:T(8,128)(2,1)S(1)}, u32[]{:S(2)}, u32[]{:S(2)}) collective-permute-start(bf16[2,48,256]{2,1,0:T(8,128)(2,1)S(1)} %constant_dynamic-slice_fusion), channel_id=1, source_target_pairs={{1,28},{3,30},{5,24},{7,26},{9,20},{11,22},{13,16},{15,18},{16,13}... | collective-permute-start | bytes 147464 | tf_op jit(solution)/shard_map/ppermute | solution.py:335
  34.1 2.4 %collective-permute-start.16 = (bf16[384,256]{1,0:T(8,128)(2,1)S(1)}, bf16[384,256]{1,0:T(8,128)(2,1)S(1)}, u32[]{:S(2)}, u32[]{:S(2)}) collective-permute-start(bf16[384,256]{1,0:T(8,128)(2,1)S(1)} %collective-permute-done.10.refs_13_), channel_id=1, source_target_pairs={{0,2},{2,0},{4,6},{6,4},{8,10},{10,8},{12,14},{14,12},{16,18},{18,... | collective-permute-start | bytes 589832 | tf_op jit(solution)/shard_map/ppermute | solution.py:304
  36.5 0.0 collective-permute-done.13
  36.5 0.1 collective-permute-start.17
  36.6 0.0 collective-permute-done.12.refs_17_
  36.6 0.4 collective-permute-start.18
  37.0 0.6 constant_dynamic-slice_fusion.1
  37.7 0.0 collective-permute-done.15
  37.7 2.9 %collective-permute-start.14 = (bf16[2,48,256]{2,1,0:T(8,128)(2,1)S(1)}, bf16[2,48,256]{2,1,0:T(8,128)(2,1)S(1)}, u32[]{:S(2)}, u32[]{:S(2)}) collective-permute-start(bf16[2,48,256]{2,1,0:T(8,128)(2,1)S(1)} %get-tuple-element.13), channel_id=1, source_target_pairs={{0,2},{2,0},{4,6},{6,4},{8,10},{10,8},{12,14},{14,12},{16,18},{18,... | collective-permute-start | bytes 147464 | tf_op jit(solution)/shard_map/ppermute | solution.py:304
  40.5 0.7 pad_add_fusion.place_ref
  41.2 0.0 collective-permute-done.16.refs_15_
  41.2 0.0 collective-permute-done.17.refs_16_
  41.2 0.0 copy-start.19
  41.2 0.2 collective-permute-done.14
  41.4 0.0 collective-permute-done.9.refs_0_
  41.4 0.0 collective-permute-done.18.refs_18_
  41.4 0.0 copy-start.20
  41.4 0.0 copy-done.5
  41.6 0.3 copy-done.18
  41.9 0.1 copy-done.19
  41.9 0.1 copy-done.22
  42.0 0.1 copy-done.16
  42.1 0.1 copy-done.20
  42.2 45.1 %shard_map.128 = bf16[48,384,128]{2,1,0:T(8,128)(2,1)} custom-call(s32[3]{0:T(128)} %pad_add_fusion.place_ref, bf16[5,2,48,256]{3,2,1,0:T(8,128)(2,1)} %copy-done.16, bf16[1,2,48,256]{3,2,1,0:T(8,128)(2,1)} %get-tuple-element.14.refs_1_, bf16[1,2,48,256]{3,2,1,0:T(8,128)(2,1)} %bitcast.65, bf16[1,2,48,256]{3,2,1,0:T(8,128)(2,1)} %bitcast.64, ...), custom_call_target="tpu_custom_call" | custom-call | tf_op jit(solution)/shard_map/pallas_call | solution.py:241
  (45 shorter events, 0.2 us)
Async XLA Ops:
  0.0 1.1 %copy-start = (bf16[4,384,256]{2,1,0:T(8,128)(2,1)S(1)}, bf16[4,384,256]{2,1,0:T(8,128)(2,1)}, u32[]{:S(2)}) copy-start(bf16[4,384,256]{2,1,0:T(8,128)(2,1)} %refs_0_.1) | copy-start | bytes 2359300
  1.1 0.8 copy-start.1
  1.9 0.7 copy-start.2
  2.6 0.7 copy-start.3
  3.3 0.7 copy-start.4
  5.3 2.1 %collective-permute-start = (bf16[2,384,256]{2,1,0:T(8,128)(2,1)S(1)}, bf16[2,384,256]{2,1,0:T(8,128)(2,1)S(1)}, u32[]{:S(2)}, u32[]{:S(2)}) collective-permute-start(bf16[2,384,256]{2,1,0:T(8,128)(2,1)S(1)} %shard_map.127), channel_id=1, source_target_pairs={{0,2},{2,0},{4,6},{6,4},{8,10},{10,8},{12,14},{14,12},{16,18},{18,... | collective-permute-start | bytes 1179656 | tf_op jit(solution)/shard_map/ppermute | solution.py:304
  7.4 34.0 %copy-start.5 = (bf16[2,384,256]{2,1,0:T(8,128)(2,1)}, bf16[2,384,256]{2,1,0:T(8,128)(2,1)S(1)}, u32[]{:S(2)}) copy-start(bf16[2,384,256]{2,1,0:T(8,128)(2,1)S(1)} %add.45.refs_4_) | copy-start | bytes 1179652
  7.5 4.9 %collective-permute-start.1 = (bf16[384,256]{1,0:T(8,128)(2,1)S(1)}, bf16[384,256]{1,0:T(8,128)(2,1)S(1)}, u32[]{:S(2)}, u32[]{:S(2)}) collective-permute-start(bf16[384,256]{1,0:T(8,128)(2,1)S(1)} %get-tuple-element.9), channel_id=1, source_target_pairs={{4,0},{10,2},{12,4},{2,6},{0,8},{18,10},{20,12},{6,14},{8,16},{26,... | collective-permute-start | bytes 589832 | tf_op jit(solution)/shard_map/ppermute | solution.py:342
  8.8 6.4 %collective-permute-start.2 = (bf16[384,256]{1,0:T(8,128)(2,1)S(1)}, bf16[384,256]{1,0:T(8,128)(2,1)S(1)}, u32[]{:S(2)}, u32[]{:S(2)}) collective-permute-start(bf16[384,256]{1,0:T(8,128)(2,1)S(1)} %get-tuple-element.10), channel_id=1, source_target_pairs={{4,0},{10,2},{12,4},{2,6},{0,8},{18,10},{20,12},{6,14},{8,16},{26,... | collective-permute-start | bytes 589832 | tf_op jit(solution)/shard_map/ppermute | solution.py:343
  12.4 29.1 %copy-start.8 = (bf16[384,256]{1,0:T(8,128)(2,1)}, bf16[384,256]{1,0:T(8,128)(2,1)S(1)}, u32[]{:S(2)}) copy-start(bf16[384,256]{1,0:T(8,128)(2,1)S(1)} %collective-permute-done.1.refs_5_) | copy-start | bytes 589828
  12.4 4.9 %collective-permute-start.5 = (bf16[384,256]{1,0:T(8,128)(2,1)S(1)}, bf16[384,256]{1,0:T(8,128)(2,1)S(1)}, u32[]{:S(2)}, u32[]{:S(2)}) collective-permute-start(bf16[384,256]{1,0:T(8,128)(2,1)S(1)} %collective-permute-done.1.refs_5_), channel_id=1, source_target_pairs={{4,0},{10,2},{12,4},{2,6},{0,8},{18,10},{20,12},{6,14},{8,16},{26,... | collective-permute-start | bytes 589832 | tf_op jit(solution)/shard_map/ppermute | solution.py:342
  13.6 7.2 %collective-permute-start.3 = (bf16[384,256]{1,0:T(8,128)(2,1)S(1)}, bf16[384,256]{1,0:T(8,128)(2,1)S(1)}, u32[]{:S(2)}, u32[]{:S(2)}) collective-permute-start(bf16[384,256]{1,0:T(8,128)(2,1)S(1)} %collective-permute-done.1.refs_5_), channel_id=1, source_target_pairs={{0,2},{2,0},{4,6},{6,4},{8,10},{10,8},{12,14},{14,12},{16,18},{18,... | collective-permute-start | bytes 589832 | tf_op jit(solution)/shard_map/ppermute | solution.py:304
  15.2 26.3 %copy-start.9 = (bf16[384,256]{1,0:T(8,128)(2,1)}, bf16[384,256]{1,0:T(8,128)(2,1)S(1)}, u32[]{:S(2)}) copy-start(bf16[384,256]{1,0:T(8,128)(2,1)S(1)} %collective-permute-done.2.refs_6_) | copy-start | bytes 589828
  15.2 5.7 %collective-permute-start.6 = (bf16[384,256]{1,0:T(8,128)(2,1)S(1)}, bf16[384,256]{1,0:T(8,128)(2,1)S(1)}, u32[]{:S(2)}, u32[]{:S(2)}) collective-permute-start(bf16[384,256]{1,0:T(8,128)(2,1)S(1)} %collective-permute-done.2.refs_6_), channel_id=1, source_target_pairs={{4,0},{10,2},{12,4},{2,6},{0,8},{18,10},{20,12},{6,14},{8,16},{26,... | collective-permute-start | bytes 589832 | tf_op jit(solution)/shard_map/ppermute | solution.py:343
  15.7 5.2 %collective-permute-start.4 = (bf16[384,256]{1,0:T(8,128)(2,1)S(1)}, bf16[384,256]{1,0:T(8,128)(2,1)S(1)}, u32[]{:S(2)}, u32[]{:S(2)}) collective-permute-start(bf16[384,256]{1,0:T(8,128)(2,1)S(1)} %collective-permute-done.2.refs_6_), channel_id=1, source_target_pairs={{0,2},{2,0},{4,6},{6,4},{8,10},{10,8},{12,14},{14,12},{16,18},{18,... | collective-permute-start | bytes 589832 | tf_op jit(solution)/shard_map/ppermute | solution.py:304
  17.3 24.2 %copy-start.10 = (bf16[384,256]{1,0:T(8,128)(2,1)}, bf16[384,256]{1,0:T(8,128)(2,1)S(1)}, u32[]{:S(2)}) copy-start(bf16[384,256]{1,0:T(8,128)(2,1)S(1)} %collective-permute-done.5.refs_9_) | copy-start | bytes 589828
  17.3 5.7 %collective-permute-start.10 = (bf16[384,256]{1,0:T(8,128)(2,1)S(1)}, bf16[384,256]{1,0:T(8,128)(2,1)S(1)}, u32[]{:S(2)}, u32[]{:S(2)}) collective-permute-start(bf16[384,256]{1,0:T(8,128)(2,1)S(1)} %collective-permute-done.5.refs_9_), channel_id=1, source_target_pairs={{4,0},{10,2},{12,4},{2,6},{0,8},{18,10},{20,12},{6,14},{8,16},{26,... | collective-permute-start | bytes 589832 | tf_op jit(solution)/shard_map/ppermute | solution.py:342
  18.4 7.8 %collective-permute-start.7 = (bf16[384,256]{1,0:T(8,128)(2,1)S(1)}, bf16[384,256]{1,0:T(8,128)(2,1)S(1)}, u32[]{:S(2)}, u32[]{:S(2)}) collective-permute-start(bf16[384,256]{1,0:T(8,128)(2,1)S(1)} %collective-permute-done.5.refs_9_), channel_id=1, source_target_pairs={{0,2},{2,0},{4,6},{6,4},{8,10},{10,8},{12,14},{14,12},{16,18},{18,... | collective-permute-start | bytes 589832 | tf_op jit(solution)/shard_map/ppermute | solution.py:304
  20.9 20.6 %copy-start.11 = (bf16[384,256]{1,0:T(8,128)(2,1)}, bf16[384,256]{1,0:T(8,128)(2,1)S(1)}, u32[]{:S(2)}) copy-start(bf16[384,256]{1,0:T(8,128)(2,1)S(1)} %collective-permute-done.3.refs_7_) | copy-start | bytes 589828
  20.9 20.6 %copy-start.13 = (bf16[384,256]{1,0:T(8,128)(2,1)}, bf16[384,256]{1,0:T(8,128)(2,1)S(1)}, u32[]{:S(2)}) copy-start(bf16[384,256]{1,0:T(8,128)(2,1)S(1)} %collective-permute-done.4.refs_8_) | copy-start | bytes 589828
  21.0 20.5 %copy-start.12 = (bf16[384,256]{1,0:T(8,128)(2,1)}, bf16[384,256]{1,0:T(8,128)(2,1)S(1)}, u32[]{:S(2)}) copy-start(bf16[384,256]{1,0:T(8,128)(2,1)S(1)} %collective-permute-done.6.refs_10_) | copy-start | bytes 589828
  21.0 4.9 %collective-permute-start.11 = (bf16[384,256]{1,0:T(8,128)(2,1)S(1)}, bf16[384,256]{1,0:T(8,128)(2,1)S(1)}, u32[]{:S(2)}, u32[]{:S(2)}) collective-permute-start(bf16[384,256]{1,0:T(8,128)(2,1)S(1)} %collective-permute-done.6.refs_10_), channel_id=1, source_target_pairs={{4,0},{10,2},{12,4},{2,6},{0,8},{18,10},{20,12},{6,14},{8,16},{26,... | collective-permute-start | bytes 589832 | tf_op jit(solution)/shard_map/ppermute | solution.py:343
  21.2 5.1 %collective-permute-start.8 = (bf16[384,256]{1,0:T(8,128)(2,1)S(1)}, bf16[384,256]{1,0:T(8,128)(2,1)S(1)}, u32[]{:S(2)}, u32[]{:S(2)}) collective-permute-start(bf16[384,256]{1,0:T(8,128)(2,1)S(1)} %collective-permute-done.6.refs_10_), channel_id=1, source_target_pairs={{0,2},{2,0},{4,6},{6,4},{8,10},{10,8},{12,14},{14,12},{16,18},{18,... | collective-permute-start | bytes 589832 | tf_op jit(solution)/shard_map/ppermute | solution.py:304
  23.0 18.5 %copy-start.6 = (bf16[384,256]{1,0:T(8,128)(2,1)}, bf16[384,256]{1,0:T(8,128)(2,1)S(1)}, u32[]{:S(2)}) copy-start(bf16[384,256]{1,0:T(8,128)(2,1)S(1)} %collective-permute-done.10.refs_13_) | copy-start | bytes 589828
  25.8 15.7 %copy-start.7 = (bf16[384,256]{1,0:T(8,128)(2,1)}, bf16[384,256]{1,0:T(8,128)(2,1)S(1)}, u32[]{:S(2)}) copy-start(bf16[384,256]{1,0:T(8,128)(2,1)S(1)} %collective-permute-done.11.refs_14_) | copy-start | bytes 589828
  25.9 10.7 %collective-permute-start.13 = (bf16[2,96,256]{2,1,0:T(8,128)(2,1)S(1)}, bf16[2,96,256]{2,1,0:T(8,128)(2,1)S(1)}, u32[]{:S(2)}, u32[]{:S(2)}) collective-permute-start(bf16[2,96,256]{2,1,0:T(8,128)(2,1)S(1)} %pad_maximum_fusion), channel_id=1, source_target_pairs={{0,1},{1,0},{2,3},{3,2},{4,5},{5,4},{6,7},{7,6},{8,9},{9,8},{10,11... | collective-permute-start | bytes 294920 | tf_op jit(solution)/shard_map/ppermute | solution.py:326
  26.2 10.4 %collective-permute-start.12 = (bf16[384,256]{1,0:T(8,128)(2,1)S(1)}, bf16[384,256]{1,0:T(8,128)(2,1)S(1)}, u32[]{:S(2)}, u32[]{:S(2)}) collective-permute-start(bf16[384,256]{1,0:T(8,128)(2,1)S(1)} %broadcast_select_fusion), channel_id=1, source_target_pairs={{4,0},{10,2},{12,4},{2,6},{0,8},{18,10},{20,12},{6,14},{8,16},{26,... | collective-permute-start | bytes 589832 | tf_op jit(solution)/shard_map/ppermute | solution.py:350
  26.3 15.2 %copy-start.14 = (bf16[384,256]{1,0:T(8,128)(2,1)}, bf16[384,256]{1,0:T(8,128)(2,1)S(1)}, u32[]{:S(2)}) copy-start(bf16[384,256]{1,0:T(8,128)(2,1)S(1)} %collective-permute-done.7.refs_11_) | copy-start | bytes 589828
  26.3 15.2 %copy-start.15 = (bf16[384,256]{1,0:T(8,128)(2,1)}, bf16[384,256]{1,0:T(8,128)(2,1)S(1)}, u32[]{:S(2)}) copy-start(bf16[384,256]{1,0:T(8,128)(2,1)S(1)} %collective-permute-done.8.refs_12_) | copy-start | bytes 589828
  26.4 15.1 %collective-permute-start.9 = (bf16[5,2,48,256]{3,2,1,0:T(8,128)(2,1)S(1)}, bf16[5,2,48,256]{3,2,1,0:T(8,128)(2,1)S(1)}, u32[]{:S(2)}, u32[]{:S(2)}) collective-permute-start(bf16[5,2,48,256]{3,2,1,0:T(8,128)(2,1)S(1)} %fusion.4), channel_id=1, source_target_pairs={{0,1},{1,0},{2,3},{3,2},{4,5},{5,4},{6,7},{7,6},{8,9},{9,8},{10,11... | collective-permute-start | bytes 737288 | tf_op jit(solution)/shard_map/ppermute | solution.py:326
  27.8 9.9 %collective-permute-start.15 = (bf16[2,48,256]{2,1,0:T(8,128)(2,1)S(1)}, bf16[2,48,256]{2,1,0:T(8,128)(2,1)S(1)}, u32[]{:S(2)}, u32[]{:S(2)}) collective-permute-start(bf16[2,48,256]{2,1,0:T(8,128)(2,1)S(1)} %constant_dynamic-slice_fusion), channel_id=1, source_target_pairs={{1,28},{3,30},{5,24},{7,26},{9,20},{11,22},{13,16},{15,18},{16,13}... | collective-permute-start | bytes 147464 | tf_op jit(solution)/shard_map/ppermute | solution.py:335
  34.1 7.1 %collective-permute-start.16 = (bf16[384,256]{1,0:T(8,128)(2,1)S(1)}, bf16[384,256]{1,0:T(8,128)(2,1)S(1)}, u32[]{:S(2)}, u32[]{:S(2)}) collective-permute-start(bf16[384,256]{1,0:T(8,128)(2,1)S(1)} %collective-permute-done.10.refs_13_), channel_id=1, source_target_pairs={{0,2},{2,0},{4,6},{6,4},{8,10},{10,8},{12,14},{14,12},{16,18},{18,... | collective-permute-start | bytes 589832 | tf_op jit(solution)/shard_map/ppermute | solution.py:304
  36.5 4.7 %collective-permute-start.17 = (bf16[384,256]{1,0:T(8,128)(2,1)S(1)}, bf16[384,256]{1,0:T(8,128)(2,1)S(1)}, u32[]{:S(2)}, u32[]{:S(2)}) collective-permute-start(bf16[384,256]{1,0:T(8,128)(2,1)S(1)} %collective-permute-done.11.refs_14_), channel_id=1, source_target_pairs={{0,2},{2,0},{4,6},{6,4},{8,10},{10,8},{12,14},{14,12},{16,18},{18,... | collective-permute-start | bytes 589832 | tf_op jit(solution)/shard_map/ppermute | solution.py:304
  36.6 4.9 %copy-start.17 = (bf16[384,256]{1,0:T(8,128)(2,1)}, bf16[384,256]{1,0:T(8,128)(2,1)S(1)}, u32[]{:S(2)}) copy-start(bf16[384,256]{1,0:T(8,128)(2,1)S(1)} %collective-permute-done.12.refs_17_) | copy-start | bytes 589828
  36.6 4.8 %collective-permute-start.18 = (bf16[384,256]{1,0:T(8,128)(2,1)S(1)}, bf16[384,256]{1,0:T(8,128)(2,1)S(1)}, u32[]{:S(2)}, u32[]{:S(2)}) collective-permute-start(bf16[384,256]{1,0:T(8,128)(2,1)S(1)} %collective-permute-done.12.refs_17_), channel_id=1, source_target_pairs={{0,2},{2,0},{4,6},{6,4},{8,10},{10,8},{12,14},{14,12},{16,18},{18,... | collective-permute-start | bytes 589832 | tf_op jit(solution)/shard_map/ppermute | solution.py:304
  37.7 3.9 %copy-start.21 = (bf16[2,48,256]{2,1,0:T(8,128)(2,1)}, bf16[2,48,256]{2,1,0:T(8,128)(2,1)S(1)}, u32[]{:S(2)}) copy-start(bf16[2,48,256]{2,1,0:T(8,128)(2,1)S(1)} %collective-permute-done.15) | copy-start | bytes 147460
  37.7 3.7 %collective-permute-start.14 = (bf16[2,48,256]{2,1,0:T(8,128)(2,1)S(1)}, bf16[2,48,256]{2,1,0:T(8,128)(2,1)S(1)}, u32[]{:S(2)}, u32[]{:S(2)}) collective-permute-start(bf16[2,48,256]{2,1,0:T(8,128)(2,1)S(1)} %get-tuple-element.13), channel_id=1, source_target_pairs={{0,2},{2,0},{4,6},{6,4},{8,10},{10,8},{12,14},{14,12},{16,18},{18,... | collective-permute-start | bytes 147464 | tf_op jit(solution)/shard_map/ppermute | solution.py:304
  41.2 0.7 copy-start.18
  41.2 0.7 copy-start.19
  41.4 0.6 copy-start.22
  41.4 0.7 copy-start.16
  41.4 0.8 copy-start.20

commit v6 on v5

--- a/solution.py
+++ b/solution.py
@@ -21,28 +21,25 @@
     return centered * lax.rsqrt(variance + EPSILON) * gain + bias
 
 
-def project_body(core_ref, *refs):
-    x_ref, gain_ref, bias_ref, weight_ref, pbias_ref = refs[6:11]
-    out_ref, sems = refs[5], refs[11]
-    copies = [pltpu.make_async_copy(refs[i], refs[6 + i], sems.at[i]) for i in range(5)]
-    for copy in copies:
-        copy.start()
-    for copy in copies:
-        copy.wait()
-    local, _, _ = x_ref.shape
-    width = weight_ref.shape[0]
+def project_body(place_ref, x_ref, packed_ref, out_ref):
+    local = x_ref.shape[0]
+    width = packed_ref.shape[0] - 3
+    weight = packed_ref[:width, :].astype(BF16)
+    gain = packed_ref[width : width + 1, :]
+    bias = packed_ref[width + 1 : width + 2, :]
+    pbias = packed_ref[width + 2 :, :width]
     group = 2 * local
     lanes = width * group
-    first = core_ref[0] * local
+    first = place_ref[0] * local
     ch = lax.rem(lax.broadcasted_iota(jnp.int32, (width, lanes), 0) + width // 2, width)
     lane = lax.broadcasted_iota(jnp.int32, (width, lanes), 1)
     total = None
     for s in range(local):
-        normed = norm_rows(x_ref[s].astype(F32), gain_ref[...], bias_ref[...]).astype(BF16)
+        normed = norm_rows(x_ref[s].astype(F32), gain, bias).astype(BF16)
         y = lax.dot_general(
-            normed, weight_ref[...], (((1,), (1,)), ((), ())), preferred_element_type=F32
+            normed, weight, (((1,), (1,)), ((), ())), preferred_element_type=F32
         )
-        y = y + pbias_ref[...]
+        y = y + pbias
         spread = (lane == ch * group + (first + s)).astype(F32).astype(BF16)
         part = jnp.dot(y.astype(BF16), spread, preferred_element_type=F32)
         total = part if total is None else total + part
@@ -55,20 +52,17 @@
     return pl.BlockSpec(a.shape, lambda i: (0,) * len(a.shape))
 
 
-def project(core, x, gain, bias, weight, pbias):
+def project(place, x, packed):
     local, residues, _ = x.shape
-    lanes = weight.shape[0] * local
-    operands = (x, gain, bias, weight, pbias)
+    lanes = (packed.shape[0] - 3) * local
+    vmem = pl.BlockSpec(memory_space=pltpu.VMEM)
     return pl.pallas_call(
         project_body,
-        in_specs=[pl.BlockSpec(memory_space=pltpu.SMEM)]
-        + [pl.BlockSpec(memory_space=pltpu.HBM)] * 5,
-        out_specs=pl.BlockSpec(memory_space=pltpu.VMEM),
+        in_specs=[pl.BlockSpec(memory_space=pltpu.SMEM), vmem, vmem],
+        out_specs=vmem,
         out_shape=jax.ShapeDtypeStruct((2, residues, lanes), BF16),
-        scratch_shapes=[pltpu.VMEM(a.shape, a.dtype) for a in operands]
-        + [pltpu.SemaphoreType.DMA((5,))],
         compiler_params=pltpu.CompilerParams(vmem_limit_bytes=32 << 20),
-    )(core, *operands)
+    )(place, x, packed)
 
 
 def power_of_two(largest):
@@ -189,10 +183,23 @@
 
         @pl.when(place_ref[1] == 0)
         def _():
-            blocks = [(r, q) for r in there_refs for q in range(r.shape[0])]
-            for i, (r, q) in enumerate(blocks):
+            blocks = []
+            for r in there_refs:
+                if len(r.shape) == 4:
+                    blocks.extend((r.at[q], 0) for q in range(r.shape[0]))
+                elif r.shape[1] == row_length:
+                    blocks.append((r, 0))
+                else:
+                    skip = r.shape[1] - 2 * row_length
+                    if skip and not blocks:
+                        blocks.append((r, 0))
+                    skip = skip + place_ref[0] * row_length
+                    blocks.append((r, pl.multiple_of(skip, row_length)))
+            for i, (r, skip) in enumerate(blocks):
                 for side in range(2):
-                    x_scr[side, i * row_length : (i + 1) * row_length, :] = r[q, side]
+                    x_scr[side, i * row_length : (i + 1) * row_length, :] = r[
+                        side, pl.ds(skip, row_length), :
+                    ]
 
         split_weight(chips * group, w_out_ref, w_ref, undo_ref, w_scr)
         prepare_rows(chips, group, x_scr, undo_ref, y_scr, lhs_scr, undo_scr)
@@ -228,11 +235,10 @@
         out_ref[g] = (pair + update + b_down_ref[...]).astype(BF16)
 
 
-def pair_kernel(place, group, rows, cols, rest):
+def pair_kernel(place, group, row_length, rows, cols, rest):
     own = cols[0]
     _, column_length, part = own.shape
     chips = (len(cols) + 1) // 2
-    row_length = rows[0].shape[2]
     zc = rest[1].shape[1]
     here = math.gcd(row_length, 8)
     depth = chips * part
@@ -305,19 +311,23 @@
 
     ring = [(src, r) for r, src in enumerate(ring_source(chips))]
 
-    mine = project(
-        core.reshape(1),
-        alignment,
-        alignment_norm_gain[None],
-        alignment_norm_bias[None],
-        projection_weight.T,
-        projection_bias_pair[None],
+    per_col = column_length // row_length
+    source = row_index // per_col
+    is_here = (source == col_index).astype(core.dtype)
+    if col_count != 2:
+        is_here = jnp.zeros_like(is_here)
+    place = jnp.stack([core, is_here, row_index % per_col])
+    pad = jnp.pad(projection_bias_pair, (0, alignment_norm_gain.shape[0] - width))
+    packed = jnp.concatenate(
+        [
+            projection_weight.T.astype(F32),
+            jnp.stack([alignment_norm_gain, alignment_norm_bias, pad]),
+        ]
     )
+    mine = project(place, alignment, packed)
     own = mine + swap(mine)
 
-    per_col = column_length // row_length
     start = (row_index % per_col) * row_length
-    source = row_index // per_col
 
     def cut(pair, first, count):
         return jnp.stack([lax.dynamic_slice_in_dim(c, first, count, 0) for c in pair])
@@ -338,36 +348,39 @@
             [(2 * r + t // per_col, 2 * t + 1 - t // per_col) for r, t in enumerate(targets)],
         )
     blocks = [cut((right, left), start, row_length)]
+    rows = []
+    both = None
+    pair_start = start - core * row_length
     for d in range(steps):
         right = lax.ppermute(right, "row", ring)
         left = lax.ppermute(left, "row", ring)
+        if two:
+            if d > 0:
+                right, left, both = lax.optimization_barrier((right, left, both))
+                rows.extend([both, swap(both)])
+            both = cut((right, left), pair_start, 2 * row_length)
+            if d == 0:
+                both = jnp.concatenate([blocks[0], both], axis=1)
+            both = across(both)
         other = (swap(right), swap(left))
         cols.extend([right, left, *other])
-        if d < steps - 1 or not two:
+        if not two:
             blocks.extend([cut(pair, start, row_length) for pair in ((right, left), other)])
-        if d == steps - 2 and two:
-            rows = [across(jnp.stack(blocks))]
     far = lax.ppermute(jnp.where(core == 0, right, left), "row", ring)
     if two:
-        both = across(cut((right, left), start - core * row_length, 2 * row_length))
         far, both = lax.optimization_barrier((far, both))
-        kept = lax.dynamic_slice_in_dim(both, core * row_length, row_length, 1)
-        given = lax.dynamic_slice_in_dim(both, (1 - core) * row_length, row_length, 1)
-        rows.extend([kept[None], swap(given)[None], far_rows[None]])
+        rows.extend([both, swap(both), far_rows])
     far_other = swap(far)
     cols.extend([far, far_other])
-    is_here = (source == col_index).astype(core.dtype)
     if not two:
         a = lax.dynamic_slice_in_dim(far, start, row_length, 0)
         b = lax.dynamic_slice_in_dim(far_other, start, row_length, 0)
         blocks.append(jnp.stack([jnp.where(core == 0, a, b), jnp.where(core == 0, b, a)]))
         gathered = lax.all_gather(jnp.stack(blocks), "col")
         rows = [lax.dynamic_index_in_dim(gathered, source, 0, False)]
-        is_here = jnp.zeros_like(is_here)
-
-    place = jnp.stack([core, is_here, row_index % per_col])
+
     rest = (w_out, b_out[None], pair_gain[None], pair_bias[None], w_up, b_up[None], w_down)
-    return pair_kernel(place, 2 * local, rows, cols, rest + (b_down[None],))
+    return pair_kernel(place, 2 * local, row_length, rows, cols, rest + (b_down[None],))
 
 
 def solution(mesh):

time: 87.7 us -> 91.7 us (1.046)
  waiting for transfers between devices: 6.68 us -> 16.1 us
  starting transfers between devices: 27.7 us -> 23.8 us
  local copies, waits for them, and re-layouts: 5.36 us -> 2.5 us
    ppermute x2 -> x3, waiting for transfers between devices: 0.01 us -> 7.56 us  [across(): return lax.ppermute(block, 'col', [(0, 1), (1, 0)])]
    ppermute x9 -> x11, starting transfers between devices: 13.8 us -> 6.47 us  [swap(): return lax.ppermute(a, 'row', [(r, r ^ 1) for r in range(row_count)])]
    unnamed x46 -> x48, local copies, waits for them, and re-layouts: 4.6 us -> 1.73 us
    ppermute x1, waiting for transfers between devices: 0.01 us -> 2.81 us  [shards(): lax.ppermute(lax.dynamic_slice_in_dim(own, first, row_length, 1), ('row',...]
    ppermute x3, waiting for transfers between devices: 2.82 us -> 0.87 us  [shards(): left = lax.ppermute(left, 'row', ring)]
    ppermute x3, starting transfers between devices: 2.05 us -> 3.9 us  [shards(): left = lax.ppermute(left, 'row', ring)]
    ppermute x1, starting transfers between devices: 0.06 us -> 1.71 us  [shards(): far = lax.ppermute(jnp.where(core == 0, right, left), 'row', ring)]
    ppermute x9 -> x11, waiting for transfers between devices: 1.58 us -> 2.55 us  [swap(): return lax.ppermute(a, 'row', [(r, r ^ 1) for r in range(row_count)])]
  transfers between devices with their start and end apart: 19 -> 22, of which waited for: 4 -> 10; matrix products, arithmetic and copies ran while one was open for 2% -> 0% of each run, Pallas kernels for 0% -> 0%
where the time goes in v6:
time: 91.7 us; the launch traced here: 91.4 us
  Pallas kernels  46.9 us (51%)
  starting transfers between devices  23.8 us (26%)
  waiting for transfers between devices  16.1 us (18%)
  local copies, waits for them, and re-layouts  2.5 us (3%)
  other arithmetic  1.71 us (2%)
    pallas_call x1, Pallas kernels, pair_kernel(): pl.pallas_call(functools.partial(pair_body, chips, here, group, len(rows)...  45.2 us
    ppermute x3, waiting for transfers between devices, across(): return lax.ppermute(block, 'col', [(0, 1), (1, 0)])  7.56 us
    ppermute x11, starting transfers between devices, swap(): return lax.ppermute(a, 'row', [(r, r ^ 1) for r in range(row_count)])  6.47 us
    ppermute x1, starting transfers between devices, shards(): lax.ppermute(lax.dynamic_slice_in_dim(own, first, row_length, 1), ('row',...  5.69 us
    ppermute x3, starting transfers between devices, shards(): right = lax.ppermute(right, 'row', ring)  4.57 us
    ppermute x3, starting transfers between devices, shards(): left = lax.ppermute(left, 'row', ring)  3.9 us
    ppermute x1, waiting for transfers between devices, shards(): lax.ppermute(lax.dynamic_slice_in_dim(own, first, row_length, 1), ('row',...  2.81 us
    ppermute x11, waiting for transfers between devices, swap(): return lax.ppermute(a, 'row', [(r, r ^ 1) for r in range(row_count)])  2.55 us
  transfers between devices with their start and end apart: 22, of which 10 were waited for; matrix products, arithmetic and copies ran while one was open for 0% of the time, Pallas kernels for 0%

profile of v6, /device:TPU:3, one launch (start us, length us, event | category | flops | bytes accessed | tf_op | source)
XLA Modules:
  0.0 91.4 jit_solution(6879560615710379221)
XLA Ops:
  0.0 0.8 convert_bitcast_fusion
  0.8 0.7 pad.4
  1.4 0.1 pad_add_fusion.place_ref
  1.5 0.7 pad_maximum_fusion.2.packed_ref
  2.2 0.0 copy-start
  2.2 1.1 %copy-done = bf16[4,384,256]{2,1,0:T(8,128)(2,1)S(1)} copy-done((bf16[4,384,256]{2,1,0:T(8,128)(2,1)S(1)}, bf16[4,384,256]{2,1,0:T(8,128)(2,1)}, u32[]{:S(2)}) %copy-start) | copy-done | bytes 786456
  3.3 1.7 %shard_map.127 = bf16[2,384,256]{2,1,0:T(8,128)(2,1)S(1)} custom-call(s32[3]{0:T(128)S(1)} %pad_add_fusion.place_ref, bf16[4,384,256]{2,1,0:T(8,128)(2,1)S(1)} %copy-done, f32[67,256]{1,0:T(8,128)S(1)} %pad_maximum_fusion.2.packed_ref), custom_call_target="tpu_custom_call" | custom-call | tf_op jit(solution)/shard_map/pallas_call | solution.py:59
  5.1 0.7 collective-permute-start
  5.8 1.3 %collective-permute-done = bf16[2,384,256]{2,1,0:T(8,128)(2,1)S(1)} collective-permute-done((bf16[2,384,256]{2,1,0:T(8,128)(2,1)S(1)}, bf16[2,384,256]{2,1,0:T(8,128)(2,1)S(1)}, u32[]{:S(2)}, u32[]{:S(2)}) %collective-permute-start) | collective-permute-done | bytes 393248 | tf_op jit(solution)/shard_map/ppermute | solution.py:310
  7.2 0.1 add.37.refs_7_
  7.3 0.0 copy-start.2
  7.3 0.1 fusion
  7.4 1.3 %collective-permute-start.1 = (bf16[384,256]{1,0:T(8,128)(2,1)S(1)}, bf16[384,256]{1,0:T(8,128)(2,1)S(1)}, u32[]{:S(2)}, u32[]{:S(2)}) collective-permute-start(bf16[384,256]{1,0:T(8,128)(2,1)S(1)} %get-tuple-element.22), channel_id=1, source_target_pairs={{4,0},{10,2},{12,4},{2,6},{0,8},{18,10},{20,12},{6,14},{8,16},{26,... | collective-permute-start | bytes 589832 | tf_op jit(solution)/shard_map/ppermute | solution.py:355
  8.6 1.3 %collective-permute-start.3 = (bf16[384,256]{1,0:T(8,128)(2,1)S(1)}, bf16[384,256]{1,0:T(8,128)(2,1)S(1)}, u32[]{:S(2)}, u32[]{:S(2)}) collective-permute-start(bf16[384,256]{1,0:T(8,128)(2,1)S(1)} %get-tuple-element.23), channel_id=1, source_target_pairs={{4,0},{10,2},{12,4},{2,6},{0,8},{18,10},{20,12},{6,14},{8,16},{26,... | collective-permute-start | bytes 589832 | tf_op jit(solution)/shard_map/ppermute | solution.py:356
  9.9 2.3 %collective-permute-done.1.refs_8_ = bf16[384,256]{1,0:T(8,128)(2,1)S(1)} collective-permute-done((bf16[384,256]{1,0:T(8,128)(2,1)S(1)}, bf16[384,256]{1,0:T(8,128)(2,1)S(1)}, u32[]{:S(2)}, u32[]{:S(2)}) %collective-permute-start.1) | collective-permute-done | bytes 196640 | tf_op jit(solution)/shard_map/ppermute | solution.py:355
  12.2 1.2 %collective-permute-start.2 = (bf16[384,256]{1,0:T(8,128)(2,1)S(1)}, bf16[384,256]{1,0:T(8,128)(2,1)S(1)}, u32[]{:S(2)}, u32[]{:S(2)}) collective-permute-start(bf16[384,256]{1,0:T(8,128)(2,1)S(1)} %collective-permute-done.1.refs_8_), channel_id=1, source_target_pairs={{4,0},{10,2},{12,4},{2,6},{0,8},{18,10},{20,12},{6,14},{8,16},{26,... | collective-permute-start | bytes 589832 | tf_op jit(solution)/shard_map/ppermute | solution.py:355
  13.5 0.9 collective-permute-done.3.refs_9_
  14.3 1.2 %collective-permute-start.4 = (bf16[384,256]{1,0:T(8,128)(2,1)S(1)}, bf16[384,256]{1,0:T(8,128)(2,1)S(1)}, u32[]{:S(2)}, u32[]{:S(2)}) collective-permute-start(bf16[384,256]{1,0:T(8,128)(2,1)S(1)} %collective-permute-done.3.refs_9_), channel_id=1, source_target_pairs={{4,0},{10,2},{12,4},{2,6},{0,8},{18,10},{20,12},{6,14},{8,16},{26,... | collective-permute-start | bytes 589832 | tf_op jit(solution)/shard_map/ppermute | solution.py:356
  15.6 0.3 collective-permute-start.5
  15.9 4.0 %collective-permute-done.5.refs_0_ = bf16[2,144,256]{2,1,0:T(8,128)(2,1)S(1)} collective-permute-done((bf16[2,144,256]{2,1,0:T(8,128)(2,1)S(1)}, bf16[2,144,256]{2,1,0:T(8,128)(2,1)S(1)}, u32[]{:S(2)}, u32[]{:S(2)}) %collective-permute-start.5) | collective-permute-done | bytes 147488 | tf_op jit(solution)/shard_map/ppermute | solution.py:336
  19.9 0.0 collective-permute-done.2.refs_12_
  19.9 0.0 collective-permute-done.4.refs_13_
  20.0 0.0 copy-start.8
  20.0 2.0 %collective-permute-start.7 = (bf16[384,256]{1,0:T(8,128)(2,1)S(1)}, bf16[384,256]{1,0:T(8,128)(2,1)S(1)}, u32[]{:S(2)}, u32[]{:S(2)}) collective-permute-start(bf16[384,256]{1,0:T(8,128)(2,1)S(1)} %collective-permute-done.2.refs_12_), channel_id=1, source_target_pairs={{4,0},{10,2},{12,4},{2,6},{0,8},{18,10},{20,12},{6,14},{8,16},{26,... | collective-permute-start | bytes 589832 | tf_op jit(solution)/shard_map/ppermute | solution.py:355
  22.0 1.4 %collective-permute-start.8 = (bf16[384,256]{1,0:T(8,128)(2,1)S(1)}, bf16[384,256]{1,0:T(8,128)(2,1)S(1)}, u32[]{:S(2)}, u32[]{:S(2)}) collective-permute-start(bf16[384,256]{1,0:T(8,128)(2,1)S(1)} %collective-permute-done.4.refs_13_), channel_id=1, source_target_pairs={{4,0},{10,2},{12,4},{2,6},{0,8},{18,10},{20,12},{6,14},{8,16},{26,... | collective-permute-start | bytes 589832 | tf_op jit(solution)/shard_map/ppermute | solution.py:356
  23.4 0.3 collective-permute-start.9
  23.7 3.5 %collective-permute-done.9.refs_2_ = bf16[2,96,256]{2,1,0:T(8,128)(2,1)S(1)} collective-permute-done((bf16[2,96,256]{2,1,0:T(8,128)(2,1)S(1)}, bf16[2,96,256]{2,1,0:T(8,128)(2,1)S(1)}, u32[]{:S(2)}, u32[]{:S(2)}) %collective-permute-start.9) | collective-permute-done | bytes 98336 | tf_op jit(solution)/shard_map/ppermute | solution.py:336
  27.3 0.0 collective-permute-done.7.refs_16_
  27.3 0.0 collective-permute-done.8.refs_17_
  27.3 0.0 copy-start.4
  27.3 1.7 %collective-permute-start.11 = (bf16[384,256]{1,0:T(8,128)(2,1)S(1)}, bf16[384,256]{1,0:T(8,128)(2,1)S(1)}, u32[]{:S(2)}, u32[]{:S(2)}) collective-permute-start(bf16[384,256]{1,0:T(8,128)(2,1)S(1)} %broadcast_select_fusion), channel_id=1, source_target_pairs={{4,0},{10,2},{12,4},{2,6},{0,8},{18,10},{20,12},{6,14},{8,16},{26,... | collective-permute-start | bytes 589832 | tf_op jit(solution)/shard_map/ppermute | solution.py:369
  29.1 0.8 collective-permute-start.12
  29.9 2.7 %collective-permute-start.15 = (bf16[384,256]{1,0:T(8,128)(2,1)S(1)}, bf16[384,256]{1,0:T(8,128)(2,1)S(1)}, u32[]{:S(2)}, u32[]{:S(2)}) collective-permute-start(bf16[384,256]{1,0:T(8,128)(2,1)S(1)} %collective-permute-done.1.refs_8_), channel_id=1, source_target_pairs={{0,2},{2,0},{4,6},{6,4},{8,10},{10,8},{12,14},{14,12},{16,18},{18,... | collective-permute-start | bytes 589832 | tf_op jit(solution)/shard_map/ppermute | solution.py:310
  32.6 5.7 %collective-permute-start.14 = (bf16[2,48,256]{2,1,0:T(8,128)(2,1)S(1)}, bf16[2,48,256]{2,1,0:T(8,128)(2,1)S(1)}, u32[]{:S(2)}, u32[]{:S(2)}) collective-permute-start(bf16[2,48,256]{2,1,0:T(8,128)(2,1)S(1)} %constant_dynamic-slice_fusion), channel_id=1, source_target_pairs={{1,28},{3,30},{5,24},{7,26},{9,20},{11,22},{13,16},{15,18},{16,13}... | collective-permute-start | bytes 147464 | tf_op jit(solution)/shard_map/ppermute | solution.py:345
  38.3 0.3 collective-permute-start.16
  38.6 2.8 %collective-permute-done.14.refs_6_ = bf16[2,48,256]{2,1,0:T(8,128)(2,1)S(1)} collective-permute-done((bf16[2,48,256]{2,1,0:T(8,128)(2,1)S(1)}, bf16[2,48,256]{2,1,0:T(8,128)(2,1)S(1)}, u32[]{:S(2)}, u32[]{:S(2)}) %collective-permute-start.14) | collective-permute-done | bytes 49184 | tf_op jit(solution)/shard_map/ppermute | solution.py:345
  41.5 0.9 collective-permute-start.6
  42.3 0.0 collective-permute-done.12.refs_4_
  42.3 0.1 collective-permute-start.17
  42.4 0.0 collective-permute-done.11.refs_20_
  42.4 0.4 collective-permute-start.18
  42.9 0.0 collective-permute-done.15.refs_10_
  42.9 0.1 collective-permute-start.19
  43.0 0.0 collective-permute-done.16.refs_11_
  43.0 0.4 collective-permute-start.20
  43.4 0.0 collective-permute-done.6.refs_1_
  43.4 0.3 collective-permute-start.21
  43.7 0.1 collective-permute-done.17.refs_14_
  43.8 0.2 collective-permute-start.10
  44.0 0.1 collective-permute-done.18.refs_15_
  44.1 0.2 collective-permute-start.13
  44.3 0.8 collective-permute-done.10.refs_3_
  45.1 0.0 collective-permute-done.19.refs_18_
  45.1 0.0 collective-permute-done.20.refs_19_
  45.1 0.0 copy-start.15
  45.1 0.3 collective-permute-done.13.refs_5_
  45.4 0.0 collective-permute-done.21.refs_21_
  45.4 0.0 copy-done.1
  45.6 0.2 copy-done.21
  45.7 0.1 copy-done.14
  45.8 0.1 copy-done.15
  45.9 0.1 copy-done.22
  46.0 0.1 copy-done.16
  46.1 45.2 %shard_map.128 = bf16[48,384,128]{2,1,0:T(8,128)(2,1)} custom-call(s32[3]{0:T(128)} %copy-done.1, bf16[2,144,256]{2,1,0:T(8,128)(2,1)} %copy-done.17, bf16[2,144,256]{2,1,0:T(8,128)(2,1)} %copy-done.18, bf16[2,96,256]{2,1,0:T(8,128)(2,1)} %copy-done.19, bf16[2,96,256]{2,1,0:T(8,128)(2,1)} %copy-done.21, bf16[2,96,256]{2,1,0:T(8,128)(2,1)} %copy-done.20, ...), custom_call_target="tpu_custom_call" | custom-call | tf_op jit(solution)/shard_map/pallas_call | solution.py:247
  (48 shorter events, 0.2 us)
Async XLA Ops:
  1.5 43.9 %copy-start.1 = (s32[3]{0:T(128)}, s32[3]{0:T(128)S(1)}, u32[]{:S(2)}) copy-start(s32[3]{0:T(128)S(1)} %pad_add_fusion.place_ref) | copy-start | bytes 40
  2.2 1.1 %copy-start = (bf16[4,384,256]{2,1,0:T(8,128)(2,1)S(1)}, bf16[4,384,256]{2,1,0:T(8,128)(2,1)}, u32[]{:S(2)}) copy-start(bf16[4,384,256]{2,1,0:T(8,128)(2,1)} %x_ref.1) | copy-start | bytes 2359300
  5.1 2.1 %collective-permute-start = (bf16[2,384,256]{2,1,0:T(8,128)(2,1)S(1)}, bf16[2,384,256]{2,1,0:T(8,128)(2,1)S(1)}, u32[]{:S(2)}, u32[]{:S(2)}) collective-permute-start(bf16[2,384,256]{2,1,0:T(8,128)(2,1)S(1)} %shard_map.127), channel_id=1, source_target_pairs={{0,2},{2,0},{4,6},{6,4},{8,10},{10,8},{12,14},{14,12},{16,18},{18,... | collective-permute-start | bytes 1179656 | tf_op jit(solution)/shard_map/ppermute | solution.py:310
  7.3 38.1 %copy-start.2 = (bf16[2,384,256]{2,1,0:T(8,128)(2,1)}, bf16[2,384,256]{2,1,0:T(8,128)(2,1)S(1)}, u32[]{:S(2)}) copy-start(bf16[2,384,256]{2,1,0:T(8,128)(2,1)S(1)} %add.37.refs_7_) | copy-start | bytes 1179652
  7.4 4.9 %collective-permute-start.1 = (bf16[384,256]{1,0:T(8,128)(2,1)S(1)}, bf16[384,256]{1,0:T(8,128)(2,1)S(1)}, u32[]{:S(2)}, u32[]{:S(2)}) collective-permute-start(bf16[384,256]{1,0:T(8,128)(2,1)S(1)} %get-tuple-element.22), channel_id=1, source_target_pairs={{4,0},{10,2},{12,4},{2,6},{0,8},{18,10},{20,12},{6,14},{8,16},{26,... | collective-permute-start | bytes 589832 | tf_op jit(solution)/shard_map/ppermute | solution.py:355
  8.6 5.7 %collective-permute-start.3 = (bf16[384,256]{1,0:T(8,128)(2,1)S(1)}, bf16[384,256]{1,0:T(8,128)(2,1)S(1)}, u32[]{:S(2)}, u32[]{:S(2)}) collective-permute-start(bf16[384,256]{1,0:T(8,128)(2,1)S(1)} %get-tuple-element.23), channel_id=1, source_target_pairs={{4,0},{10,2},{12,4},{2,6},{0,8},{18,10},{20,12},{6,14},{8,16},{26,... | collective-permute-start | bytes 589832 | tf_op jit(solution)/shard_map/ppermute | solution.py:356
  12.2 33.2 %copy-start.5 = (bf16[384,256]{1,0:T(8,128)(2,1)}, bf16[384,256]{1,0:T(8,128)(2,1)S(1)}, u32[]{:S(2)}) copy-start(bf16[384,256]{1,0:T(8,128)(2,1)S(1)} %collective-permute-done.1.refs_8_) | copy-start | bytes 589828
  12.2 7.7 %collective-permute-start.2 = (bf16[384,256]{1,0:T(8,128)(2,1)S(1)}, bf16[384,256]{1,0:T(8,128)(2,1)S(1)}, u32[]{:S(2)}, u32[]{:S(2)}) collective-permute-start(bf16[384,256]{1,0:T(8,128)(2,1)S(1)} %collective-permute-done.1.refs_8_), channel_id=1, source_target_pairs={{4,0},{10,2},{12,4},{2,6},{0,8},{18,10},{20,12},{6,14},{8,16},{26,... | collective-permute-start | bytes 589832 | tf_op jit(solution)/shard_map/ppermute | solution.py:355
  14.3 31.1 %copy-start.6 = (bf16[384,256]{1,0:T(8,128)(2,1)}, bf16[384,256]{1,0:T(8,128)(2,1)S(1)}, u32[]{:S(2)}) copy-start(bf16[384,256]{1,0:T(8,128)(2,1)S(1)} %collective-permute-done.3.refs_9_) | copy-start | bytes 589828
  14.3 5.6 %collective-permute-start.4 = (bf16[384,256]{1,0:T(8,128)(2,1)S(1)}, bf16[384,256]{1,0:T(8,128)(2,1)S(1)}, u32[]{:S(2)}, u32[]{:S(2)}) collective-permute-start(bf16[384,256]{1,0:T(8,128)(2,1)S(1)} %collective-permute-done.3.refs_9_), channel_id=1, source_target_pairs={{4,0},{10,2},{12,4},{2,6},{0,8},{18,10},{20,12},{6,14},{8,16},{26,... | collective-permute-start | bytes 589832 | tf_op jit(solution)/shard_map/ppermute | solution.py:356
  15.6 4.4 %collective-permute-start.5 = (bf16[2,144,256]{2,1,0:T(8,128)(2,1)S(1)}, bf16[2,144,256]{2,1,0:T(8,128)(2,1)S(1)}, u32[]{:S(2)}, u32[]{:S(2)}) collective-permute-start(bf16[2,144,256]{2,1,0:T(8,128)(2,1)S(1)} %maximum_maximum_fusion), channel_id=1, source_target_pairs={{0,1},{1,0},{2,3},{3,2},{4,5},{5,4},{6,7},{7,6},{8,9},{9,8},{10,11... | collective-permute-start | bytes 442376 | tf_op jit(solution)/shard_map/ppermute | solution.py:336
  19.9 25.5 %copy-start.17 = (bf16[2,144,256]{2,1,0:T(8,128)(2,1)}, bf16[2,144,256]{2,1,0:T(8,128)(2,1)S(1)}, u32[]{:S(2)}) copy-start(bf16[2,144,256]{2,1,0:T(8,128)(2,1)S(1)} %collective-permute-done.5.refs_0_) | copy-start | bytes 442372
  19.9 25.5 %copy-start.7 = (bf16[384,256]{1,0:T(8,128)(2,1)}, bf16[384,256]{1,0:T(8,128)(2,1)S(1)}, u32[]{:S(2)}) copy-start(bf16[384,256]{1,0:T(8,128)(2,1)S(1)} %collective-permute-done.2.refs_12_) | copy-start | bytes 589828
  20.0 25.5 %copy-start.8 = (bf16[384,256]{1,0:T(8,128)(2,1)}, bf16[384,256]{1,0:T(8,128)(2,1)S(1)}, u32[]{:S(2)}) copy-start(bf16[384,256]{1,0:T(8,128)(2,1)S(1)} %collective-permute-done.4.refs_13_) | copy-start | bytes 589828
  20.0 7.3 %collective-permute-start.7 = (bf16[384,256]{1,0:T(8,128)(2,1)S(1)}, bf16[384,256]{1,0:T(8,128)(2,1)S(1)}, u32[]{:S(2)}, u32[]{:S(2)}) collective-permute-start(bf16[384,256]{1,0:T(8,128)(2,1)S(1)} %collective-permute-done.2.refs_12_), channel_id=1, source_target_pairs={{4,0},{10,2},{12,4},{2,6},{0,8},{18,10},{20,12},{6,14},{8,16},{26,... | collective-permute-start | bytes 589832 | tf_op jit(solution)/shard_map/ppermute | solution.py:355
  22.0 5.2 %collective-permute-start.8 = (bf16[384,256]{1,0:T(8,128)(2,1)S(1)}, bf16[384,256]{1,0:T(8,128)(2,1)S(1)}, u32[]{:S(2)}, u32[]{:S(2)}) collective-permute-start(bf16[384,256]{1,0:T(8,128)(2,1)S(1)} %collective-permute-done.4.refs_13_), channel_id=1, source_target_pairs={{4,0},{10,2},{12,4},{2,6},{0,8},{18,10},{20,12},{6,14},{8,16},{26,... | collective-permute-start | bytes 589832 | tf_op jit(solution)/shard_map/ppermute | solution.py:356
  23.4 3.8 %collective-permute-start.9 = (bf16[2,96,256]{2,1,0:T(8,128)(2,1)S(1)}, bf16[2,96,256]{2,1,0:T(8,128)(2,1)S(1)}, u32[]{:S(2)}, u32[]{:S(2)}) collective-permute-start(bf16[2,96,256]{2,1,0:T(8,128)(2,1)S(1)} %pad_maximum_fusion), channel_id=1, source_target_pairs={{0,1},{1,0},{2,3},{3,2},{4,5},{5,4},{6,7},{7,6},{8,9},{9,8},{10,11... | collective-permute-start | bytes 294920 | tf_op jit(solution)/shard_map/ppermute | solution.py:336
  27.2 18.2 %copy-start.19 = (bf16[2,96,256]{2,1,0:T(8,128)(2,1)}, bf16[2,96,256]{2,1,0:T(8,128)(2,1)S(1)}, u32[]{:S(2)}) copy-start(bf16[2,96,256]{2,1,0:T(8,128)(2,1)S(1)} %collective-permute-done.9.refs_2_) | copy-start | bytes 294916
  27.3 18.2 %copy-start.3 = (bf16[384,256]{1,0:T(8,128)(2,1)}, bf16[384,256]{1,0:T(8,128)(2,1)S(1)}, u32[]{:S(2)}) copy-start(bf16[384,256]{1,0:T(8,128)(2,1)S(1)} %collective-permute-done.7.refs_16_) | copy-start | bytes 589828
  27.3 18.2 %copy-start.4 = (bf16[384,256]{1,0:T(8,128)(2,1)}, bf16[384,256]{1,0:T(8,128)(2,1)S(1)}, u32[]{:S(2)}) copy-start(bf16[384,256]{1,0:T(8,128)(2,1)S(1)} %collective-permute-done.8.refs_17_) | copy-start | bytes 589828
  27.3 15.1 %collective-permute-start.11 = (bf16[384,256]{1,0:T(8,128)(2,1)S(1)}, bf16[384,256]{1,0:T(8,128)(2,1)S(1)}, u32[]{:S(2)}, u32[]{:S(2)}) collective-permute-start(bf16[384,256]{1,0:T(8,128)(2,1)S(1)} %broadcast_select_fusion), channel_id=1, source_target_pairs={{4,0},{10,2},{12,4},{2,6},{0,8},{18,10},{20,12},{6,14},{8,16},{26,... | collective-permute-start | bytes 589832 | tf_op jit(solution)/shard_map/ppermute | solution.py:369
  29.1 13.3 %collective-permute-start.12 = (bf16[2,96,256]{2,1,0:T(8,128)(2,1)S(1)}, bf16[2,96,256]{2,1,0:T(8,128)(2,1)S(1)}, u32[]{:S(2)}, u32[]{:S(2)}) collective-permute-start(bf16[2,96,256]{2,1,0:T(8,128)(2,1)S(1)} %pad_maximum_fusion.1), channel_id=1, source_target_pairs={{0,1},{1,0},{2,3},{3,2},{4,5},{5,4},{6,7},{7,6},{8,9},{9,8},{10,11... | collective-permute-start | bytes 294920 | tf_op jit(solution)/shard_map/ppermute | solution.py:336
  29.9 13.0 %collective-permute-start.15 = (bf16[384,256]{1,0:T(8,128)(2,1)S(1)}, bf16[384,256]{1,0:T(8,128)(2,1)S(1)}, u32[]{:S(2)}, u32[]{:S(2)}) collective-permute-start(bf16[384,256]{1,0:T(8,128)(2,1)S(1)} %collective-permute-done.1.refs_8_), channel_id=1, source_target_pairs={{0,2},{2,0},{4,6},{6,4},{8,10},{10,8},{12,14},{14,12},{16,18},{18,... | collective-permute-start | bytes 589832 | tf_op jit(solution)/shard_map/ppermute | solution.py:310
  32.6 8.8 %collective-permute-start.14 = (bf16[2,48,256]{2,1,0:T(8,128)(2,1)S(1)}, bf16[2,48,256]{2,1,0:T(8,128)(2,1)S(1)}, u32[]{:S(2)}, u32[]{:S(2)}) collective-permute-start(bf16[2,48,256]{2,1,0:T(8,128)(2,1)S(1)} %constant_dynamic-slice_fusion), channel_id=1, source_target_pairs={{1,28},{3,30},{5,24},{7,26},{9,20},{11,22},{13,16},{15,18},{16,13}... | collective-permute-start | bytes 147464 | tf_op jit(solution)/shard_map/ppermute | solution.py:345
  38.3 4.7 %collective-permute-start.16 = (bf16[384,256]{1,0:T(8,128)(2,1)S(1)}, bf16[384,256]{1,0:T(8,128)(2,1)S(1)}, u32[]{:S(2)}, u32[]{:S(2)}) collective-permute-start(bf16[384,256]{1,0:T(8,128)(2,1)S(1)} %collective-permute-done.3.refs_9_), channel_id=1, source_target_pairs={{0,2},{2,0},{4,6},{6,4},{8,10},{10,8},{12,14},{14,12},{16,18},{18,... | collective-permute-start | bytes 589832 | tf_op jit(solution)/shard_map/ppermute | solution.py:310
  41.5 4.0 %copy-start.23 = (bf16[2,48,256]{2,1,0:T(8,128)(2,1)}, bf16[2,48,256]{2,1,0:T(8,128)(2,1)S(1)}, u32[]{:S(2)}) copy-start(bf16[2,48,256]{2,1,0:T(8,128)(2,1)S(1)} %collective-permute-done.14.refs_6_) | copy-start | bytes 147460
  41.5 1.9 %collective-permute-start.6 = (bf16[2,144,256]{2,1,0:T(8,128)(2,1)S(1)}, bf16[2,144,256]{2,1,0:T(8,128)(2,1)S(1)}, u32[]{:S(2)}, u32[]{:S(2)}) collective-permute-start(bf16[2,144,256]{2,1,0:T(8,128)(2,1)S(1)} %collective-permute-done.5.refs_0_), channel_id=1, source_target_pairs={{0,2},{2,0},{4,6},{6,4},{8,10},{10,8},{12,14},{14,12},{16,18},{18,... | collective-permute-start | bytes 442376 | tf_op jit(solution)/shard_map/ppermute | solution.py:310
  42.3 3.1 %copy-start.20 = (bf16[2,96,256]{2,1,0:T(8,128)(2,1)}, bf16[2,96,256]{2,1,0:T(8,128)(2,1)S(1)}, u32[]{:S(2)}) copy-start(bf16[2,96,256]{2,1,0:T(8,128)(2,1)S(1)} %collective-permute-done.12.refs_4_) | copy-start | bytes 294916
  42.3 1.4 %collective-permute-start.17 = (bf16[384,256]{1,0:T(8,128)(2,1)S(1)}, bf16[384,256]{1,0:T(8,128)(2,1)S(1)}, u32[]{:S(2)}, u32[]{:S(2)}) collective-permute-start(bf16[384,256]{1,0:T(8,128)(2,1)S(1)} %collective-permute-done.2.refs_12_), channel_id=1, source_target_pairs={{0,2},{2,0},{4,6},{6,4},{8,10},{10,8},{12,14},{14,12},{16,18},{18,... | collective-permute-start | bytes 589832 | tf_op jit(solution)/shard_map/ppermute | solution.py:310
  42.4 3.1 %copy-start.9 = (bf16[384,256]{1,0:T(8,128)(2,1)}, bf16[384,256]{1,0:T(8,128)(2,1)S(1)}, u32[]{:S(2)}) copy-start(bf16[384,256]{1,0:T(8,128)(2,1)S(1)} %collective-permute-done.11.refs_20_) | copy-start | bytes 589828
  42.4 1.6 %collective-permute-start.18 = (bf16[384,256]{1,0:T(8,128)(2,1)S(1)}, bf16[384,256]{1,0:T(8,128)(2,1)S(1)}, u32[]{:S(2)}, u32[]{:S(2)}) collective-permute-start(bf16[384,256]{1,0:T(8,128)(2,1)S(1)} %collective-permute-done.4.refs_13_), channel_id=1, source_target_pairs={{0,2},{2,0},{4,6},{6,4},{8,10},{10,8},{12,14},{14,12},{16,18},{18,... | collective-permute-start | bytes 589832 | tf_op jit(solution)/shard_map/ppermute | solution.py:310
  42.9 2.6 %copy-start.10 = (bf16[384,256]{1,0:T(8,128)(2,1)}, bf16[384,256]{1,0:T(8,128)(2,1)S(1)}, u32[]{:S(2)}) copy-start(bf16[384,256]{1,0:T(8,128)(2,1)S(1)} %collective-permute-done.15.refs_10_) | copy-start | bytes 589828
  42.9 2.2 %collective-permute-start.19 = (bf16[384,256]{1,0:T(8,128)(2,1)S(1)}, bf16[384,256]{1,0:T(8,128)(2,1)S(1)}, u32[]{:S(2)}, u32[]{:S(2)}) collective-permute-start(bf16[384,256]{1,0:T(8,128)(2,1)S(1)} %collective-permute-done.7.refs_16_), channel_id=1, source_target_pairs={{0,2},{2,0},{4,6},{6,4},{8,10},{10,8},{12,14},{14,12},{16,18},{18,... | collective-permute-start | bytes 589832 | tf_op jit(solution)/shard_map/ppermute | solution.py:310
  43.0 2.6 %copy-start.11 = (bf16[384,256]{1,0:T(8,128)(2,1)}, bf16[384,256]{1,0:T(8,128)(2,1)S(1)}, u32[]{:S(2)}) copy-start(bf16[384,256]{1,0:T(8,128)(2,1)S(1)} %collective-permute-done.16.refs_11_) | copy-start | bytes 589828
  43.0 2.1 %collective-permute-start.20 = (bf16[384,256]{1,0:T(8,128)(2,1)S(1)}, bf16[384,256]{1,0:T(8,128)(2,1)S(1)}, u32[]{:S(2)}, u32[]{:S(2)}) collective-permute-start(bf16[384,256]{1,0:T(8,128)(2,1)S(1)} %collective-permute-done.8.refs_17_), channel_id=1, source_target_pairs={{0,2},{2,0},{4,6},{6,4},{8,10},{10,8},{12,14},{14,12},{16,18},{18,... | collective-permute-start | bytes 589832 | tf_op jit(solution)/shard_map/ppermute | solution.py:310
  43.4 2.1 %copy-start.18 = (bf16[2,144,256]{2,1,0:T(8,128)(2,1)}, bf16[2,144,256]{2,1,0:T(8,128)(2,1)S(1)}, u32[]{:S(2)}) copy-start(bf16[2,144,256]{2,1,0:T(8,128)(2,1)S(1)} %collective-permute-done.6.refs_1_) | copy-start | bytes 442372
  43.4 2.0 %collective-permute-start.21 = (bf16[384,256]{1,0:T(8,128)(2,1)S(1)}, bf16[384,256]{1,0:T(8,128)(2,1)S(1)}, u32[]{:S(2)}, u32[]{:S(2)}) collective-permute-start(bf16[384,256]{1,0:T(8,128)(2,1)S(1)} %collective-permute-done.11.refs_20_), channel_id=1, source_target_pairs={{0,2},{2,0},{4,6},{6,4},{8,10},{10,8},{12,14},{14,12},{16,18},{18,... | collective-permute-start | bytes 589832 | tf_op jit(solution)/shard_map/ppermute | solution.py:310
  43.8 1.8 %copy-start.12 = (bf16[384,256]{1,0:T(8,128)(2,1)}, bf16[384,256]{1,0:T(8,128)(2,1)S(1)}, u32[]{:S(2)}) copy-start(bf16[384,256]{1,0:T(8,128)(2,1)S(1)} %collective-permute-done.17.refs_14_) | copy-start | bytes 589828
  43.8 1.3 %collective-permute-start.10 = (bf16[2,96,256]{2,1,0:T(8,128)(2,1)S(1)}, bf16[2,96,256]{2,1,0:T(8,128)(2,1)S(1)}, u32[]{:S(2)}, u32[]{:S(2)}) collective-permute-start(bf16[2,96,256]{2,1,0:T(8,128)(2,1)S(1)} %collective-permute-done.9.refs_2_), channel_id=1, source_target_pairs={{0,2},{2,0},{4,6},{6,4},{8,10},{10,8},{12,14},{14,12},{16,18},{18,... | collective-permute-start | bytes 294920 | tf_op jit(solution)/shard_map/ppermute | solution.py:310
  44.1 1.5 %copy-start.13 = (bf16[384,256]{1,0:T(8,128)(2,1)}, bf16[384,256]{1,0:T(8,128)(2,1)S(1)}, u32[]{:S(2)}) copy-start(bf16[384,256]{1,0:T(8,128)(2,1)S(1)} %collective-permute-done.18.refs_15_) | copy-start | bytes 589828
  44.1 1.3 %collective-permute-start.13 = (bf16[2,96,256]{2,1,0:T(8,128)(2,1)S(1)}, bf16[2,96,256]{2,1,0:T(8,128)(2,1)S(1)}, u32[]{:S(2)}, u32[]{:S(2)}) collective-permute-start(bf16[2,96,256]{2,1,0:T(8,128)(2,1)S(1)} %collective-permute-done.12.refs_4_), channel_id=1, source_target_pairs={{0,2},{2,0},{4,6},{6,4},{8,10},{10,8},{12,14},{14,12},{16,18},{18,... | collective-permute-start | bytes 294920 | tf_op jit(solution)/shard_map/ppermute | solution.py:310
  45.1 0.6 copy-start.21
  45.1 0.7 copy-start.14
  45.1 0.8 copy-start.15
  45.4 0.6 copy-start.22
  45.4 0.7 copy-start.16

commit v7 on v5

--- a/solution.py
+++ b/solution.py
@@ -22,15 +22,12 @@
 
 
 def project_body(core_ref, *refs):
-    x_ref, gain_ref, bias_ref, weight_ref, pbias_ref = refs[6:11]
-    out_ref, sems = refs[5], refs[11]
-    copies = [pltpu.make_async_copy(refs[i], refs[6 + i], sems.at[i]) for i in range(5)]
-    for copy in copies:
-        copy.start()
-    for copy in copies:
-        copy.wait()
-    local, _, _ = x_ref.shape
+    x_ref, weight_ref, vectors_ref, out_ref = refs
+    local, _, channels = x_ref.shape
     width = weight_ref.shape[0]
+    gain = vectors_ref[:, :channels]
+    bias = vectors_ref[:, channels : 2 * channels]
+    pbias = vectors_ref[:, 2 * channels :]
     group = 2 * local
     lanes = width * group
     first = core_ref[0] * local
@@ -38,11 +35,11 @@
     lane = lax.broadcasted_iota(jnp.int32, (width, lanes), 1)
     total = None
     for s in range(local):
-        normed = norm_rows(x_ref[s].astype(F32), gain_ref[...], bias_ref[...]).astype(BF16)
+        normed = norm_rows(x_ref[s].astype(F32), gain, bias).astype(BF16)
         y = lax.dot_general(
             normed, weight_ref[...], (((1,), (1,)), ((), ())), preferred_element_type=F32
         )
-        y = y + pbias_ref[...]
+        y = y + pbias
         spread = (lane == ch * group + (first + s)).astype(F32).astype(BF16)
         part = jnp.dot(y.astype(BF16), spread, preferred_element_type=F32)
         total = part if total is None else total + part
@@ -55,20 +52,17 @@
     return pl.BlockSpec(a.shape, lambda i: (0,) * len(a.shape))
 
 
-def project(core, x, gain, bias, weight, pbias):
+def project(core, x, weight, vectors):
     local, residues, _ = x.shape
     lanes = weight.shape[0] * local
-    operands = (x, gain, bias, weight, pbias)
+    vmem = pl.BlockSpec(memory_space=pltpu.VMEM)
     return pl.pallas_call(
         project_body,
-        in_specs=[pl.BlockSpec(memory_space=pltpu.SMEM)]
-        + [pl.BlockSpec(memory_space=pltpu.HBM)] * 5,
-        out_specs=pl.BlockSpec(memory_space=pltpu.VMEM),
+        in_specs=[pl.BlockSpec(memory_space=pltpu.SMEM)] + [vmem] * 3,
+        out_specs=vmem,
         out_shape=jax.ShapeDtypeStruct((2, residues, lanes), BF16),
-        scratch_shapes=[pltpu.VMEM(a.shape, a.dtype) for a in operands]
-        + [pltpu.SemaphoreType.DMA((5,))],
         compiler_params=pltpu.CompilerParams(vmem_limit_bytes=32 << 20),
-    )(core, *operands)
+    )(core, x, weight, vectors)
 
 
 def power_of_two(largest):
@@ -143,6 +137,18 @@
             lhs_scr[q, :, side * lanes : (side + 1) * lanes] = both
 
 
+def row_places(chips, refs, row_length):
+    if len(refs) == 1:
+        return [(refs[0].at[q], q, 0, False) for q in range(chips)]
+    first, first_other, later, later_other, far = refs
+    places = [(first, 0, 0, False)]
+    for skip, pair in ((row_length, (first, first_other)), (0, (later, later_other))):
+        for k in range((pair[0].shape[1] - skip) // (2 * row_length)):
+            for r in pair:
+                places.append((r, len(places), skip + 2 * k * row_length, True))
+    return places + [(far, chips - 1, 0, False)]
+
+
 def pair_body(chips, here, group, row_parts, place_ref, *refs):
     there_refs = refs[:row_parts]
     refs = refs[row_parts:]
@@ -189,10 +195,13 @@
 
         @pl.when(place_ref[1] == 0)
         def _():
-            blocks = [(r, q) for r in there_refs for q in range(r.shape[0])]
-            for i, (r, q) in enumerate(blocks):
+            for r, i, skip, core_rows in row_places(chips, there_refs, row_length):
+                if core_rows:
+                    skip = pl.multiple_of(skip + place_ref[0] * row_length, row_length)
                 for side in range(2):
-                    x_scr[side, i * row_length : (i + 1) * row_length, :] = r[q, side]
+                    x_scr[side, i * row_length : (i + 1) * row_length, :] = r[
+                        side, pl.ds(skip, row_length), :
+                    ]
 
         split_weight(chips * group, w_out_ref, w_ref, undo_ref, w_scr)
         prepare_rows(chips, group, x_scr, undo_ref, y_scr, lhs_scr, undo_scr)
@@ -228,11 +237,10 @@
         out_ref[g] = (pair + update + b_down_ref[...]).astype(BF16)
 
 
-def pair_kernel(place, group, rows, cols, rest):
+def pair_kernel(place, group, row_length, rows, cols, rest):
     own = cols[0]
     _, column_length, part = own.shape
     chips = (len(cols) + 1) // 2
-    row_length = rows[0].shape[2]
     zc = rest[1].shape[1]
     here = math.gcd(row_length, 8)
     depth = chips * part
@@ -305,14 +313,8 @@
 
     ring = [(src, r) for r, src in enumerate(ring_source(chips))]
 
-    mine = project(
-        core.reshape(1),
-        alignment,
-        alignment_norm_gain[None],
-        alignment_norm_bias[None],
-        projection_weight.T,
-        projection_bias_pair[None],
-    )
+    vectors = jnp.concatenate([alignment_norm_gain, alignment_norm_bias, projection_bias_pair])
+    mine = project(core.reshape(1), alignment, projection_weight.T, vectors[None])
     own = mine + swap(mine)
 
     per_col = column_length // row_length
@@ -329,6 +331,8 @@
     cols = [own]
     steps = chips // 2 - 1
     two = col_count == 2
+    is_here = (source == col_index).astype(core.dtype) if two else jnp.zeros_like(core)
+    place = jnp.stack([core, is_here, row_index % per_col])
     if two:
         targets = [row_count - 2 - r + 2 * (r % 2) for r in range(row_count)]
         first = (row_count - 2 - row_index + 2 * core) % per_col * row_length
@@ -338,36 +342,43 @@
             [(2 * r + t // per_col, 2 * t + 1 - t // per_col) for r, t in enumerate(targets)],
         )
     blocks = [cut((right, left), start, row_length)]
+    later = []
+    pair_start = start - core * row_length
     for d in range(steps):
         right = lax.ppermute(right, "row", ring)
         left = lax.ppermute(left, "row", ring)
+        if two:
+            if d == 1:
+                right, left, far_rows, place = lax.optimization_barrier(
+                    (right, left, far_rows, place)
+                )
+            if d == steps - 1 and d > 1:
+                right, left, early = lax.optimization_barrier((right, left, early))
+            both = cut((right, left), pair_start, 2 * row_length)
+            later.append(both)
+            if d == steps - 2:
+                early = across(jnp.concatenate([blocks[0], *later], axis=1))
+                later = []
         other = (swap(right), swap(left))
         cols.extend([right, left, *other])
-        if d < steps - 1 or not two:
+        if not two:
             blocks.extend([cut(pair, start, row_length) for pair in ((right, left), other)])
-        if d == steps - 2 and two:
-            rows = [across(jnp.stack(blocks))]
     far = lax.ppermute(jnp.where(core == 0, right, left), "row", ring)
     if two:
-        both = across(cut((right, left), start - core * row_length, 2 * row_length))
-        far, both = lax.optimization_barrier((far, both))
-        kept = lax.dynamic_slice_in_dim(both, core * row_length, row_length, 1)
-        given = lax.dynamic_slice_in_dim(both, (1 - core) * row_length, row_length, 1)
-        rows.extend([kept[None], swap(given)[None], far_rows[None]])
+        late = across(jnp.concatenate(later, axis=1))
+        early_other = swap(early)
+        far, late, early_other = lax.optimization_barrier((far, late, early_other))
+        rows = [early, early_other, late, swap(late), far_rows]
     far_other = swap(far)
     cols.extend([far, far_other])
-    is_here = (source == col_index).astype(core.dtype)
     if not two:
         a = lax.dynamic_slice_in_dim(far, start, row_length, 0)
         b = lax.dynamic_slice_in_dim(far_other, start, row_length, 0)
         blocks.append(jnp.stack([jnp.where(core == 0, a, b), jnp.where(core == 0, b, a)]))
         gathered = lax.all_gather(jnp.stack(blocks), "col")
         rows = [lax.dynamic_index_in_dim(gathered, source, 0, False)]
-        is_here = jnp.zeros_like(is_here)
-
-    place = jnp.stack([core, is_here, row_index % per_col])
     rest = (w_out, b_out[None], pair_gain[None], pair_bias[None], w_up, b_up[None], w_down)
-    return pair_kernel(place, 2 * local, rows, cols, rest + (b_down[None],))
+    return pair_kernel(place, 2 * local, row_length, rows, cols, rest + (b_down[None],))
 
 
 def solution(mesh):

time: 87.7 us -> 87.4 us (level)
  the two profiles are of different devices: /device:TPU:3 before, /device:TPU:0 now
where the time goes in v7:
time: 87.4 us; the launch traced here: 87.2 us
  Pallas kernels  46.3 us (53%)
  starting transfers between devices  18.2 us (21%)
  waiting for transfers between devices  18.1 us (21%)
  local copies, waits for them, and re-layouts  2.6 us (3%)
  other arithmetic  1.47 us (2%)
    pallas_call x1, Pallas kernels, pair_kernel(): pl.pallas_call(functools.partial(pair_body, chips, here, group, len(rows)...  45.1 us
    ppermute x3, waiting for transfers between devices, shards(): right = lax.ppermute(right, 'row', ring)  6.92 us
    ppermute x3, starting transfers between devices, shards(): left = lax.ppermute(left, 'row', ring)  5.18 us
    ppermute x3, starting transfers between devices, shards(): right = lax.ppermute(right, 'row', ring)  5.07 us
    ppermute x2, starting transfers between devices, across(): return lax.ppermute(block, 'col', [(0, 1), (1, 0)])  4.85 us
    ppermute x2, waiting for transfers between devices, across(): return lax.ppermute(block, 'col', [(0, 1), (1, 0)])  4.62 us
    ppermute x3, waiting for transfers between devices, shards(): left = lax.ppermute(left, 'row', ring)  4.24 us
    unnamed x44, local copies, waits for them, and re-layouts  2.49 us
  transfers between devices with their start and end apart: 20, of which 13 were waited for; matrix products, arithmetic and copies ran while one was open for 1% of the time, Pallas kernels for 0%

profile of v7, /device:TPU:0, one launch (start us, length us, event | category | flops | bytes accessed | tf_op | source)
XLA Modules:
  0.0 87.2 jit_solution(14912615147459235558)
XLA Ops:
  0.0 0.7 pad_maximum_fusion.1
  0.7 0.0 copy-start
  0.7 1.1 %copy-done = bf16[4,384,256]{2,1,0:T(8,128)(2,1)S(1)} copy-done((bf16[4,384,256]{2,1,0:T(8,128)(2,1)S(1)}, bf16[4,384,256]{2,1,0:T(8,128)(2,1)}, u32[]{:S(2)}) %copy-start) | copy-done | bytes 786456
  1.9 0.8 copy-done.1
  2.6 1.2 %shard_map.127 = bf16[2,384,256]{2,1,0:T(8,128)(2,1)S(1)} custom-call(s32[1]{0:T(128)} %bitcast.core_ref, bf16[4,384,256]{2,1,0:T(8,128)(2,1)S(1)} %copy-done, bf16[64,256]{1,0:T(8,128)(2,1)S(1)} %bitcast.25, f32[1,576]{1,0:T(1,128)S(1)} %broadcast_in_dim.18.refs_2_), custom_call_target="tpu_custom_call" | custom-call | tf_op jit(solution)/shard_map/pallas_call | solution.py:59
  3.8 0.5 collective-permute-start
  4.3 0.6 pad_add_fusion.place_ref
  4.9 0.8 collective-permute-done
  5.7 0.1 add.34.refs_5_
  5.8 0.0 copy-start.2
  5.8 0.1 fusion
  5.8 3.0 %collective-permute-start.1 = (bf16[384,256]{1,0:T(8,128)(2,1)S(1)}, bf16[384,256]{1,0:T(8,128)(2,1)S(1)}, u32[]{:S(2)}, u32[]{:S(2)}) collective-permute-start(bf16[384,256]{1,0:T(8,128)(2,1)S(1)} %get-tuple-element.26), channel_id=1, source_target_pairs={{4,0},{10,2},{12,4},{2,6},{0,8},{18,10},{20,12},{6,14},{8,16},{26,... | collective-permute-start | bytes 589832 | tf_op jit(solution)/shard_map/ppermute | solution.py:348
  8.8 1.6 %collective-permute-start.3 = (bf16[384,256]{1,0:T(8,128)(2,1)S(1)}, bf16[384,256]{1,0:T(8,128)(2,1)S(1)}, u32[]{:S(2)}, u32[]{:S(2)}) collective-permute-start(bf16[384,256]{1,0:T(8,128)(2,1)S(1)} %get-tuple-element.27), channel_id=1, source_target_pairs={{4,0},{10,2},{12,4},{2,6},{0,8},{18,10},{20,12},{6,14},{8,16},{26,... | collective-permute-start | bytes 589832 | tf_op jit(solution)/shard_map/ppermute | solution.py:349
  10.4 0.7 collective-permute-start.5
  11.1 1.3 %collective-permute-done.1.refs_6_ = bf16[384,256]{1,0:T(8,128)(2,1)S(1)} collective-permute-done((bf16[384,256]{1,0:T(8,128)(2,1)S(1)}, bf16[384,256]{1,0:T(8,128)(2,1)S(1)}, u32[]{:S(2)}, u32[]{:S(2)}) %collective-permute-start.1) | collective-permute-done | bytes 196640 | tf_op jit(solution)/shard_map/ppermute | solution.py:348
  12.4 2.1 %collective-permute-start.2 = (bf16[384,256]{1,0:T(8,128)(2,1)S(1)}, bf16[384,256]{1,0:T(8,128)(2,1)S(1)}, u32[]{:S(2)}, u32[]{:S(2)}) collective-permute-start(bf16[384,256]{1,0:T(8,128)(2,1)S(1)} %collective-permute-done.1.refs_6_), channel_id=1, source_target_pairs={{4,0},{10,2},{12,4},{2,6},{0,8},{18,10},{20,12},{6,14},{8,16},{26,... | collective-permute-start | bytes 589832 | tf_op jit(solution)/shard_map/ppermute | solution.py:348
  14.5 0.0 collective-permute-done.3.refs_7_
  14.5 2.1 %collective-permute-start.4 = (bf16[384,256]{1,0:T(8,128)(2,1)S(1)}, bf16[384,256]{1,0:T(8,128)(2,1)S(1)}, u32[]{:S(2)}, u32[]{:S(2)}) collective-permute-start(bf16[384,256]{1,0:T(8,128)(2,1)S(1)} %collective-permute-done.3.refs_7_), channel_id=1, source_target_pairs={{4,0},{10,2},{12,4},{2,6},{0,8},{18,10},{20,12},{6,14},{8,16},{26,... | collective-permute-start | bytes 589832 | tf_op jit(solution)/shard_map/ppermute | solution.py:349
  16.6 0.0 collective-permute-done.5.refs_4_
  16.6 0.0 copy-start.21
  16.6 1.5 %collective-permute-done.2.refs_10_ = bf16[384,256]{1,0:T(8,128)(2,1)S(1)} collective-permute-done((bf16[384,256]{1,0:T(8,128)(2,1)S(1)}, bf16[384,256]{1,0:T(8,128)(2,1)S(1)}, u32[]{:S(2)}, u32[]{:S(2)}) %collective-permute-start.2) | collective-permute-done | bytes 196640 | tf_op jit(solution)/shard_map/ppermute | solution.py:348
  18.1 2.1 %collective-permute-done.4.refs_11_ = bf16[384,256]{1,0:T(8,128)(2,1)S(1)} collective-permute-done((bf16[384,256]{1,0:T(8,128)(2,1)S(1)}, bf16[384,256]{1,0:T(8,128)(2,1)S(1)}, u32[]{:S(2)}, u32[]{:S(2)}) %collective-permute-start.4) | collective-permute-done | bytes 196640 | tf_op jit(solution)/shard_map/ppermute | solution.py:349
  20.3 4.7 %collective-permute-start.8 = (bf16[2,240,256]{2,1,0:T(8,128)(2,1)S(1)}, bf16[2,240,256]{2,1,0:T(8,128)(2,1)S(1)}, u32[]{:S(2)}, u32[]{:S(2)}) collective-permute-start(bf16[2,240,256]{2,1,0:T(8,128)(2,1)S(1)} %maximum_maximum_fusion), channel_id=1, source_target_pairs={{0,1},{1,0},{2,3},{3,2},{4,5},{5,4},{6,7},{7,6},{8,9},{9,8},{10,11... | collective-permute-start | bytes 737288 | tf_op jit(solution)/shard_map/ppermute | solution.py:328
  25.0 0.0 collective-permute-start.6
  25.0 1.5 %collective-permute-start.7 = (bf16[384,256]{1,0:T(8,128)(2,1)S(1)}, bf16[384,256]{1,0:T(8,128)(2,1)S(1)}, u32[]{:S(2)}, u32[]{:S(2)}) collective-permute-start(bf16[384,256]{1,0:T(8,128)(2,1)S(1)} %collective-permute-done.4.refs_11_), channel_id=1, source_target_pairs={{4,0},{10,2},{12,4},{2,6},{0,8},{18,10},{20,12},{6,14},{8,16},{26,... | collective-permute-start | bytes 589832 | tf_op jit(solution)/shard_map/ppermute | solution.py:349
  26.5 0.0 collective-permute-start.13
  26.5 4.1 %collective-permute-done.6.refs_14_ = bf16[384,256]{1,0:T(8,128)(2,1)S(1)} collective-permute-done((bf16[384,256]{1,0:T(8,128)(2,1)S(1)}, bf16[384,256]{1,0:T(8,128)(2,1)S(1)}, u32[]{:S(2)}, u32[]{:S(2)}) %collective-permute-start.6) | collective-permute-done | bytes 196640 | tf_op jit(solution)/shard_map/ppermute | solution.py:348
  30.7 2.1 %collective-permute-done.7.refs_15_ = bf16[384,256]{1,0:T(8,128)(2,1)S(1)} collective-permute-done((bf16[384,256]{1,0:T(8,128)(2,1)S(1)}, bf16[384,256]{1,0:T(8,128)(2,1)S(1)}, u32[]{:S(2)}, u32[]{:S(2)}) %collective-permute-start.7) | collective-permute-done | bytes 196640 | tf_op jit(solution)/shard_map/ppermute | solution.py:349
  32.8 0.0 collective-permute-done.8.refs_0_
  32.8 0.2 collective-permute-start.9
  33.1 0.1 collective-permute-start.11
  33.2 0.1 collective-permute-start.10
  33.3 0.5 collective-permute-start.14
  33.8 4.6 %collective-permute-done.10.refs_2_ = bf16[2,96,256]{2,1,0:T(8,128)(2,1)S(1)} collective-permute-done((bf16[2,96,256]{2,1,0:T(8,128)(2,1)S(1)}, bf16[2,96,256]{2,1,0:T(8,128)(2,1)S(1)}, u32[]{:S(2)}, u32[]{:S(2)}) %collective-permute-start.10) | collective-permute-done | bytes 98336 | tf_op jit(solution)/shard_map/ppermute | solution.py:328
  38.4 0.0 collective-permute-start.15
  38.4 0.3 collective-permute-done.9.refs_18_
  38.7 0.2 collective-permute-start.16
  39.0 0.0 collective-permute-done.11.refs_1_
  39.0 0.3 collective-permute-start.17
  39.3 0.0 collective-permute-done.13.refs_8_
  39.3 0.2 collective-permute-start.18
  39.5 0.0 collective-permute-done.14.refs_9_
  39.5 0.3 collective-permute-start.19
  39.8 0.1 collective-permute-done.15.refs_12_
  39.9 0.1 collective-permute-start.12
  40.0 0.2 collective-permute-done.16.refs_13_
  40.2 0.3 collective-permute-done.17.refs_16_
  40.5 0.3 collective-permute-done.18.refs_17_
  40.7 0.4 collective-permute-done.12.refs_3_
  41.2 0.0 collective-permute-done.19.refs_19_
  41.2 0.0 copy-done.2
  41.2 0.0 copy-done.5
  41.2 0.0 copy-done.6
  41.2 0.0 copy-done.21
  41.2 0.0 copy-done.7
  41.2 0.0 copy-done.8
  41.2 0.0 copy-done.3
  41.3 0.0 copy-done.4
  41.3 0.0 copy-done.9
  41.3 0.0 copy-done.19
  41.4 0.1 copy-done.17
  41.4 0.4 copy-done.20
  41.8 0.1 copy-done.18
  41.9 45.1 %shard_map.128 = bf16[48,384,128]{2,1,0:T(8,128)(2,1)} custom-call(s32[3]{0:T(128)} %pad_add_fusion.place_ref, bf16[2,240,256]{2,1,0:T(8,128)(2,1)} %copy-done.9, bf16[2,240,256]{2,1,0:T(8,128)(2,1)} %copy-done.10, bf16[2,96,256]{2,1,0:T(8,128)(2,1)} %copy-done.19, bf16[2,96,256]{2,1,0:T(8,128)(2,1)} %copy-done.20, bf16[2,48,256]{2,1,0:T(8,128)(2,1)} %copy-done.21, ...), custom_call_target="tpu_custom_call" | custom-call | tf_op jit(solution)/shard_map/pallas_call | solution.py:249
  (37 shorter events, 0.2 us)
Async XLA Ops:
  0.7 1.1 %copy-start = (bf16[4,384,256]{2,1,0:T(8,128)(2,1)S(1)}, bf16[4,384,256]{2,1,0:T(8,128)(2,1)}, u32[]{:S(2)}) copy-start(bf16[4,384,256]{2,1,0:T(8,128)(2,1)} %refs_0_.1) | copy-start | bytes 2359300
  1.9 0.8 copy-start.1
  3.8 1.9 %collective-permute-start = (bf16[2,384,256]{2,1,0:T(8,128)(2,1)S(1)}, bf16[2,384,256]{2,1,0:T(8,128)(2,1)S(1)}, u32[]{:S(2)}, u32[]{:S(2)}) collective-permute-start(bf16[2,384,256]{2,1,0:T(8,128)(2,1)S(1)} %shard_map.127), channel_id=1, source_target_pairs={{0,2},{2,0},{4,6},{6,4},{8,10},{10,8},{12,14},{14,12},{16,18},{18,... | collective-permute-start | bytes 1179656 | tf_op jit(solution)/shard_map/ppermute | solution.py:312
  5.8 35.4 %copy-start.2 = (bf16[2,384,256]{2,1,0:T(8,128)(2,1)}, bf16[2,384,256]{2,1,0:T(8,128)(2,1)S(1)}, u32[]{:S(2)}) copy-start(bf16[2,384,256]{2,1,0:T(8,128)(2,1)S(1)} %add.34.refs_5_) | copy-start | bytes 1179652
  5.8 6.6 %collective-permute-start.1 = (bf16[384,256]{1,0:T(8,128)(2,1)S(1)}, bf16[384,256]{1,0:T(8,128)(2,1)S(1)}, u32[]{:S(2)}, u32[]{:S(2)}) collective-permute-start(bf16[384,256]{1,0:T(8,128)(2,1)S(1)} %get-tuple-element.26), channel_id=1, source_target_pairs={{4,0},{10,2},{12,4},{2,6},{0,8},{18,10},{20,12},{6,14},{8,16},{26,... | collective-permute-start | bytes 589832 | tf_op jit(solution)/shard_map/ppermute | solution.py:348
  8.8 5.7 %collective-permute-start.3 = (bf16[384,256]{1,0:T(8,128)(2,1)S(1)}, bf16[384,256]{1,0:T(8,128)(2,1)S(1)}, u32[]{:S(2)}, u32[]{:S(2)}) collective-permute-start(bf16[384,256]{1,0:T(8,128)(2,1)S(1)} %get-tuple-element.27), channel_id=1, source_target_pairs={{4,0},{10,2},{12,4},{2,6},{0,8},{18,10},{20,12},{6,14},{8,16},{26,... | collective-permute-start | bytes 589832 | tf_op jit(solution)/shard_map/ppermute | solution.py:349
  10.4 6.2 %collective-permute-start.5 = (bf16[2,48,256]{2,1,0:T(8,128)(2,1)S(1)}, bf16[2,48,256]{2,1,0:T(8,128)(2,1)S(1)}, u32[]{:S(2)}, u32[]{:S(2)}) collective-permute-start(bf16[2,48,256]{2,1,0:T(8,128)(2,1)S(1)} %constant_dynamic-slice_fusion.2), channel_id=1, source_target_pairs={{1,28},{3,30},{5,24},{7,26},{9,20},{11,22},{13,16},{15,18},{16,13}... | collective-permute-start | bytes 147464 | tf_op jit(solution)/shard_map/ppermute | solution.py:339
  12.4 28.8 %copy-start.5 = (bf16[384,256]{1,0:T(8,128)(2,1)}, bf16[384,256]{1,0:T(8,128)(2,1)S(1)}, u32[]{:S(2)}) copy-start(bf16[384,256]{1,0:T(8,128)(2,1)S(1)} %collective-permute-done.1.refs_6_) | copy-start | bytes 589828
  12.4 5.7 %collective-permute-start.2 = (bf16[384,256]{1,0:T(8,128)(2,1)S(1)}, bf16[384,256]{1,0:T(8,128)(2,1)S(1)}, u32[]{:S(2)}, u32[]{:S(2)}) collective-permute-start(bf16[384,256]{1,0:T(8,128)(2,1)S(1)} %collective-permute-done.1.refs_6_), channel_id=1, source_target_pairs={{4,0},{10,2},{12,4},{2,6},{0,8},{18,10},{20,12},{6,14},{8,16},{26,... | collective-permute-start | bytes 589832 | tf_op jit(solution)/shard_map/ppermute | solution.py:348
  14.5 26.7 %copy-start.6 = (bf16[384,256]{1,0:T(8,128)(2,1)}, bf16[384,256]{1,0:T(8,128)(2,1)S(1)}, u32[]{:S(2)}) copy-start(bf16[384,256]{1,0:T(8,128)(2,1)S(1)} %collective-permute-done.3.refs_7_) | copy-start | bytes 589828
  14.5 5.7 %collective-permute-start.4 = (bf16[384,256]{1,0:T(8,128)(2,1)S(1)}, bf16[384,256]{1,0:T(8,128)(2,1)S(1)}, u32[]{:S(2)}, u32[]{:S(2)}) collective-permute-start(bf16[384,256]{1,0:T(8,128)(2,1)S(1)} %collective-permute-done.3.refs_7_), channel_id=1, source_target_pairs={{4,0},{10,2},{12,4},{2,6},{0,8},{18,10},{20,12},{6,14},{8,16},{26,... | collective-permute-start | bytes 589832 | tf_op jit(solution)/shard_map/ppermute | solution.py:349
  16.6 24.6 %copy-start.21 = (bf16[2,48,256]{2,1,0:T(8,128)(2,1)}, bf16[2,48,256]{2,1,0:T(8,128)(2,1)S(1)}, u32[]{:S(2)}) copy-start(bf16[2,48,256]{2,1,0:T(8,128)(2,1)S(1)} %collective-permute-done.5.refs_4_) | copy-start | bytes 147460
  18.1 23.1 %copy-start.7 = (bf16[384,256]{1,0:T(8,128)(2,1)}, bf16[384,256]{1,0:T(8,128)(2,1)S(1)}, u32[]{:S(2)}) copy-start(bf16[384,256]{1,0:T(8,128)(2,1)S(1)} %collective-permute-done.2.refs_10_) | copy-start | bytes 589828
  20.2 21.0 %copy-start.8 = (bf16[384,256]{1,0:T(8,128)(2,1)}, bf16[384,256]{1,0:T(8,128)(2,1)S(1)}, u32[]{:S(2)}) copy-start(bf16[384,256]{1,0:T(8,128)(2,1)S(1)} %collective-permute-done.4.refs_11_) | copy-start | bytes 589828
  20.3 12.5 %collective-permute-start.8 = (bf16[2,240,256]{2,1,0:T(8,128)(2,1)S(1)}, bf16[2,240,256]{2,1,0:T(8,128)(2,1)S(1)}, u32[]{:S(2)}, u32[]{:S(2)}) collective-permute-start(bf16[2,240,256]{2,1,0:T(8,128)(2,1)S(1)} %maximum_maximum_fusion), channel_id=1, source_target_pairs={{0,1},{1,0},{2,3},{3,2},{4,5},{5,4},{6,7},{7,6},{8,9},{9,8},{10,11... | collective-permute-start | bytes 737288 | tf_op jit(solution)/shard_map/ppermute | solution.py:328
  25.0 5.7 %collective-permute-start.6 = (bf16[384,256]{1,0:T(8,128)(2,1)S(1)}, bf16[384,256]{1,0:T(8,128)(2,1)S(1)}, u32[]{:S(2)}, u32[]{:S(2)}) collective-permute-start(bf16[384,256]{1,0:T(8,128)(2,1)S(1)} %collective-permute-done.2.refs_10_), channel_id=1, source_target_pairs={{4,0},{10,2},{12,4},{2,6},{0,8},{18,10},{20,12},{6,14},{8,16},{26,... | collective-permute-start | bytes 589832 | tf_op jit(solution)/shard_map/ppermute | solution.py:348
  25.0 7.8 %collective-permute-start.7 = (bf16[384,256]{1,0:T(8,128)(2,1)S(1)}, bf16[384,256]{1,0:T(8,128)(2,1)S(1)}, u32[]{:S(2)}, u32[]{:S(2)}) collective-permute-start(bf16[384,256]{1,0:T(8,128)(2,1)S(1)} %collective-permute-done.4.refs_11_), channel_id=1, source_target_pairs={{4,0},{10,2},{12,4},{2,6},{0,8},{18,10},{20,12},{6,14},{8,16},{26,... | collective-permute-start | bytes 589832 | tf_op jit(solution)/shard_map/ppermute | solution.py:349
  26.5 12.7 %collective-permute-start.13 = (bf16[384,256]{1,0:T(8,128)(2,1)S(1)}, bf16[384,256]{1,0:T(8,128)(2,1)S(1)}, u32[]{:S(2)}, u32[]{:S(2)}) collective-permute-start(bf16[384,256]{1,0:T(8,128)(2,1)S(1)} %collective-permute-done.1.refs_6_), channel_id=1, source_target_pairs={{0,2},{2,0},{4,6},{6,4},{8,10},{10,8},{12,14},{14,12},{16,18},{18,... | collective-permute-start | bytes 589832 | tf_op jit(solution)/shard_map/ppermute | solution.py:312
  30.6 10.6 %copy-start.3 = (bf16[384,256]{1,0:T(8,128)(2,1)}, bf16[384,256]{1,0:T(8,128)(2,1)S(1)}, u32[]{:S(2)}) copy-start(bf16[384,256]{1,0:T(8,128)(2,1)S(1)} %collective-permute-done.6.refs_14_) | copy-start | bytes 589828
  32.8 8.5 %copy-start.4 = (bf16[384,256]{1,0:T(8,128)(2,1)}, bf16[384,256]{1,0:T(8,128)(2,1)S(1)}, u32[]{:S(2)}) copy-start(bf16[384,256]{1,0:T(8,128)(2,1)S(1)} %collective-permute-done.7.refs_15_) | copy-start | bytes 589828
  32.8 8.5 %copy-start.9 = (bf16[2,240,256]{2,1,0:T(8,128)(2,1)}, bf16[2,240,256]{2,1,0:T(8,128)(2,1)S(1)}, u32[]{:S(2)}) copy-start(bf16[2,240,256]{2,1,0:T(8,128)(2,1)S(1)} %collective-permute-done.8.refs_0_) | copy-start | bytes 737284
  32.8 5.9 %collective-permute-start.9 = (bf16[384,256]{1,0:T(8,128)(2,1)S(1)}, bf16[384,256]{1,0:T(8,128)(2,1)S(1)}, u32[]{:S(2)}, u32[]{:S(2)}) collective-permute-start(bf16[384,256]{1,0:T(8,128)(2,1)S(1)} %broadcast_select_fusion), channel_id=1, source_target_pairs={{4,0},{10,2},{12,4},{2,6},{0,8},{18,10},{20,12},{6,14},{8,16},{26,... | collective-permute-start | bytes 589832 | tf_op jit(solution)/shard_map/ppermute | solution.py:366
  33.1 5.9 %collective-permute-start.11 = (bf16[2,240,256]{2,1,0:T(8,128)(2,1)S(1)}, bf16[2,240,256]{2,1,0:T(8,128)(2,1)S(1)}, u32[]{:S(2)}, u32[]{:S(2)}) collective-permute-start(bf16[2,240,256]{2,1,0:T(8,128)(2,1)S(1)} %collective-permute-done.8.refs_0_), channel_id=1, source_target_pairs={{0,2},{2,0},{4,6},{6,4},{8,10},{10,8},{12,14},{14,12},{16,18},{18,... | collective-permute-start | bytes 737288 | tf_op jit(solution)/shard_map/ppermute | solution.py:312
  33.2 5.3 %collective-permute-start.10 = (bf16[2,96,256]{2,1,0:T(8,128)(2,1)S(1)}, bf16[2,96,256]{2,1,0:T(8,128)(2,1)S(1)}, u32[]{:S(2)}, u32[]{:S(2)}) collective-permute-start(bf16[2,96,256]{2,1,0:T(8,128)(2,1)S(1)} %pad_maximum_fusion), channel_id=1, source_target_pairs={{0,1},{1,0},{2,3},{3,2},{4,5},{5,4},{6,7},{7,6},{8,9},{9,8},{10,11... | collective-permute-start | bytes 294920 | tf_op jit(solution)/shard_map/ppermute | solution.py:328
  33.3 6.2 %collective-permute-start.14 = (bf16[384,256]{1,0:T(8,128)(2,1)S(1)}, bf16[384,256]{1,0:T(8,128)(2,1)S(1)}, u32[]{:S(2)}, u32[]{:S(2)}) collective-permute-start(bf16[384,256]{1,0:T(8,128)(2,1)S(1)} %collective-permute-done.3.refs_7_), channel_id=1, source_target_pairs={{0,2},{2,0},{4,6},{6,4},{8,10},{10,8},{12,14},{14,12},{16,18},{18,... | collective-permute-start | bytes 589832 | tf_op jit(solution)/shard_map/ppermute | solution.py:312
  38.4 2.8 %copy-start.19 = (bf16[2,96,256]{2,1,0:T(8,128)(2,1)}, bf16[2,96,256]{2,1,0:T(8,128)(2,1)S(1)}, u32[]{:S(2)}) copy-start(bf16[2,96,256]{2,1,0:T(8,128)(2,1)S(1)} %collective-permute-done.10.refs_2_) | copy-start | bytes 294916
  38.4 1.4 %collective-permute-start.15 = (bf16[384,256]{1,0:T(8,128)(2,1)S(1)}, bf16[384,256]{1,0:T(8,128)(2,1)S(1)}, u32[]{:S(2)}, u32[]{:S(2)}) collective-permute-start(bf16[384,256]{1,0:T(8,128)(2,1)S(1)} %collective-permute-done.2.refs_10_), channel_id=1, source_target_pairs={{0,2},{2,0},{4,6},{6,4},{8,10},{10,8},{12,14},{14,12},{16,18},{18,... | collective-permute-start | bytes 589832 | tf_op jit(solution)/shard_map/ppermute | solution.py:312
  38.7 2.6 %copy-start.12 = (bf16[384,256]{1,0:T(8,128)(2,1)}, bf16[384,256]{1,0:T(8,128)(2,1)S(1)}, u32[]{:S(2)}) copy-start(bf16[384,256]{1,0:T(8,128)(2,1)S(1)} %collective-permute-done.9.refs_18_) | copy-start | bytes 589828
  38.7 1.4 %collective-permute-start.16 = (bf16[384,256]{1,0:T(8,128)(2,1)S(1)}, bf16[384,256]{1,0:T(8,128)(2,1)S(1)}, u32[]{:S(2)}, u32[]{:S(2)}) collective-permute-start(bf16[384,256]{1,0:T(8,128)(2,1)S(1)} %collective-permute-done.4.refs_11_), channel_id=1, source_target_pairs={{0,2},{2,0},{4,6},{6,4},{8,10},{10,8},{12,14},{14,12},{16,18},{18,... | collective-permute-start | bytes 589832 | tf_op jit(solution)/shard_map/ppermute | solution.py:312
  39.0 2.3 %copy-start.10 = (bf16[2,240,256]{2,1,0:T(8,128)(2,1)}, bf16[2,240,256]{2,1,0:T(8,128)(2,1)S(1)}, u32[]{:S(2)}) copy-start(bf16[2,240,256]{2,1,0:T(8,128)(2,1)S(1)} %collective-permute-done.11.refs_1_) | copy-start | bytes 737284
  39.0 1.5 %collective-permute-start.17 = (bf16[384,256]{1,0:T(8,128)(2,1)S(1)}, bf16[384,256]{1,0:T(8,128)(2,1)S(1)}, u32[]{:S(2)}, u32[]{:S(2)}) collective-permute-start(bf16[384,256]{1,0:T(8,128)(2,1)S(1)} %collective-permute-done.6.refs_14_), channel_id=1, source_target_pairs={{0,2},{2,0},{4,6},{6,4},{8,10},{10,8},{12,14},{14,12},{16,18},{18,... | collective-permute-start | bytes 589832 | tf_op jit(solution)/shard_map/ppermute | solution.py:312
  39.3 2.1 %copy-start.11 = (bf16[384,256]{1,0:T(8,128)(2,1)}, bf16[384,256]{1,0:T(8,128)(2,1)S(1)}, u32[]{:S(2)}) copy-start(bf16[384,256]{1,0:T(8,128)(2,1)S(1)} %collective-permute-done.13.refs_8_) | copy-start | bytes 589828
  39.3 1.5 %collective-permute-start.18 = (bf16[384,256]{1,0:T(8,128)(2,1)S(1)}, bf16[384,256]{1,0:T(8,128)(2,1)S(1)}, u32[]{:S(2)}, u32[]{:S(2)}) collective-permute-start(bf16[384,256]{1,0:T(8,128)(2,1)S(1)} %collective-permute-done.7.refs_15_), channel_id=1, source_target_pairs={{0,2},{2,0},{4,6},{6,4},{8,10},{10,8},{12,14},{14,12},{16,18},{18,... | collective-permute-start | bytes 589832 | tf_op jit(solution)/shard_map/ppermute | solution.py:312
  39.5 1.8 %copy-start.13 = (bf16[384,256]{1,0:T(8,128)(2,1)}, bf16[384,256]{1,0:T(8,128)(2,1)S(1)}, u32[]{:S(2)}) copy-start(bf16[384,256]{1,0:T(8,128)(2,1)S(1)} %collective-permute-done.14.refs_9_) | copy-start | bytes 589828
  39.5 1.7 %collective-permute-start.19 = (bf16[384,256]{1,0:T(8,128)(2,1)S(1)}, bf16[384,256]{1,0:T(8,128)(2,1)S(1)}, u32[]{:S(2)}, u32[]{:S(2)}) collective-permute-start(bf16[384,256]{1,0:T(8,128)(2,1)S(1)} %collective-permute-done.9.refs_18_), channel_id=1, source_target_pairs={{0,2},{2,0},{4,6},{6,4},{8,10},{10,8},{12,14},{14,12},{16,18},{18,... | collective-permute-start | bytes 589832 | tf_op jit(solution)/shard_map/ppermute | solution.py:312
  39.9 1.4 %copy-start.14 = (bf16[384,256]{1,0:T(8,128)(2,1)}, bf16[384,256]{1,0:T(8,128)(2,1)S(1)}, u32[]{:S(2)}) copy-start(bf16[384,256]{1,0:T(8,128)(2,1)S(1)} %collective-permute-done.15.refs_12_) | copy-start | bytes 589828
  39.9 1.3 %collective-permute-start.12 = (bf16[2,96,256]{2,1,0:T(8,128)(2,1)S(1)}, bf16[2,96,256]{2,1,0:T(8,128)(2,1)S(1)}, u32[]{:S(2)}, u32[]{:S(2)}) collective-permute-start(bf16[2,96,256]{2,1,0:T(8,128)(2,1)S(1)} %collective-permute-done.10.refs_2_), channel_id=1, source_target_pairs={{0,2},{2,0},{4,6},{6,4},{8,10},{10,8},{12,14},{14,12},{16,18},{18,... | collective-permute-start | bytes 294920 | tf_op jit(solution)/shard_map/ppermute | solution.py:312
  40.2 1.2 %copy-start.15 = (bf16[384,256]{1,0:T(8,128)(2,1)}, bf16[384,256]{1,0:T(8,128)(2,1)S(1)}, u32[]{:S(2)}) copy-start(bf16[384,256]{1,0:T(8,128)(2,1)S(1)} %collective-permute-done.16.refs_13_) | copy-start | bytes 589828
  40.5 0.9 %copy-start.16 = (bf16[384,256]{1,0:T(8,128)(2,1)}, bf16[384,256]{1,0:T(8,128)(2,1)S(1)}, u32[]{:S(2)}) copy-start(bf16[384,256]{1,0:T(8,128)(2,1)S(1)} %collective-permute-done.17.refs_16_) | copy-start | bytes 589828
  40.7 0.7 copy-start.17
  41.2 0.6 copy-start.20
  41.2 0.7 copy-start.18
